TPU v7x, 256 devices: a whole 4x4x8 slice. The times are simulated.
256 devices in a mesh: ctx: 32 (over z, x), head: 4 (over y_lo, core), rep: 2 (over y_hi).
Axes of the slice: x: 4, y: 4 (y_hi: 2, y_lo: 2; y = y_hi * 2 + y_lo), z: 8, core: 2. Of those that a mesh axis runs over, the one named last changes fastest.
Arguments:
- prefill_queries: bfloat16 [8192, 12288], P(('rep', 'ctx'), 'head'), parts along dimension 0, may hold values from -10 to 10
- prefill_keys: bfloat16 [8192, 1024], P(('rep', 'ctx'), 'head'), parts along dimension 0, may hold values from -5 to 5
- prefill_values: bfloat16 [8192, 1024], P(('rep', 'ctx'), 'head'), parts along dimension 0, may hold values from -6 to 6
- block_pair: int32 [64], P('rep'), parts along dimension 0, may hold values from 0 to 31, each once
- decode_queries: bfloat16 [64, 3, 12288], P('rep', None, 'head'), parts along dimension 0, may hold values from -10 to 10
- cache_keys: bfloat16 [64, 4096, 1024], P('rep', 'ctx', 'head'), parts along dimension 0, may hold values from -5 to 5
- cache_values: bfloat16 [64, 4096, 1024], P('rep', 'ctx', 'head'), parts along dimension 0, may hold values from -6 to 6
- draft_keys: bfloat16 [64, 3, 1024], P('rep', None, 'head'), parts along dimension 0, may hold values from -5 to 5
- draft_values: bfloat16 [64, 3, 1024], P('rep', None, 'head'), parts along dimension 0, may hold values from -6 to 6
- cache_len: int32 [64], P('rep'), parts along dimension 0, may hold values from 1 to 4096, as said below
Outputs:
- prefill_out: bfloat16 [8192, 12288], P(('rep', 'ctx'), 'head'), parts along dimension 0
- decode_out: bfloat16 [64, 3, 12288], P('rep', None, 'head'), parts along dimension 0
There are 2 independent parts, one for each index of `rep`. A program takes and returns all parts, laid end to end along the dimension named above; each array names one. Nothing has to cross between parts.
Inputs may be any that keep to these rules, and one draw needn't show every extreme that they name: A permutation: index c of ctx holds prompt blocks block_pair[c] and 63 - block_pair[c], the lower one first. Request r holds its cache in slots 0 to cache_len[r] - 1; some request fills all 4096 slots.
All inputs are finite; a program needn't handle non-finite values.
Results may differ from a plain program's by a relative error of at most 0.004.
Values may be sent and summed in bfloat16 or wider, within the bound.
No kernel may reach another device: no remote copies, remote signals or barrier semaphores. Data moves between devices by JAX's collectives and lax.ppermute only.
A program may use at most 128 MiB of HBM per device.

v0:
```python
import jax
import jax.numpy as jnp
from jax import lax
from jax.sharding import PartitionSpec as P

D_HEAD = 128
HEADS = 96
KV_HEADS = 8


NEG = -1e30
KEY_BLOCK = 512


def layout_positions(block_pair, rows, tok_dev):
    count = block_pair.shape[0]
    device = rows // tok_dev
    within = rows % tok_dev
    half = tok_dev // 2
    table = jnp.arange(count, dtype=jnp.int32)
    pair = jnp.sum(jnp.where(device[:, None] == table[None, :], block_pair[None, :], 0), axis=1)
    block = jnp.where(within < half, pair, 2 * count - 1 - pair)
    return block * half + within % half


def block_scores(queries, query_pos, keys, key_pos, scale):
    scores = jnp.einsum("qkgd,nkd->qkgn", queries, keys, preferred_element_type=jnp.float32) * scale
    visible = (key_pos[None, :] <= query_pos[:, None])[:, None, None, :]
    return (jnp.where(visible, scores, NEG), visible)


def draft_scores(queries, new_keys, scale):
    rows, steps = (queries.shape[0], queries.shape[1])
    keys = new_keys.reshape(rows, steps, queries.shape[2], queries.shape[4])
    scores = (
        jnp.einsum("rtkgd,rukd->rtkgu", queries, keys, preferred_element_type=jnp.float32) * scale
    )
    order = jnp.arange(steps, dtype=jnp.int32)
    causal = (order[None, :] <= order[:, None])[None, :, None, None, :]
    return (jnp.where(causal, scores, NEG), causal)


def weigh(scores, mask, top, values):
    weights = jnp.where(mask, jnp.exp(scores - top[..., None]), 0.0)
    mixed = jnp.einsum(
        "rtkgn,rnkd->rtkgd",
        weights.astype(jnp.bfloat16),
        values,
        preferred_element_type=jnp.float32,
    )
    return (jnp.sum(weights, axis=-1), mixed)


def local(
    prefill_queries,
    prefill_keys,
    prefill_values,
    block_pair,
    decode_queries,
    cache_keys,
    cache_values,
    draft_keys,
    draft_values,
    cache_len,
):
    tok_dev = prefill_queries.shape[0]
    kv_local = prefill_keys.shape[1] // D_HEAD
    group = HEADS // KV_HEADS
    heads_local = kv_local * group
    scale = D_HEAD ** (-0.5)
    queries = prefill_queries.reshape(tok_dev, kv_local, group, D_HEAD)
    own_rows = lax.axis_index("ctx") * tok_dev + jnp.arange(tok_dev, dtype=jnp.int32)
    query_pos = layout_positions(block_pair, own_rows, tok_dev)
    start = jnp.int32(0)
    top = jnp.full((tok_dev, kv_local, group), NEG, jnp.float32)
    total = jnp.zeros((tok_dev, kv_local, group), jnp.float32)
    mixed = jnp.zeros((tok_dev, kv_local, group, D_HEAD), jnp.float32)
    keys_piece = lax.all_gather(prefill_keys, "ctx", axis=0, tiled=True)
    values_piece = lax.all_gather(prefill_values, "ctx", axis=0, tiled=True)
    count = keys_piece.shape[0]
    for begin in range(0, count, KEY_BLOCK):
        width = min(KEY_BLOCK, count - begin)
        key_pos = layout_positions(
            block_pair, start + begin + jnp.arange(width, dtype=jnp.int32), tok_dev
        )
        key_rows = keys_piece[begin : begin + width].reshape(width, kv_local, D_HEAD)
        value_rows = values_piece[begin : begin + width].reshape(width, kv_local, D_HEAD)
        scores, visible = block_scores(queries, query_pos, key_rows, key_pos, scale)
        new_top = jnp.maximum(top, jnp.max(scores, axis=-1))
        factor = jnp.exp(top - new_top)
        weights = jnp.where(visible, jnp.exp(scores - new_top[..., None]), 0.0)
        total = total * factor + jnp.sum(weights, axis=-1)
        mixed = mixed * factor[..., None] + jnp.einsum(
            "qkgn,nkd->qkgd",
            weights.astype(jnp.bfloat16),
            value_rows,
            preferred_element_type=jnp.float32,
        )
        top = new_top
    top_rows, total, mixed = (top, total, mixed)
    prefill_out = (
        (mixed / total[..., None]).astype(jnp.bfloat16).reshape(tok_dev, heads_local * D_HEAD)
    )
    rows, steps = (decode_queries.shape[0], decode_queries.shape[1])
    cache_dev = cache_keys.shape[1]
    queries_dec = decode_queries.reshape(rows, steps, kv_local, group, D_HEAD)
    slots = lax.axis_index("ctx") * cache_dev + jnp.arange(cache_dev, dtype=jnp.int32)
    live = (slots[None, :] < cache_len[:, None])[:, None, None, None, :]
    cache_k = cache_keys.reshape(rows, cache_dev, kv_local, D_HEAD)
    cache_v = cache_values.reshape(rows, cache_dev, kv_local, D_HEAD)
    draft_v = draft_values.reshape(rows, steps, kv_local, D_HEAD)
    scores = (
        jnp.einsum("rtkgd,rckd->rtkgc", queries_dec, cache_k, preferred_element_type=jnp.float32)
        * scale
    )
    scores = jnp.where(live, scores, NEG)
    local_top = jnp.max(scores, axis=-1)
    d_scores, causal = draft_scores(queries_dec, draft_keys, scale)
    d_top = jnp.max(d_scores, axis=-1)
    top = lax.pmax(jnp.maximum(local_top, d_top), "ctx")
    total, mixed = weigh(scores, live, top, cache_v)
    total, mixed = lax.psum((total, mixed), "ctx")
    d_total, d_mixed = weigh(d_scores, causal, top, draft_v)
    finished = (mixed + d_mixed) / (total + d_total)[..., None]
    decode_out = finished.astype(jnp.bfloat16).reshape(rows, steps, heads_local * D_HEAD)
    return (prefill_out, decode_out)


def solution(mesh):
    return jax.shard_map(
        local,
        mesh=mesh,
        in_specs=(
            P(("rep", "ctx"), "head"),
            P(("rep", "ctx"), "head"),
            P(("rep", "ctx"), "head"),
            P("rep"),
            P("rep", None, "head"),
            P("rep", "ctx", "head"),
            P("rep", "ctx", "head"),
            P("rep", None, "head"),
            P("rep", None, "head"),
            P("rep"),
        ),
        out_specs=(P(("rep", "ctx"), "head"), P("rep", None, "head")),
        check_vma=False,
    )
```

profile of v0, /device:TPU:16, one launch (start us, length us, event | category | flops | bytes accessed | tf_op | source)
XLA Modules:
  0.0 542.6 jit_solution(5798779421447493738)
XLA Ops:
  9.6 2.6 reshape.990
  14.5 2.8 bitcast_reduce_fusion
  17.3 145.9 %pmax.7 = f32[32,3,2,12]{3,1,2,0:T(4,128)S(1)} all-reduce(f32[32,3,2,12]{3,1,2,0:T(4,128)S(1)} %max.229), channel_id=1, replica_groups=mesh['ctx'=32,'head'=4,'rep'=2] {'ctx'}, use_global_device_ids=true, to_apply=%region_27.28 | all-reduce | flops 2304 | bytes 18432 | tf_op jit(solution)/shard_map/pmax | solution.py:120
  163.2 2.5 reshape.993
  165.8 3.4 fusion.65
  171.2 2.4 fusion.72
  173.6 138.3 %psum.15 = f32[32,3,2,12]{3,1,2,0:T(4,128)S(1)} all-reduce(f32[32,3,2,12]{3,1,2,0:T(4,128)S(1)} %fusion.72), channel_id=1, replica_groups=mesh['ctx'=32,'head'=4,'rep'=2] {'ctx'}, use_global_device_ids=true, to_apply=%region_30.31 | all-reduce | flops 2304 | bytes 18432 | tf_op jit(solution)/shard_map/psum | solution.py:122
  313.6 1.7 all-reduce.2.cloned.1.call-done
  315.3 2.4 fusion.53
  319.1 74.3 %all-gather.5.cloned.1.call-done = bf16[4096,256]{1,0:T(8,128)(2,1)} async-done(((bf16[128,256]{1,0:T(8,128)(2,1)}), bf16[4096,256]{1,0:T(8,128)(2,1)}) %all-gather.5.cloned.1.call-update) | async-done | bytes 2097168 | tf_op jit(solution)/shard_map/all_gather | solution.py:79
  401.8 66.3 %all-gather.3.cloned.1.call-done = bf16[4096,256]{0,1:T(8,128)(2,1)} async-done(((bf16[128,256]{0,1:T(8,128)(2,1)}), bf16[4096,256]{0,1:T(8,128)(2,1)}) %all-gather.3.cloned.1.call-update) | async-done | bytes 2097168 | tf_op jit(solution)/shard_map/all_gather | solution.py:78
  468.2 1.7 fusion.173
  474.4 3.7 fusion.4
  478.1 3.7 fusion.5
  481.9 3.7 fusion.6
  485.6 3.7 fusion.7
  489.3 4.5 fusion.22
  493.8 5.8 %fusion.24 = f32[2,128,12,128]{1,3,2,0:T(8,128)} fusion(bf16[512,2,128,1]{0,2,3,1:T(8,128)(2,1)S(1)} %bitcast.312, f32[2,512,128,12]{2,1,3,0:T(8,128)} %get-tuple-element.58, f32[128,2,12]{0,2,1:T(8,128)S(1)} %get-tuple-element.24, pred[128,512]{0,1:T(8,128)(4,1)S(1)} %get-tuple-element.56), kind=kOutput, calls=%fused_computation.40 | convolution fusion | flops 410517504 | bytes 8204288 | tf_op jit(solution)/shard_map/qkgn,nkd->qkgd/dot_general | solution.py:93
  501.2 5.8 %fusion.26 = f32[2,128,12,128]{1,3,2,0:T(8,128)} fusion(bf16[512,2,128,1]{0,2,3,1:T(8,128)(2,1)S(1)} %bitcast.311, f32[2,512,128,12]{2,1,3,0:T(8,128)} %get-tuple-element.60, f32[128,2,12]{0,2,1:T(8,128)S(1)} %get-tuple-element.25, pred[128,512]{0,1:T(8,128)(4,1)S(1)} %get-tuple-element.55), kind=kOutput, calls=%fused_computation.41 | convolution fusion | flops 410517504 | bytes 8204288 | tf_op jit(solution)/shard_map/qkgn,nkd->qkgd/dot_general | solution.py:93
  508.6 5.8 %fusion.28 = f32[2,128,12,128]{1,3,2,0:T(8,128)} fusion(bf16[512,2,128,1]{0,2,3,1:T(8,128)(2,1)S(1)} %bitcast.310, f32[2,512,128,12]{2,1,3,0:T(8,128)} %get-tuple-element.62, f32[128,2,12]{0,2,1:T(8,128)S(1)} %get-tuple-element.26, pred[128,512]{0,1:T(8,128)(4,1)S(1)} %get-tuple-element.54), kind=kOutput, calls=%fused_computation.42 | convolution fusion | flops 410517504 | bytes 8204288 | tf_op jit(solution)/shard_map/qkgn,nkd->qkgd/dot_general | solution.py:93
  515.9 2.9 fusion.30
  518.8 1.8 fusion.14
  527.1 1.7 fusion.36
  531.7 2.7 fusion.57
  (109 shorter events, 37.7 us)
Async XLA Ops:
  7.2 308.2 %all-reduce.2.cloned.1.call-start = ((), (), s32[]{:S(2)}) async-start(), calls=%async_computation.2 | async-start | bytes 3145728 | tf_op jit(solution)/shard_map/psum | solution.py:122
  14.4 297.4 %copy-start.1 = (f32[32,3,2,12,3]{3,4,1,2,0:T(4,128)}, f32[32,3,2,12,3]{3,4,1,2,0:T(4,128)S(1)}, u32[]{:S(2)}) copy-start(f32[32,3,2,12,3]{3,4,1,2,0:T(4,128)S(1)} %get-tuple-element.76) | copy-start | bytes 82948
  17.3 152.8 %copy-start.10 = (bf16[128,256]{1,0:T(8,128)(2,1)S(1)}, bf16[128,256]{1,0:T(8,128)(2,1)}, u32[]{:S(2)}) copy-start(bf16[128,256]{1,0:T(8,128)(2,1)} %param.11) | copy-start | bytes 196612
  17.3 153.5 %copy-start.11 = (bf16[32,3,256]{2,0,1:T(8,128)(2,1)S(1)}, bf16[32,3,256]{2,0,1:T(8,128)(2,1)}, u32[]{:S(2)}) copy-start(bf16[32,3,256]{2,0,1:T(8,128)(2,1)} %param.18) | copy-start | bytes 147460
  17.3 153.5 %copy-start = (bf16[128,3072]{1,0:T(8,128)(2,1)S(1)}, bf16[128,3072]{1,0:T(8,128)(2,1)}, u32[]{:S(2)}) copy-start(bf16[128,3072]{1,0:T(8,128)(2,1)} %param.10) | copy-start | bytes 2359300
  165.8 146.6 %copy-start.12 = (s32[32]{0:T(128)S(1)}, s32[32]{0:T(128)}, u32[]{:S(2)}) copy-start(s32[32]{0:T(128)} %param.13) | copy-start | bytes 388
  169.2 224.2 %all-gather.5.cloned.1.call-start = ((), (), s32[]{:S(2)}) async-start(), calls=%async_computation.1 | async-start | bytes 2162688 | tf_op jit(solution)/shard_map/all_gather | solution.py:79
  170.0 298.2 %all-gather.3.cloned.1.call-start = ((), (), s32[]{:S(2)}) async-start(), calls=%async_computation | async-start | bytes 2162688 | tf_op jit(solution)/shard_map/all_gather | solution.py:78
  485.6 8.2 %copy-start.9 = (bf16[512,256]{0,1:T(8,128)(2,1)S(1)}, bf16[512,256]{0,1:T(8,128)(2,1)}, u32[]{:S(2)}) copy-start(bf16[512,256]{0,1:T(8,128)(2,1)} %copy.117) | copy-start | bytes 786436
  493.8 5.9 %slice-start.4 = ((s8[6291456]{0:T(1024)(128)(4,1)}), s8[4194304]{0:T(1024)(128)(4,1)S(1)}, s32[]{:S(2)}) async-start(s8[6291456]{0:T(1024)(128)(4,1)} %bitcast.292), calls=%async_computation.7 | async-start | bytes 8388608
  493.8 5.9 %slice-start.5 = ((s8[6291456]{0:T(1024)(128)(4,1)}), s8[2097152]{0:T(1024)(128)(4,1)S(1)}, s32[]{:S(2)}) async-start(s8[6291456]{0:T(1024)(128)(4,1)} %bitcast.292), calls=%async_computation.8 | async-start | bytes 4194304
  493.8 7.4 %copy-start.8 = (bf16[512,256]{0,1:T(8,128)(2,1)S(1)}, bf16[512,256]{0,1:T(8,128)(2,1)}, u32[]{:S(2)}) copy-start(bf16[512,256]{0,1:T(8,128)(2,1)} %copy.113) | copy-start | bytes 786436
  501.2 5.8 %slice-start.2 = ((s8[6291456]{0:T(1024)(128)(4,1)}), s8[4194304]{0:T(1024)(128)(4,1)S(1)}, s32[]{:S(2)}) async-start(s8[6291456]{0:T(1024)(128)(4,1)} %bitcast.290), calls=%async_computation.5 | async-start | bytes 8388608
  501.2 5.8 %slice-start.3 = ((s8[6291456]{0:T(1024)(128)(4,1)}), s8[2097152]{0:T(1024)(128)(4,1)S(1)}, s32[]{:S(2)}) async-start(s8[6291456]{0:T(1024)(128)(4,1)} %bitcast.290), calls=%async_computation.6 | async-start | bytes 4194304
  501.2 7.3 %copy-start.7 = (bf16[512,256]{0,1:T(8,128)(2,1)S(1)}, bf16[512,256]{0,1:T(8,128)(2,1)}, u32[]{:S(2)}) copy-start(bf16[512,256]{0,1:T(8,128)(2,1)} %copy.109) | copy-start | bytes 786436
  508.5 5.8 %slice-start = ((s8[6291456]{0:T(1024)(128)(4,1)}), s8[4194304]{0:T(1024)(128)(4,1)S(1)}, s32[]{:S(2)}) async-start(s8[6291456]{0:T(1024)(128)(4,1)} %bitcast.288), calls=%async_computation.3 | async-start | bytes 8388608
  508.6 5.8 %slice-start.1 = ((s8[6291456]{0:T(1024)(128)(4,1)}), s8[2097152]{0:T(1024)(128)(4,1)S(1)}, s32[]{:S(2)}) async-start(s8[6291456]{0:T(1024)(128)(4,1)} %bitcast.288), calls=%async_computation.4 | async-start | bytes 4194304
  508.6 7.3 %copy-start.6 = (bf16[512,256]{0,1:T(8,128)(2,1)S(1)}, bf16[512,256]{0,1:T(8,128)(2,1)}, u32[]{:S(2)}) copy-start(bf16[512,256]{0,1:T(8,128)(2,1)} %copy.105) | copy-start | bytes 786436
  515.9 4.7 copy-start.5
  520.6 3.2 copy-start.4
  523.8 3.3 copy-start.3
  528.8 2.0 copy-start.14
  528.8 2.4 copy-start.15
  528.8 2.9 copy-start.16
  (2 other events, 3.2 us)
Sparse Core Ops, SparseCore 0:
  169.3 145.9 all-reduce.1
  318.2 75.1 all-gather.4
  396.2 71.9 all-gather.2
where the time goes:
time: 548 us; the launch traced here: 543 us
  blocking collectives  284 us (52%)
  waiting for transfers between devices  143 us (26%)
  matrix products  57.4 us (10%)
  local copies, waits for them, and re-layouts  22.6 us (4%)
  other arithmetic  20.4 us (4%)
  between operations  14.8 us (3%)
    pmax x1, blocking collectives, local(): top = lax.pmax(jnp.maximum(local_top, d_top), 'ctx')  146 us
    psum x1, blocking collectives, local(): total, mixed = lax.psum((total, mixed), 'ctx')  138 us
    all_gather x1, waiting for transfers between devices, local(): values_piece = lax.all_gather(prefill_values, 'ctx', axis=0, tiled=True)  74.3 us
    all_gather x1, waiting for transfers between devices, local(): keys_piece = lax.all_gather(prefill_keys, 'ctx', axis=0, tiled=True)  66.3 us
    dot_general x8, matrix products, local(): jnp.einsum('qkgn,nkd->qkgd', weights.astype(jnp.bfloat16), value_rows, pr...  28 us
    dot_general x8, matrix products, block_scores(): jnp.einsum('qkgd,nkd->qkgn', queries, keys, preferred_element_type=jnp.fl...  19.3 us
    reduce_sum x8, other arithmetic, local(): total = total * factor + jnp.sum(weights, axis=-1)  15.5 us
  transfers between devices with their start and end apart: 3, of which 3 were waited for; matrix products, arithmetic and copies ran while one was open for 3% of the time, Pallas kernels for 0%

commit v1 on v0

v1 whole, which is shorter than its diff:
```python
import functools

import jax
import jax.numpy as jnp
from jax import lax
from jax.experimental import pallas as pl
from jax.experimental.pallas import tpu as pltpu
from jax.sharding import PartitionSpec as P

D = 128
HEADS = 96
KV_HEADS = 8
GROUP = HEADS // KV_HEADS
KV_LOC = 2
H_LOC = KV_LOC * GROUP
HALF = 64
NZ, NX = 8, 4
N = NZ * NX
REQ = 32
STEPS = 3
ROWS = STEPS * H_LOC
PAY = ROWS + 8
NEG = -1e30
C2 = float(D**-0.5 * 1.4426950408889634)
CHUNK = 512
VMEM_LIMIT = 40 * 1024 * 1024
RB = 4


def row_iota(shape):
    return lax.broadcasted_iota(jnp.int32, shape, 0)


def lane_iota(shape):
    return lax.broadcasted_iota(jnp.int32, shape, 1)


def dot_t(a, b):
    return lax.dot_general(a, b, (((1,), (1,)), ((), ())), preferred_element_type=jnp.float32)


def dot(a, b):
    return lax.dot_general(a, b, (((1,), (0,)), ((), ())), preferred_element_type=jnp.float32)


def to_lanes(col_bc, rows):
    diag = row_iota((rows, D)) == lane_iota((rows, D))
    return jnp.sum(jnp.where(diag, col_bc, 0.0), axis=0, keepdims=True)


def decode_kernel(ctx_ref, len_ref, q_ref, k_ref, v_ref, out_ref):
    first = ctx_ref[0] * D
    step = pl.program_id(0)
    shape = (ROWS, 2 * D)
    lane = lane_iota(shape)
    kv_of_row = (lax.rem(row_iota(shape), H_LOC) >= GROUP).astype(jnp.int32)
    kv_of_lane = (lane >= D).astype(jnp.int32)
    same = kv_of_row == kv_of_lane
    slot = jnp.where(lane >= D, lane - D, lane) + first
    sub = row_iota((8, D))
    for i in range(RB):
        length = len_ref[step * RB + i]
        k = k_ref[i]
        v = v_ref[i]
        k2 = jnp.concatenate([k[:, :D], k[:, D:]], axis=0)
        v2 = jnp.concatenate([v[:, :D], v[:, D:]], axis=0)
        s = dot_t(q_ref[i], k2) * C2
        live = same & (slot < length)
        s = jnp.where(live, s, NEG)
        top = jnp.max(s, axis=1, keepdims=True).astype(jnp.bfloat16).astype(jnp.float32)
        p = jnp.where(live, jnp.exp2(s - top), 0.0)
        total = jnp.sum(p, axis=1, keepdims=True)
        o = dot(p.astype(jnp.bfloat16), v2)
        t_hi = total.astype(jnp.bfloat16).astype(jnp.float32)
        t_lo = total - t_hi
        m_row = to_lanes(jnp.broadcast_to(top, (ROWS, D)), ROWS)
        h_row = to_lanes(jnp.broadcast_to(t_hi, (ROWS, D)), ROWS)
        l_row = to_lanes(jnp.broadcast_to(t_lo, (ROWS, D)), ROWS)
        tail = jnp.where(sub == 0, m_row, jnp.where(sub == 1, h_row, jnp.where(sub == 2, l_row, 0.0)))
        out_ref[i] = jnp.concatenate([o, tail], axis=0).astype(jnp.bfloat16)


def decode_partials(ctx, cache_len, q72, cache_k, cache_v):
    return pl.pallas_call(
        decode_kernel,
        out_shape=jax.ShapeDtypeStruct((REQ, PAY, D), jnp.bfloat16),
        grid_spec=pltpu.PrefetchScalarGridSpec(
            num_scalar_prefetch=2,
            grid=(REQ // RB,),
            in_specs=[
                pl.BlockSpec((RB, ROWS, D), lambda i, c, n: (i, 0, 0)),
                pl.BlockSpec((RB, D, 2 * D), lambda i, c, n: (i, 0, 0)),
                pl.BlockSpec((RB, D, 2 * D), lambda i, c, n: (i, 0, 0)),
            ],
            out_specs=pl.BlockSpec((RB, PAY, D), lambda i, c, n: (i, 0, 0)),
        ),
        compiler_params=pltpu.CompilerParams(vmem_limit_bytes=VMEM_LIMIT),
        cost_estimate=pl.CostEstimate(
            flops=REQ * ROWS * 256 * D * 4, bytes_accessed=6 * 2**20, transcendentals=REQ * ROWS * 256
        ),
        name="decode_partials",
    )(ctx, cache_len, q72, cache_k, cache_v)


def combine_kernel(ctx_ref, recv_ref, q_ref, dk_ref, dv_ref, out_ref):
    dk = dk_ref[0].astype(jnp.float32)
    dv = dv_ref[0].astype(jnp.float32)
    k2 = jnp.concatenate([dk[:, :D], dk[:, D:]], axis=0).astype(jnp.bfloat16)
    v2 = jnp.concatenate([dv[:, :D], dv[:, D:]], axis=0).astype(jnp.bfloat16)
    s = dot_t(q_ref[0], k2) * C2
    shape = (ROWS, 16)
    row, lane = row_iota(shape), lane_iota(shape)
    kv_of_row = (lax.rem(row, H_LOC) >= GROUP).astype(jnp.int32)
    kv_of_lane = (lane >= 8).astype(jnp.int32)
    token = jnp.where(lane >= 8, lane - 8, lane)
    time = (row >= H_LOC).astype(jnp.int32) + (row >= 2 * H_LOC).astype(jnp.int32)
    seen = (kv_of_row == kv_of_lane) & (token <= time)
    s = jnp.where(seen, s, NEG)
    d_top = jnp.max(s, axis=1, keepdims=True)
    p = jnp.where(seen, jnp.exp2(s - d_top), 0.0)
    d_total = jnp.sum(p, axis=1, keepdims=True)
    d_out = dot(p.astype(jnp.bfloat16), v2)
    d_m = to_lanes(jnp.broadcast_to(d_top, (ROWS, D)), ROWS)
    d_l = to_lanes(jnp.broadcast_to(d_total, (ROWS, D)), ROWS)

    tails = recv_ref[:, ROWS:, :].astype(jnp.float32)
    m = tails[:, 0, :]
    total = tails[:, 1, :] + tails[:, 2, :]
    top = jnp.maximum(jnp.max(m, axis=0, keepdims=True), d_m)
    w = jnp.exp2(m - top)
    w_d = jnp.exp2(d_m - top)
    whole = jnp.sum(w * total, axis=0, keepdims=True) + w_d * d_l
    inv = 1.0 / jnp.where(whole > 0.0, whole, 1.0)
    w_all = jnp.concatenate([w * inv, jnp.broadcast_to(w_d * inv, (8, D)), jnp.zeros((D - N - 8, D), jnp.float32)], axis=0)
    w_cols = jnp.transpose(w_all)[:ROWS]
    acc = d_out * w_cols[:, N : N + 1]
    for src in range(N):
        acc = acc + recv_ref[src, :ROWS, :].astype(jnp.float32) * w_cols[:, src : src + 1]
    out_ref[...] = acc.astype(jnp.bfloat16)


def combine(ctx, recv, q72, dk8, dv8):
    return pl.pallas_call(
        combine_kernel,
        out_shape=jax.ShapeDtypeStruct((ROWS, D), jnp.bfloat16),
        grid_spec=pltpu.PrefetchScalarGridSpec(
            num_scalar_prefetch=1,
            grid=(1,),
            in_specs=[
                pl.BlockSpec((N, PAY, D), lambda i, c: (0, 0, 0)),
                pl.BlockSpec((1, ROWS, D), lambda i, c: (c[0], 0, 0)),
                pl.BlockSpec((1, 8, 2 * D), lambda i, c: (c[0], 0, 0)),
                pl.BlockSpec((1, 8, 2 * D), lambda i, c: (c[0], 0, 0)),
            ],
            out_specs=pl.BlockSpec((ROWS, D), lambda i, c: (0, 0)),
        ),
        compiler_params=pltpu.CompilerParams(vmem_limit_bytes=VMEM_LIMIT),
        cost_estimate=pl.CostEstimate(flops=4 * 2**20, bytes_accessed=2**20, transcendentals=2**14),
        name="combine",
    )(ctx, recv, q72, dk8, dv8)


def flash_step(qs_ref, kv_ref, m_ref, l_ref, acc_ref, part, kv, start, limit):
    rows = GROUP * HALF
    rb = 256
    k = kv_ref[pl.ds(start, CHUNK), kv * D : (kv + 1) * D]
    v = kv_ref[pl.ds(start, CHUNK), (KV_LOC + kv) * D : (KV_LOC + kv + 1) * D]
    for r in range(0, rows, rb):
        at = pl.ds(r, rb)
        s = dot_t(qs_ref[part, kv, at, :], k)
        if limit is not None:
            pos = start + lane_iota((rb, CHUNK))
            own = limit + (row_iota((rb, CHUNK)) & (HALF - 1))
            s = jnp.where(pos <= own, s, NEG)
        m_old = m_ref[part, kv, at, :]
        m_new = jnp.maximum(m_old, jnp.max(s, axis=1, keepdims=True))
        alpha = jnp.exp2((m_old - m_new) * C2)
        base = m_new * C2
        total = jnp.zeros((rb, D), jnp.float32)
        pieces = []
        for j in range(0, CHUNK, D):
            p = jnp.exp2(s[:, j : j + D] * C2 - base)
            total = total + p
            pieces.append(p.astype(jnp.bfloat16))
        p16 = jnp.concatenate(pieces, axis=1)
        l_ref[part, kv, at, :] = l_ref[part, kv, at, :] * alpha + total
        acc_ref[part, kv, at, :] = acc_ref[part, kv, at, :] * alpha + dot(p16, v)
        m_ref[part, kv, at, :] = m_new


def prefill_kernel(pair_ref, ctx_ref, *refs, blocks):
    n_in = len(blocks)
    q_ref = refs[0]
    srcs = refs[1 : 1 + n_in]
    out_ref = refs[1 + n_in]
    kv_lo, kv_hi, qs, m_ref, l_ref, acc_ref, sems = refs[2 + n_in :]
    ctx = ctx_ref[0]
    z, x = ctx // NX, lax.rem(ctx, NX)

    def copies():
        made = []
        for ref, (high, places) in zip(srcs, blocks):
            for j, (dz, dx) in enumerate(places):
                src = lax.rem(z + NZ - dz, NZ) * NX + lax.rem(x + NX - dx, NX)
                pair = pair_ref[src]
                if high:
                    dst = kv_hi.at[pl.ds(pl.multiple_of((N - 1 - pair) * HALF, HALF), HALF)]
                else:
                    dst = kv_lo.at[pl.ds(pl.multiple_of(pair * HALF, HALF), HALF)]
                made.append(pltpu.make_async_copy(ref.at[j], dst, sems.at[len(made)]))
        return made

    made = copies()
    for c in made:
        c.start()
    for part in range(2):
        for h in range(H_LOC):
            kv, g = divmod(h, GROUP)
            qs[part, kv, g * HALF : (g + 1) * HALF, :] = q_ref[part * HALF : (part + 1) * HALF, h * D : (h + 1) * D]
    m_ref[...] = jnp.full_like(m_ref, NEG)
    l_ref[...] = jnp.zeros_like(l_ref)
    acc_ref[...] = jnp.zeros_like(acc_ref)
    for c in made:
        c.wait()

    b = pair_ref[ctx]
    per = CHUNK // HALF
    step = functools.partial(flash_step, qs)

    def dense(ref, part, count):
        @pl.loop(0, count)
        def _(i):
            for kv in range(KV_LOC):
                step(ref, m_ref, l_ref, acc_ref, part, kv, pl.multiple_of(i * CHUNK, CHUNK), None)

    def last(ref, part, full, block):
        for kv in range(KV_LOC):
            step(ref, m_ref, l_ref, acc_ref, part, kv, pl.multiple_of(full * CHUNK, CHUNK), block * HALF)

    dense(kv_lo, 1, N * HALF // CHUNK)
    dense(kv_lo, 0, b // per)
    last(kv_lo, 0, b // per, b)
    hb = N - 1 - b
    dense(kv_hi, 1, hb // per)
    last(kv_hi, 1, hb // per, hb)
    for part in range(2):
        for h in range(H_LOC):
            kv, g = divmod(h, GROUP)
            at = pl.ds(g * HALF, HALF)
            total = jnp.sum(l_ref[part, kv, at, :], axis=1, keepdims=True)
            out_ref[part * HALF : (part + 1) * HALF, h * D : (h + 1) * D] = (acc_ref[part, kv, at, :] / total).astype(
                jnp.bfloat16
            )


def prefill(block_pair, ctx, queries, arrays, blocks):
    rows = GROUP * HALF
    return pl.pallas_call(
        functools.partial(prefill_kernel, blocks=blocks),
        out_shape=jax.ShapeDtypeStruct(queries.shape, jnp.bfloat16),
        grid_spec=pltpu.PrefetchScalarGridSpec(
            num_scalar_prefetch=2,
            grid=(1,),
            in_specs=[pl.BlockSpec(queries.shape, lambda i, p, c: (0, 0))]
            + [pl.BlockSpec(memory_space=pl.ANY)] * len(arrays),
            out_specs=pl.BlockSpec(queries.shape, lambda i, p, c: (0, 0)),
            scratch_shapes=[
                pltpu.VMEM((N * HALF, 2 * KV_LOC * D), jnp.bfloat16),
                pltpu.VMEM((N * HALF, 2 * KV_LOC * D), jnp.bfloat16),
                pltpu.VMEM((2, KV_LOC, rows, D), jnp.bfloat16),
                pltpu.VMEM((2, KV_LOC, rows, D), jnp.float32),
                pltpu.VMEM((2, KV_LOC, rows, D), jnp.float32),
                pltpu.VMEM((2, KV_LOC, rows, D), jnp.float32),
                pltpu.SemaphoreType.DMA((2 * N,)),
            ],
        ),
        compiler_params=pltpu.CompilerParams(vmem_limit_bytes=VMEM_LIMIT),
        cost_estimate=pl.CostEstimate(flops=4 * 2**30, bytes_accessed=6 * 2**20, transcendentals=7 * 2**20),
        name="prefill",
    )(block_pair, ctx, queries, *arrays)


def shift(x, dz, dx):
    def to(i):
        z, xx = divmod(i, NX)
        return ((z + dz) % NZ) * NX + (xx + dx) % NX

    return lax.ppermute(x, "ctx", [(i, to(i)) for i in range(N)])


def gather_low(own):
    parts = [own, shift(own, 0, 1), shift(own, 0, -1), shift(own, 0, 2)]
    xs = [0, 1, -1, 2]
    ring = jnp.stack(parts)
    out = [(ring, [(0, d) for d in xs])]
    up = down = ring
    for dz in range(1, 4):
        up, down = shift(up, 1, 0), shift(down, -1, 0)
        out.append((up, [(dz, d) for d in xs]))
        out.append((down, [(-dz, d) for d in xs]))
    out.append((shift(up[:2], 1, 0), [(4, d) for d in xs[:2]]))
    out.append((shift(down[2:], -1, 0), [(4, d) for d in xs[2:]]))
    return out


def gather_high(own):
    parts, zs = [own], [0]
    up = down = own
    for dz in range(1, 4):
        up, down = shift(up, 1, 0), shift(down, -1, 0)
        parts += [up, down]
        zs += [dz, -dz]
    parts.append(shift(up, 1, 0))
    zs.append(4)
    ring = jnp.stack(parts)
    right, left = shift(ring, 0, 1), shift(ring, 0, -1)
    return [
        (ring, [(d, 0) for d in zs]),
        (right, [(d, 1) for d in zs]),
        (left, [(d, -1) for d in zs]),
        (shift(right[:4], 0, 1), [(d, 2) for d in zs[:4]]),
        (shift(left[4:], 0, -1), [(d, 2) for d in zs[4:]]),
    ]


def local(
    prefill_queries,
    prefill_keys,
    prefill_values,
    block_pair,
    decode_queries,
    cache_keys,
    cache_values,
    draft_keys,
    draft_values,
    cache_len,
):
    ctx = lax.axis_index("ctx").astype(jnp.int32).reshape(1)
    kv = jnp.concatenate([prefill_keys, prefill_values], axis=1)
    low = gather_low(kv[:HALF])
    high = gather_high(kv[HALF:])

    q72 = decode_queries.reshape(REQ, ROWS, D)
    pad = ((0, 0), (0, 8 - STEPS), (0, 0))
    dk8, dv8 = jnp.pad(draft_keys, pad), jnp.pad(draft_values, pad)
    partials = decode_partials(ctx, cache_len, q72, cache_keys, cache_values)
    recv = lax.all_to_all(partials, "ctx", 0, 0, tiled=True)
    done = combine(ctx, recv, q72, dk8, dv8)
    spread = lax.all_to_all(jnp.broadcast_to(done[None], (N, ROWS, D)), "ctx", 0, 0, tiled=True)
    decode_out = spread.reshape(REQ, STEPS, H_LOC * D)

    arrays = [a for a, _ in low] + [a for a, _ in high]
    blocks = [(False, p) for _, p in low] + [(True, p) for _, p in high]
    prefill_out = prefill(block_pair, ctx, prefill_queries, arrays, blocks)
    return (prefill_out, decode_out)


def solution(mesh):
    return jax.shard_map(
        local,
        mesh=mesh,
        in_specs=(
            P(("rep", "ctx"), "head"),
            P(("rep", "ctx"), "head"),
            P(("rep", "ctx"), "head"),
            P("rep"),
            P("rep", None, "head"),
            P("rep", "ctx", "head"),
            P("rep", "ctx", "head"),
            P("rep", None, "head"),
            P("rep", None, "head"),
            P("rep"),
        ),
        out_specs=(P(("rep", "ctx"), "head"), P("rep", None, "head")),
        check_vma=False,
    )
```

time: 548 us -> 144 us (0.26)
  blocking collectives: 284 us -> 0 us
  waiting for transfers between devices: 143 us -> 43.1 us
  matrix products: 57.4 us -> 0 us
  starting transfers between devices: 0.12 us -> 48.1 us
  Pallas kernels: 0 us -> 36.9 us
  other arithmetic: 20.4 us -> 0.94 us
  between operations: 14.8 us -> 0.91 us
  local copies, waits for them, and re-layouts: 22.6 us -> 13.5 us
    pmax x1 -> x0, blocking collectives: 146 us -> none  [local(): top = lax.pmax(jnp.maximum(local_top, d_top), 'ctx')]
    all_gather x2 -> x0, waiting for transfers between devices: 141 us -> none  [the longest x1 74.3 us: local(): values_piece = lax.all_gather(prefill_values, 'ctx', axis=0, tiled=True)]
    psum x1 -> x0, blocking collectives: 138 us -> none  [local(): total, mixed = lax.psum((total, mixed), 'ctx')]
    dot_general x20 -> x0, matrix products: 57.4 us -> none  [the longest x8 28 us: local(): jnp.einsum('qkgn,nkd->qkgd', weights.astype(jnp.bfloat16), value_rows, pr...]
    ppermute x0 -> x22, waiting for transfers between devices: none -> 43.1 us  [shift(): return lax.ppermute(x, 'ctx', [(i, to(i)) for i in range(N)])]
    pallas_call x0 -> x3, Pallas kernels: none -> 36.9 us  [the longest x1 27.6 us: prefill(): pl.pallas_call(functools.partial(prefill_kernel, blocks=blocks), out_shap...]
    ppermute x0 -> x22, starting transfers between devices: none -> 34.6 us  [shift(): return lax.ppermute(x, 'ctx', [(i, to(i)) for i in range(N)])]
    reduce_sum x12 -> x0, other arithmetic: 18.5 us -> none  [the longest x8 15.5 us: local(): total = total * factor + jnp.sum(weights, axis=-1)]
  transfers between devices with their start and end apart: 3 -> 24, of which waited for: 3 -> 7; matrix products, arithmetic and copies ran while one was open for 3% -> 5% of each run, Pallas kernels for 0% -> 26%
where the time goes in v1:
time: 144 us
  starting transfers between devices  48.1 us (33%)
  waiting for transfers between devices  43.1 us (30%)
  Pallas kernels  36.9 us (26%)
  local copies, waits for them, and re-layouts  13.5 us (9%)
    ppermute x22, waiting for transfers between devices, shift(): return lax.ppermute(x, 'ctx', [(i, to(i)) for i in range(N)])  43.1 us
    ppermute x22, starting transfers between devices, shift(): return lax.ppermute(x, 'ctx', [(i, to(i)) for i in range(N)])  34.6 us
    pallas_call x1, Pallas kernels, prefill(): pl.pallas_call(functools.partial(prefill_kernel, blocks=blocks), out_shap...  27.6 us
    unnamed x26, local copies, waits for them, and re-layouts  9.34 us
    pallas_call x1, Pallas kernels, decode_partials(): pl.pallas_call(decode_kernel, out_shape=jax.ShapeDtypeStruct((REQ, PAY, D...  8.4 us
    all_to_all x1, starting transfers between devices, local(): recv = lax.all_to_all(partials, 'ctx', 0, 0, tiled=True)  7.39 us
    all_to_all x1, starting transfers between devices, local(): lax.all_to_all(jnp.broadcast_to(done[None], (N, ROWS, D)), 'ctx', 0, 0, t...  6.17 us
  transfers between devices with their start and end apart: 24, of which 7 were waited for; matrix products, arithmetic and copies ran while one was open for 5% of the time, Pallas kernels for 26%

profile of v1, /device:TPU:16, one launch (start us, length us, event | category | flops | bytes accessed | tf_op | source)
XLA Modules:
  0.0 143.5 jit_solution(15505665052749631351)
XLA Ops:
  3.8 1.9 %collective-permute-start.11 = (bf16[64,512]{1,0:T(8,128)(2,1)}, bf16[64,512]{1,0:T(8,128)(2,1)}, u32[]{:S(2)}, u32[]{:S(2)}) collective-permute-start(bf16[64,512]{1,0:T(8,128)(2,1)} %get-tuple-element.4), channel_id=1, source_target_pairs={{0,32},{8,40},{16,48},{24,56},{32,64},{40,72},{48,80},{56,88},{64,... | collective-permute-start | bytes 196616 | tf_op jit(solution)/shard_map/ppermute | solution.py:288
  5.7 3.9 %collective-permute-start.12 = (bf16[64,512]{1,0:T(8,128)(2,1)}, bf16[64,512]{1,0:T(8,128)(2,1)}, u32[]{:S(2)}, u32[]{:S(2)}) collective-permute-start(bf16[64,512]{1,0:T(8,128)(2,1)} %get-tuple-element.4), channel_id=1, source_target_pairs={{0,224},{8,232},{16,240},{24,248},{32,0},{40,8},{48,16},{56,24},{6... | collective-permute-start | bytes 196616 | tf_op jit(solution)/shard_map/ppermute | solution.py:288
  11.1 1.7 %collective-permute-start.1 = (bf16[64,512]{1,0:T(8,128)(2,1)}, bf16[64,512]{1,0:T(8,128)(2,1)}, u32[]{:S(2)}, u32[]{:S(2)}) collective-permute-start(bf16[64,512]{1,0:T(8,128)(2,1)} %get-tuple-element.6), channel_id=1, source_target_pairs={{0,24},{8,0},{16,8},{24,16},{32,56},{40,32},{48,40},{56,48},{64,88... | collective-permute-start | bytes 196616 | tf_op jit(solution)/shard_map/ppermute | solution.py:288
  12.9 1.8 %collective-permute-start.2 = (bf16[64,512]{1,0:T(8,128)(2,1)}, bf16[64,512]{1,0:T(8,128)(2,1)}, u32[]{:S(2)}, u32[]{:S(2)}) collective-permute-start(bf16[64,512]{1,0:T(8,128)(2,1)} %get-tuple-element.6), channel_id=1, source_target_pairs={{0,16},{8,24},{16,0},{24,8},{32,48},{40,56},{48,32},{56,40},{64,80... | collective-permute-start | bytes 196616 | tf_op jit(solution)/shard_map/ppermute | solution.py:288
  14.7 1.6 %copy.15 = bf16[32,3,3072]{2,1,0:T(4,128)(2,1)S(1)} copy(bf16[32,3,3072]{2,0,1:T(8,128)(2,1)} %param.14) | data formatting | bytes 1179648 | tf_op args[4]
  16.9 1.6 %copy-done.1 = bf16[32,128,256]{2,1,0:T(8,128)(2,1)S(1)} copy-done((bf16[32,128,256]{2,1,0:T(8,128)(2,1)S(1)}, bf16[32,128,256]{2,1,0:T(8,128)(2,1)}, u32[]{:S(2)}) %copy-start.1) | copy-done | bytes 2097176
  18.4 8.4 %decode_partials.1 = bf16[32,80,128]{2,1,0:T(8,128)(2,1)} custom-call(s32[1]{0:T(128)} %bitcast.ctx_ref, s32[32]{0:T(128)S(1)} %copy-done.2, bf16[32,72,128]{2,1,0:T(8,128)(2,1)S(1)} %reshape.15.q_ref, bf16[32,128,256]{2,1,0:T(8,128)(2,1)S(1)} %copy-done, bf16[32,128,256]{2,1,0:T(8,128)(2,1)S(1)} %copy-done.1), custom_call_target="tpu_custom_call" | custom-call | flops 301989888 | bytes 6291456 | tf_op jit(solution)/shard_map/decode_partials/pallas_call | solution.py:84
  26.8 7.4 %all-to-all-start = ((bf16[32,80,128]{2,1,0:T(8,128)(2,1)}), bf16[32,80,128]{2,1,0:T(8,128)(2,1)S(1)}, u32[]{:S(2)}, u32[]{:S(2)}) async-start(bf16[32,80,128]{2,1,0:T(8,128)(2,1)} %decode_partials.1), calls=%async_computation | async-start | bytes 1310720 | tf_op jit(solution)/shard_map/all_to_all | solution.py:347
  35.2 3.1 %collective-permute-start.4 = (bf16[4,64,512]{2,1,0:T(8,128)(2,1)S(1)}, bf16[4,64,512]{2,1,0:T(8,128)(2,1)}, u32[]{:S(2)}, u32[]{:S(2)}) collective-permute-start(bf16[4,64,512]{2,1,0:T(8,128)(2,1)S(1)} %pad_maximum_fusion.refs_1_), channel_id=1, source_target_pairs={{0,224},{8,232},{16,240},{24,248},{32,0},{40,8},{48,16},{56,24},{6... | collective-permute-start | bytes 786440 | tf_op jit(solution)/shard_map/ppermute | solution.py:288
  40.0 2.5 %collective-permute-start.14 = (bf16[64,512]{1,0:T(8,128)(2,1)}, bf16[64,512]{1,0:T(8,128)(2,1)S(1)}, u32[]{:S(2)}, u32[]{:S(2)}) collective-permute-start(bf16[64,512]{1,0:T(8,128)(2,1)} %collective-permute-done.12), channel_id=1, source_target_pairs={{0,224},{8,232},{16,240},{24,248},{32,0},{40,8},{48,16},{56,24},{6... | collective-permute-start | bytes 196616 | tf_op jit(solution)/shard_map/ppermute | solution.py:288
  43.4 13.8 %collective-permute-done.13 = bf16[64,512]{1,0:T(8,128)(2,1)S(1)} collective-permute-done((bf16[64,512]{1,0:T(8,128)(2,1)}, bf16[64,512]{1,0:T(8,128)(2,1)S(1)}, u32[]{:S(2)}, u32[]{:S(2)}) %collective-permute-start.13) | collective-permute-done | bytes 65568 | tf_op jit(solution)/shard_map/ppermute | solution.py:288
  57.2 3.2 %collective-permute-start.16 = (bf16[64,512]{1,0:T(8,128)(2,1)S(1)}, bf16[64,512]{1,0:T(8,128)(2,1)S(1)}, u32[]{:S(2)}, u32[]{:S(2)}) collective-permute-start(bf16[64,512]{1,0:T(8,128)(2,1)S(1)} %collective-permute-done.14), channel_id=1, source_target_pairs={{0,224},{8,232},{16,240},{24,248},{32,0},{40,8},{48,16},{56,24},{6... | collective-permute-start | bytes 196616 | tf_op jit(solution)/shard_map/ppermute | solution.py:288
  60.5 2.2 %collective-permute-done.15 = bf16[64,512]{1,0:T(8,128)(2,1)S(1)} collective-permute-done((bf16[64,512]{1,0:T(8,128)(2,1)S(1)}, bf16[64,512]{1,0:T(8,128)(2,1)S(1)}, u32[]{:S(2)}, u32[]{:S(2)}) %collective-permute-start.15) | collective-permute-done | bytes 65568 | tf_op jit(solution)/shard_map/ppermute | solution.py:288
  62.7 5.4 %collective-permute-done.17 = bf16[64,512]{1,0:T(8,128)(2,1)S(1)} collective-permute-done((bf16[64,512]{1,0:T(8,128)(2,1)S(1)}, bf16[64,512]{1,0:T(8,128)(2,1)S(1)}, u32[]{:S(2)}, u32[]{:S(2)}) %collective-permute-start.17) | collective-permute-done | bytes 65568 | tf_op jit(solution)/shard_map/ppermute | solution.py:288
  69.6 1.8 %collective-permute-start.19 = (bf16[8,64,512]{2,1,0:T(8,128)(2,1)S(1)}, bf16[8,64,512]{2,1,0:T(8,128)(2,1)S(1)}, u32[]{:S(2)}, u32[]{:S(2)}) collective-permute-start(bf16[8,64,512]{2,1,0:T(8,128)(2,1)S(1)} %bitcast_dynamic-update-slice_fusion.refs_10_), channel_id=1, source_target_pairs={{0,24},{8,0},{16,8},{24,16},{32,56},{40,32},{48,40},{56,48},{64,88... | collective-permute-start | bytes 1572872 | tf_op jit(solution)/shard_map/ppermute | solution.py:288
  75.0 6.2 %all-to-all-start.1 = ((bf16[32,72,128]{2,1,0:T(8,128)(2,1)}), bf16[32,72,128]{2,1,0:T(8,128)(2,1)}, u32[]{:S(2)}, u32[]{:S(2)}) async-start(bf16[32,72,128]{2,1,0:T(8,128)(2,1)} %broadcast_in_dim.2), calls=%async_computation.1 | async-start | bytes 1179648 | tf_op jit(solution)/shard_map/all_to_all | solution.py:349
  81.2 3.1 %collective-permute-start.6 = (bf16[4,64,512]{2,1,0:T(8,128)(2,1)}, bf16[4,64,512]{2,1,0:T(8,128)(2,1)S(1)}, u32[]{:S(2)}, u32[]{:S(2)}) collective-permute-start(bf16[4,64,512]{2,1,0:T(8,128)(2,1)} %collective-permute-done.4.refs_3_), channel_id=1, source_target_pairs={{0,224},{8,232},{16,240},{24,248},{32,0},{40,8},{48,16},{56,24},{6... | collective-permute-start | bytes 786440 | tf_op jit(solution)/shard_map/ppermute | solution.py:288
  84.3 13.5 %collective-permute-done.6.refs_5_ = bf16[4,64,512]{2,1,0:T(8,128)(2,1)S(1)} collective-permute-done((bf16[4,64,512]{2,1,0:T(8,128)(2,1)}, bf16[4,64,512]{2,1,0:T(8,128)(2,1)S(1)}, u32[]{:S(2)}, u32[]{:S(2)}) %collective-permute-start.6) | collective-permute-done | bytes 262176 | tf_op jit(solution)/shard_map/ppermute | solution.py:288
  101.4 1.9 %collective-permute-start.21 = (bf16[4,64,512]{2,1,0:T(8,128)(2,1)S(1)}, bf16[4,64,512]{2,1,0:T(8,128)(2,1)S(1)}, u32[]{:S(2)}, u32[]{:S(2)}) collective-permute-start(bf16[4,64,512]{2,1,0:T(8,128)(2,1)S(1)} %slice.29), channel_id=1, source_target_pairs={{0,24},{8,0},{16,8},{24,16},{32,56},{40,32},{48,40},{56,48},{64,88... | collective-permute-start | bytes 786440 | tf_op jit(solution)/shard_map/ppermute | solution.py:288
  103.3 2.0 %collective-permute-done.8.refs_7_ = bf16[4,64,512]{2,1,0:T(8,128)(2,1)S(1)} collective-permute-done((bf16[4,64,512]{2,1,0:T(8,128)(2,1)S(1)}, bf16[4,64,512]{2,1,0:T(8,128)(2,1)S(1)}, u32[]{:S(2)}, u32[]{:S(2)}) %collective-permute-start.8) | collective-permute-done | bytes 262176 | tf_op jit(solution)/shard_map/ppermute | solution.py:288
  105.2 2.2 %collective-permute-start.10 = (bf16[2,64,512]{2,1,0:T(8,128)(2,1)S(1)}, bf16[2,64,512]{2,1,0:T(8,128)(2,1)S(1)}, u32[]{:S(2)}, u32[]{:S(2)}) collective-permute-start(bf16[2,64,512]{2,1,0:T(8,128)(2,1)S(1)} %slice.26), channel_id=1, source_target_pairs={{0,224},{8,232},{16,240},{24,248},{32,0},{40,8},{48,16},{56,24},{6... | collective-permute-start | bytes 393224 | tf_op jit(solution)/shard_map/ppermute | solution.py:288
  107.5 2.8 %collective-permute-done.10.refs_9_ = bf16[2,64,512]{2,1,0:T(8,128)(2,1)S(1)} collective-permute-done((bf16[2,64,512]{2,1,0:T(8,128)(2,1)S(1)}, bf16[2,64,512]{2,1,0:T(8,128)(2,1)S(1)}, u32[]{:S(2)}, u32[]{:S(2)}) %collective-permute-start.10) | collective-permute-done | bytes 131104 | tf_op jit(solution)/shard_map/ppermute | solution.py:288
  110.3 3.4 %collective-permute-done.9.refs_8_ = bf16[2,64,512]{2,1,0:T(8,128)(2,1)S(1)} collective-permute-done((bf16[2,64,512]{2,1,0:T(8,128)(2,1)S(1)}, bf16[2,64,512]{2,1,0:T(8,128)(2,1)S(1)}, u32[]{:S(2)}, u32[]{:S(2)}) %collective-permute-start.9) | collective-permute-done | bytes 131104 | tf_op jit(solution)/shard_map/ppermute | solution.py:288
  113.7 27.6 %prefill.1 = bf16[128,3072]{1,0:T(8,128)(2,1)} custom-call(s32[32]{0:T(128)S(1)} %copy-done.4, s32[1]{0:T(128)} %bitcast.ctx_ref, bf16[128,3072]{1,0:T(8,128)(2,1)S(1)} %copy-done.3, bf16[4,64,512]{2,1,0:T(8,128)(2,1)S(1)} %pad_maximum_fusion.refs_1_, bf16[4,64,512]{2,1,0:T(8,128)(2,1)} %collective-permute-done.3.refs_2_, ...), custom_call_target="tpu_custom_call" | custom-call | flops 4294967296 | bytes 6291456 | tf_op jit(solution)/shard_map/prefill/pallas_call | solution.py:258
  (66 shorter events, 19.6 us)
Async XLA Ops:
  3.8 34.6 %collective-permute-start.11 = (bf16[64,512]{1,0:T(8,128)(2,1)}, bf16[64,512]{1,0:T(8,128)(2,1)}, u32[]{:S(2)}, u32[]{:S(2)}) collective-permute-start(bf16[64,512]{1,0:T(8,128)(2,1)} %get-tuple-element.4), channel_id=1, source_target_pairs={{0,32},{8,40},{16,48},{24,56},{32,64},{40,72},{48,80},{56,88},{64,... | collective-permute-start | bytes 196616 | tf_op jit(solution)/shard_map/ppermute | solution.py:288
  5.7 34.3 %collective-permute-start.12 = (bf16[64,512]{1,0:T(8,128)(2,1)}, bf16[64,512]{1,0:T(8,128)(2,1)}, u32[]{:S(2)}, u32[]{:S(2)}) collective-permute-start(bf16[64,512]{1,0:T(8,128)(2,1)} %get-tuple-element.4), channel_id=1, source_target_pairs={{0,224},{8,232},{16,240},{24,248},{32,0},{40,8},{48,16},{56,24},{6... | collective-permute-start | bytes 196616 | tf_op jit(solution)/shard_map/ppermute | solution.py:288
  9.7 24.6 %collective-permute-start = (bf16[64,512]{1,0:T(8,128)(2,1)}, bf16[64,512]{1,0:T(8,128)(2,1)}, u32[]{:S(2)}, u32[]{:S(2)}) collective-permute-start(bf16[64,512]{1,0:T(8,128)(2,1)} %get-tuple-element.6), channel_id=1, source_target_pairs={{0,8},{8,16},{16,24},{24,0},{32,40},{40,48},{48,56},{56,32},{64,72... | collective-permute-start | bytes 196616 | tf_op jit(solution)/shard_map/ppermute | solution.py:288
  11.1 23.1 %collective-permute-start.1 = (bf16[64,512]{1,0:T(8,128)(2,1)}, bf16[64,512]{1,0:T(8,128)(2,1)}, u32[]{:S(2)}, u32[]{:S(2)}) collective-permute-start(bf16[64,512]{1,0:T(8,128)(2,1)} %get-tuple-element.6), channel_id=1, source_target_pairs={{0,24},{8,0},{16,8},{24,16},{32,56},{40,32},{48,40},{56,48},{64,88... | collective-permute-start | bytes 196616 | tf_op jit(solution)/shard_map/ppermute | solution.py:288
  12.9 21.4 %collective-permute-start.2 = (bf16[64,512]{1,0:T(8,128)(2,1)}, bf16[64,512]{1,0:T(8,128)(2,1)}, u32[]{:S(2)}, u32[]{:S(2)}) collective-permute-start(bf16[64,512]{1,0:T(8,128)(2,1)} %get-tuple-element.6), channel_id=1, source_target_pairs={{0,16},{8,24},{16,0},{24,8},{32,48},{40,56},{48,32},{56,40},{64,80... | collective-permute-start | bytes 196616 | tf_op jit(solution)/shard_map/ppermute | solution.py:288
  26.8 46.3 %all-to-all-start = ((bf16[32,80,128]{2,1,0:T(8,128)(2,1)}), bf16[32,80,128]{2,1,0:T(8,128)(2,1)S(1)}, u32[]{:S(2)}, u32[]{:S(2)}) async-start(bf16[32,80,128]{2,1,0:T(8,128)(2,1)} %decode_partials.1), calls=%async_computation | async-start | bytes 1310720 | tf_op jit(solution)/shard_map/all_to_all | solution.py:347
  35.2 45.9 %collective-permute-start.4 = (bf16[4,64,512]{2,1,0:T(8,128)(2,1)S(1)}, bf16[4,64,512]{2,1,0:T(8,128)(2,1)}, u32[]{:S(2)}, u32[]{:S(2)}) collective-permute-start(bf16[4,64,512]{2,1,0:T(8,128)(2,1)S(1)} %pad_maximum_fusion.refs_1_), channel_id=1, source_target_pairs={{0,224},{8,232},{16,240},{24,248},{32,0},{40,8},{48,16},{56,24},{6... | collective-permute-start | bytes 786440 | tf_op jit(solution)/shard_map/ppermute | solution.py:288
  38.4 45.9 %collective-permute-start.3 = (bf16[4,64,512]{2,1,0:T(8,128)(2,1)S(1)}, bf16[4,64,512]{2,1,0:T(8,128)(2,1)}, u32[]{:S(2)}, u32[]{:S(2)}) collective-permute-start(bf16[4,64,512]{2,1,0:T(8,128)(2,1)S(1)} %pad_maximum_fusion.refs_1_), channel_id=1, source_target_pairs={{0,32},{8,40},{16,48},{24,56},{32,64},{40,72},{48,80},{56,88},{64,... | collective-permute-start | bytes 786440 | tf_op jit(solution)/shard_map/ppermute | solution.py:288
  38.4 18.8 %collective-permute-start.13 = (bf16[64,512]{1,0:T(8,128)(2,1)}, bf16[64,512]{1,0:T(8,128)(2,1)S(1)}, u32[]{:S(2)}, u32[]{:S(2)}) collective-permute-start(bf16[64,512]{1,0:T(8,128)(2,1)} %collective-permute-done.11), channel_id=1, source_target_pairs={{0,32},{8,40},{16,48},{24,56},{32,64},{40,72},{48,80},{56,88},{64,... | collective-permute-start | bytes 196616 | tf_op jit(solution)/shard_map/ppermute | solution.py:288
  40.0 17.2 %collective-permute-start.14 = (bf16[64,512]{1,0:T(8,128)(2,1)}, bf16[64,512]{1,0:T(8,128)(2,1)S(1)}, u32[]{:S(2)}, u32[]{:S(2)}) collective-permute-start(bf16[64,512]{1,0:T(8,128)(2,1)} %collective-permute-done.12), channel_id=1, source_target_pairs={{0,224},{8,232},{16,240},{24,248},{32,0},{40,8},{48,16},{56,24},{6... | collective-permute-start | bytes 196616 | tf_op jit(solution)/shard_map/ppermute | solution.py:288
  57.2 5.5 %collective-permute-start.15 = (bf16[64,512]{1,0:T(8,128)(2,1)S(1)}, bf16[64,512]{1,0:T(8,128)(2,1)S(1)}, u32[]{:S(2)}, u32[]{:S(2)}) collective-permute-start(bf16[64,512]{1,0:T(8,128)(2,1)S(1)} %collective-permute-done.13), channel_id=1, source_target_pairs={{0,32},{8,40},{16,48},{24,56},{32,64},{40,72},{48,80},{56,88},{64,... | collective-permute-start | bytes 196616 | tf_op jit(solution)/shard_map/ppermute | solution.py:288
  57.2 5.5 %collective-permute-start.16 = (bf16[64,512]{1,0:T(8,128)(2,1)S(1)}, bf16[64,512]{1,0:T(8,128)(2,1)S(1)}, u32[]{:S(2)}, u32[]{:S(2)}) collective-permute-start(bf16[64,512]{1,0:T(8,128)(2,1)S(1)} %collective-permute-done.14), channel_id=1, source_target_pairs={{0,224},{8,232},{16,240},{24,248},{32,0},{40,8},{48,16},{56,24},{6... | collective-permute-start | bytes 196616 | tf_op jit(solution)/shard_map/ppermute | solution.py:288
  62.7 5.5 %collective-permute-start.17 = (bf16[64,512]{1,0:T(8,128)(2,1)S(1)}, bf16[64,512]{1,0:T(8,128)(2,1)S(1)}, u32[]{:S(2)}, u32[]{:S(2)}) collective-permute-start(bf16[64,512]{1,0:T(8,128)(2,1)S(1)} %collective-permute-done.15), channel_id=1, source_target_pairs={{0,32},{8,40},{16,48},{24,56},{32,64},{40,72},{48,80},{56,88},{64,... | collective-permute-start | bytes 196616 | tf_op jit(solution)/shard_map/ppermute | solution.py:288
  68.2 31.7 %collective-permute-start.18 = (bf16[8,64,512]{2,1,0:T(8,128)(2,1)S(1)}, bf16[8,64,512]{2,1,0:T(8,128)(2,1)S(1)}, u32[]{:S(2)}, u32[]{:S(2)}) collective-permute-start(bf16[8,64,512]{2,1,0:T(8,128)(2,1)S(1)} %bitcast_dynamic-update-slice_fusion.refs_10_), channel_id=1, source_target_pairs={{0,8},{8,16},{16,24},{24,0},{32,40},{40,48},{48,56},{56,32},{64,72... | collective-permute-start | bytes 1572872 | tf_op jit(solution)/shard_map/ppermute | solution.py:288
  69.6 31.8 %collective-permute-start.19 = (bf16[8,64,512]{2,1,0:T(8,128)(2,1)S(1)}, bf16[8,64,512]{2,1,0:T(8,128)(2,1)S(1)}, u32[]{:S(2)}, u32[]{:S(2)}) collective-permute-start(bf16[8,64,512]{2,1,0:T(8,128)(2,1)S(1)} %bitcast_dynamic-update-slice_fusion.refs_10_), channel_id=1, source_target_pairs={{0,24},{8,0},{16,8},{24,16},{32,56},{40,32},{48,40},{56,48},{64,88... | collective-permute-start | bytes 1572872 | tf_op jit(solution)/shard_map/ppermute | solution.py:288
  75.0 66.3 %all-to-all-start.1 = ((bf16[32,72,128]{2,1,0:T(8,128)(2,1)}), bf16[32,72,128]{2,1,0:T(8,128)(2,1)}, u32[]{:S(2)}, u32[]{:S(2)}) async-start(bf16[32,72,128]{2,1,0:T(8,128)(2,1)} %broadcast_in_dim.2), calls=%async_computation.1 | async-start | bytes 1179648 | tf_op jit(solution)/shard_map/all_to_all | solution.py:349
  81.2 16.6 %collective-permute-start.6 = (bf16[4,64,512]{2,1,0:T(8,128)(2,1)}, bf16[4,64,512]{2,1,0:T(8,128)(2,1)S(1)}, u32[]{:S(2)}, u32[]{:S(2)}) collective-permute-start(bf16[4,64,512]{2,1,0:T(8,128)(2,1)} %collective-permute-done.4.refs_3_), channel_id=1, source_target_pairs={{0,224},{8,232},{16,240},{24,248},{32,0},{40,8},{48,16},{56,24},{6... | collective-permute-start | bytes 786440 | tf_op jit(solution)/shard_map/ppermute | solution.py:288
  84.3 15.1 %collective-permute-start.5 = (bf16[4,64,512]{2,1,0:T(8,128)(2,1)}, bf16[4,64,512]{2,1,0:T(8,128)(2,1)S(1)}, u32[]{:S(2)}, u32[]{:S(2)}) collective-permute-start(bf16[4,64,512]{2,1,0:T(8,128)(2,1)} %collective-permute-done.3.refs_2_), channel_id=1, source_target_pairs={{0,32},{8,40},{16,48},{24,56},{32,64},{40,72},{48,80},{56,88},{64,... | collective-permute-start | bytes 786440 | tf_op jit(solution)/shard_map/ppermute | solution.py:288
  97.8 7.4 %collective-permute-start.8 = (bf16[4,64,512]{2,1,0:T(8,128)(2,1)S(1)}, bf16[4,64,512]{2,1,0:T(8,128)(2,1)S(1)}, u32[]{:S(2)}, u32[]{:S(2)}) collective-permute-start(bf16[4,64,512]{2,1,0:T(8,128)(2,1)S(1)} %collective-permute-done.6.refs_5_), channel_id=1, source_target_pairs={{0,224},{8,232},{16,240},{24,248},{32,0},{40,8},{48,16},{56,24},{6... | collective-permute-start | bytes 786440 | tf_op jit(solution)/shard_map/ppermute | solution.py:288
  99.3 8.1 %collective-permute-start.7 = (bf16[4,64,512]{2,1,0:T(8,128)(2,1)S(1)}, bf16[4,64,512]{2,1,0:T(8,128)(2,1)S(1)}, u32[]{:S(2)}, u32[]{:S(2)}) collective-permute-start(bf16[4,64,512]{2,1,0:T(8,128)(2,1)S(1)} %collective-permute-done.5.refs_4_), channel_id=1, source_target_pairs={{0,32},{8,40},{16,48},{24,56},{32,64},{40,72},{48,80},{56,88},{64,... | collective-permute-start | bytes 786440 | tf_op jit(solution)/shard_map/ppermute | solution.py:288
  99.9 13.8 %collective-permute-start.20 = (bf16[4,64,512]{2,1,0:T(8,128)(2,1)S(1)}, bf16[4,64,512]{2,1,0:T(8,128)(2,1)S(1)}, u32[]{:S(2)}, u32[]{:S(2)}) collective-permute-start(bf16[4,64,512]{2,1,0:T(8,128)(2,1)S(1)} %slice.28), channel_id=1, source_target_pairs={{0,8},{8,16},{16,24},{24,0},{32,40},{40,48},{48,56},{56,32},{64,72... | collective-permute-start | bytes 786440 | tf_op jit(solution)/shard_map/ppermute | solution.py:288
  101.4 12.3 %collective-permute-start.21 = (bf16[4,64,512]{2,1,0:T(8,128)(2,1)S(1)}, bf16[4,64,512]{2,1,0:T(8,128)(2,1)S(1)}, u32[]{:S(2)}, u32[]{:S(2)}) collective-permute-start(bf16[4,64,512]{2,1,0:T(8,128)(2,1)S(1)} %slice.29), channel_id=1, source_target_pairs={{0,24},{8,0},{16,8},{24,16},{32,56},{40,32},{48,40},{56,48},{64,88... | collective-permute-start | bytes 786440 | tf_op jit(solution)/shard_map/ppermute | solution.py:288
  105.2 5.0 %collective-permute-start.10 = (bf16[2,64,512]{2,1,0:T(8,128)(2,1)S(1)}, bf16[2,64,512]{2,1,0:T(8,128)(2,1)S(1)}, u32[]{:S(2)}, u32[]{:S(2)}) collective-permute-start(bf16[2,64,512]{2,1,0:T(8,128)(2,1)S(1)} %slice.26), channel_id=1, source_target_pairs={{0,224},{8,232},{16,240},{24,248},{32,0},{40,8},{48,16},{56,24},{6... | collective-permute-start | bytes 393224 | tf_op jit(solution)/shard_map/ppermute | solution.py:288
  107.4 6.3 %collective-permute-start.9 = (bf16[2,64,512]{2,1,0:T(8,128)(2,1)S(1)}, bf16[2,64,512]{2,1,0:T(8,128)(2,1)S(1)}, u32[]{:S(2)}, u32[]{:S(2)}) collective-permute-start(bf16[2,64,512]{2,1,0:T(8,128)(2,1)S(1)} %slice.25), channel_id=1, source_target_pairs={{0,32},{8,40},{16,48},{24,56},{32,64},{40,72},{48,80},{56,88},{64,... | collective-permute-start | bytes 393224 | tf_op jit(solution)/shard_map/ppermute | solution.py:288
  (7 other events, 130.6 us)

commit v2 on v1

v2 whole, which is shorter than its diff:
```python
import functools

import jax
import jax.numpy as jnp
from jax import lax
from jax.experimental import pallas as pl
from jax.experimental.pallas import tpu as pltpu
from jax.sharding import PartitionSpec as P

D = 128
HEADS = 96
KV_HEADS = 8
GROUP = HEADS // KV_HEADS
KV_LOC = 2
H_LOC = KV_LOC * GROUP
HALF = 64
NZ, NX = 8, 4
N = NZ * NX
REQ = 32
STEPS = 3
ROWS = STEPS * H_LOC
PAY = ROWS + 8
NEG = -1e30
C2 = float(D**-0.5 * 1.4426950408889634)
CHUNK = 512
LANES = 256
QROWS = GROUP * HALF
VMEM_LIMIT = 48 * 1024 * 1024
RB = 4


def row_iota(shape):
    return lax.broadcasted_iota(jnp.int32, shape, 0)


def lane_iota(shape):
    return lax.broadcasted_iota(jnp.int32, shape, 1)


def dot_t(a, b):
    return lax.dot_general(a, b, (((1,), (1,)), ((), ())), preferred_element_type=jnp.float32)


def dot(a, b):
    return lax.dot_general(a, b, (((1,), (0,)), ((), ())), preferred_element_type=jnp.float32)


def dot_tl(a, b):
    return lax.dot_general(a, b, (((0,), (0,)), ((), ())), preferred_element_type=jnp.float32)


def to_lanes(col_bc, rows):
    diag = row_iota((rows, D)) == lane_iota((rows, D))
    return jnp.sum(jnp.where(diag, col_bc, 0.0), axis=0, keepdims=True)


def split(x, terms):
    out = []
    for _ in range(terms):
        out.append(x.astype(jnp.bfloat16).astype(jnp.float32))
        x = x - out[-1]
    return out


def decode_kernel(ctx_ref, len_ref, q_ref, k_ref, v_ref, out_ref):
    first = ctx_ref[0] * D
    step = pl.program_id(0)
    shape = (ROWS, 2 * D)
    lane = lane_iota(shape)
    kv_of_row = (lax.rem(row_iota(shape), H_LOC) >= GROUP).astype(jnp.int32)
    kv_of_lane = (lane >= D).astype(jnp.int32)
    same = kv_of_row == kv_of_lane
    slot = jnp.where(lane >= D, lane - D, lane) + first
    sub = row_iota((8, D))
    for i in range(RB):
        length = len_ref[step * RB + i]
        k = k_ref[i]
        v = v_ref[i]
        k2 = jnp.concatenate([k[:, :D], k[:, D:]], axis=0)
        v2 = jnp.concatenate([v[:, :D], v[:, D:]], axis=0)
        s = dot_t(q_ref[i], k2) * C2
        live = same & (slot < length)
        s = jnp.where(live, s, NEG)
        top = jnp.max(s, axis=1, keepdims=True)
        p = jnp.where(live, jnp.exp2(s - top), 0.0)
        total = jnp.sum(p, axis=1, keepdims=True)
        o = dot(p.astype(jnp.bfloat16), v2)
        tail = jnp.zeros((8, D), jnp.float32)
        for j, term in enumerate(split(top, 3) + split(total, 2)):
            tail = jnp.where(sub == j, to_lanes(jnp.broadcast_to(term, (ROWS, D)), ROWS), tail)
        out_ref[i] = jnp.concatenate([o, tail], axis=0).astype(jnp.bfloat16)


def decode_partials(ctx, cache_len, q72, cache_k, cache_v):
    return pl.pallas_call(
        decode_kernel,
        out_shape=jax.ShapeDtypeStruct((REQ, PAY, D), jnp.bfloat16),
        grid_spec=pltpu.PrefetchScalarGridSpec(
            num_scalar_prefetch=2,
            grid=(REQ // RB,),
            in_specs=[
                pl.BlockSpec((RB, ROWS, D), lambda i, c, n: (i, 0, 0)),
                pl.BlockSpec((RB, D, 2 * D), lambda i, c, n: (i, 0, 0)),
                pl.BlockSpec((RB, D, 2 * D), lambda i, c, n: (i, 0, 0)),
            ],
            out_specs=pl.BlockSpec((RB, PAY, D), lambda i, c, n: (i, 0, 0)),
        ),
        compiler_params=pltpu.CompilerParams(vmem_limit_bytes=VMEM_LIMIT),
        cost_estimate=pl.CostEstimate(
            flops=REQ * ROWS * 256 * D * 4, bytes_accessed=6 * 2**20, transcendentals=REQ * ROWS * 256
        ),
        name="decode_partials",
    )(ctx, cache_len, q72, cache_k, cache_v)


def combine_kernel(ctx_ref, recv_ref, q_ref, dk_ref, dv_ref, out_ref):
    dk = dk_ref[0].astype(jnp.float32)
    dv = dv_ref[0].astype(jnp.float32)
    k2 = jnp.concatenate([dk[:, :D], dk[:, D:]], axis=0).astype(jnp.bfloat16)
    v2 = jnp.concatenate([dv[:, :D], dv[:, D:]], axis=0).astype(jnp.bfloat16)
    s = dot_t(q_ref[0], k2) * C2
    shape = (ROWS, 16)
    row, lane = row_iota(shape), lane_iota(shape)
    kv_of_row = (lax.rem(row, H_LOC) >= GROUP).astype(jnp.int32)
    kv_of_lane = (lane >= 8).astype(jnp.int32)
    token = jnp.where(lane >= 8, lane - 8, lane)
    time = (row >= H_LOC).astype(jnp.int32) + (row >= 2 * H_LOC).astype(jnp.int32)
    seen = (kv_of_row == kv_of_lane) & (token <= time)
    s = jnp.where(seen, s, NEG)
    d_top = jnp.max(s, axis=1, keepdims=True)
    p = jnp.where(seen, jnp.exp2(s - d_top), 0.0)
    d_total = jnp.sum(p, axis=1, keepdims=True)
    d_out = dot(p.astype(jnp.bfloat16), v2)
    d_m = to_lanes(jnp.broadcast_to(d_top, (ROWS, D)), ROWS)
    d_l = to_lanes(jnp.broadcast_to(d_total, (ROWS, D)), ROWS)

    tails = recv_ref[:, ROWS:, :].astype(jnp.float32)
    m = (tails[:, 0, :] + tails[:, 1, :]) + tails[:, 2, :]
    total = tails[:, 3, :] + tails[:, 4, :]
    top = jnp.maximum(jnp.max(m, axis=0, keepdims=True), d_m)
    w = jnp.exp2(m - top)
    w_d = jnp.exp2(d_m - top)
    whole = jnp.sum(w * total, axis=0, keepdims=True) + w_d * d_l
    inv = 1.0 / jnp.where(whole > 0.0, whole, 1.0)
    w_all = jnp.concatenate([w * inv, jnp.broadcast_to(w_d * inv, (8, D)), jnp.zeros((D - N - 8, D), jnp.float32)], axis=0)
    w_cols = jnp.transpose(w_all)[:ROWS]
    acc = d_out * w_cols[:, N : N + 1]
    for src in range(N):
        acc = acc + recv_ref[src, :ROWS, :].astype(jnp.float32) * w_cols[:, src : src + 1]
    out_ref[...] = acc.astype(jnp.bfloat16)


def combine(ctx, recv, q72, dk8, dv8):
    return pl.pallas_call(
        combine_kernel,
        out_shape=jax.ShapeDtypeStruct((ROWS, D), jnp.bfloat16),
        grid_spec=pltpu.PrefetchScalarGridSpec(
            num_scalar_prefetch=1,
            grid=(1,),
            in_specs=[
                pl.BlockSpec((N, PAY, D), lambda i, c: (0, 0, 0)),
                pl.BlockSpec((1, ROWS, D), lambda i, c: (c[0], 0, 0)),
                pl.BlockSpec((1, 8, 2 * D), lambda i, c: (c[0], 0, 0)),
                pl.BlockSpec((1, 8, 2 * D), lambda i, c: (c[0], 0, 0)),
            ],
            out_specs=pl.BlockSpec((ROWS, D), lambda i, c: (0, 0)),
        ),
        compiler_params=pltpu.CompilerParams(vmem_limit_bytes=VMEM_LIMIT),
        cost_estimate=pl.CostEstimate(flops=4 * 2**20, bytes_accessed=2**20, transcendentals=2**14),
        name="combine",
    )(ctx, recv, q72, dk8, dv8)


def prefill_kernel(pair_ref, ctx_ref, *refs, blocks, first, final):
    refs = list(refs)
    q_ref = refs.pop(0)
    srcs = [refs.pop(0) for _ in blocks]
    if not first:
        acc_in, ml_in = refs.pop(0), refs.pop(0)
    if final:
        out_ref = refs.pop(0)
    else:
        acc_out, ml_out = refs.pop(0), refs.pop(0)
    kv_lo, kv_hi, qs, m_ref, l_ref, acc_ref, sems = refs
    ctx = ctx_ref[0]
    z, x = ctx // NX, lax.rem(ctx, NX)
    b = pair_ref[ctx]

    places = [(ref, j, dz, dx) for ref, at in zip(srcs, blocks) for j, (dz, dx) in enumerate(at)]
    n = len(places)
    pairs = [pair_ref[lax.rem(z + NZ - dz, NZ) * NX + lax.rem(x + NX - dx, NX)] for _, _, dz, dx in places]
    made = []
    n_lo = n_hi = jnp.int32(0)
    for i, (ref, j, _, _) in enumerate(places):
        rank = jnp.int32(0)
        for k in range(n):
            if k != i:
                rank = rank + (pairs[k] < pairs[i]).astype(jnp.int32)
        n_lo = n_lo + (pairs[i] < b).astype(jnp.int32)
        n_hi = n_hi + (pairs[i] > b).astype(jnp.int32)
        for half, dst, r in ((0, kv_lo, rank), (1, kv_hi, n - 1 - rank)):
            copy = pltpu.make_async_copy(
                ref.at[j, pl.ds(half * HALF, HALF)],
                dst.at[pl.ds(pl.multiple_of(r * HALF, HALF), HALF)],
                sems.at[len(made)],
            )
            copy.start()
            made.append(copy)
    for part in range(2):
        for kv in range(KV_LOC):
            rows = [
                q_ref[part * HALF : (part + 1) * HALF, (kv * GROUP + g) * D : (kv * GROUP + g + 1) * D]
                for g in range(GROUP)
            ]
            t = jnp.transpose(jnp.concatenate(rows, axis=0).astype(jnp.float32) * C2)
            top = t.astype(jnp.bfloat16)
            qs[part, kv, :D, :] = top
            qs[part, kv, D:, :] = (t - top.astype(jnp.float32)).astype(jnp.bfloat16)
    if first:
        m_ref[...] = jnp.full_like(m_ref, NEG)
        l_ref[...] = jnp.zeros_like(l_ref)
        acc_ref[...] = jnp.zeros_like(acc_ref)
    else:
        acc_ref[...] = acc_in[...]
        m_ref[...] = ml_in[:, :, 0:1, :]
        l_ref[...] = ml_in[:, :, 1:2, :]
    for copy in made:
        copy.wait()

    def step(ref, part, start, limit, diag):
        keys, values = [], []
        for kv in range(KV_LOC):
            k = ref[pl.ds(start, CHUNK), kv * D : (kv + 1) * D]
            keys.append(jnp.concatenate([k, k], axis=1))
            values.append(ref[pl.ds(start, CHUNK), (KV_LOC + kv) * D : (KV_LOC + kv + 1) * D])

        def score(kv, r):
            s = dot(keys[kv], qs[part, kv, :, r : r + LANES])
            if limit is not None:
                pos = start + row_iota((CHUNK, LANES))
                own = limit + (lane_iota((CHUNK, LANES)) & (HALF - 1)) if diag else limit - 1
                s = jnp.where(pos <= own, s, NEG)
            return s

        def soft(kv, r, s):
            at = slice(r, r + LANES)
            old = m_ref[part, kv, :, at]
            new = jnp.maximum(old, jnp.max(s, axis=0, keepdims=True))
            alpha = jnp.exp2(old - new)
            p = jnp.exp2(s - new)
            m_ref[part, kv, :, at] = new
            l_ref[part, kv, :, at] = l_ref[part, kv, :, at] * alpha + jnp.sum(p, axis=0, keepdims=True)
            return alpha, p.astype(jnp.bfloat16)

        def mix(kv, r, alpha, p):
            at = slice(r, r + LANES)
            acc_ref[part, kv, :, at] = acc_ref[part, kv, :, at] * alpha + dot_tl(values[kv], p)

        units = [(kv, r) for kv in range(KV_LOC) for r in range(0, QROWS, LANES)]
        s = score(*units[0])
        pending = None
        for i, u in enumerate(units):
            following = score(*units[i + 1]) if i + 1 < len(units) else None
            if pending is not None:
                mix(*pending)
            pending = (*u, *soft(*u, s))
            s = following
        mix(*pending)

    def dense(ref, part, count):
        @pl.loop(0, count)
        def _(i):
            step(ref, part, pl.multiple_of(i * CHUNK, CHUNK), None, False)

    def prefix(ref, part, count):
        limit = count * HALF
        full = limit // CHUNK
        dense(ref, part, full)
        start = pl.multiple_of(full * CHUNK, CHUNK)
        if first:
            step(ref, part, start, limit, True)
        else:

            @pl.when(limit > full * CHUNK)
            def _():
                step(ref, part, start, limit, False)

    dense(kv_lo, 1, n * HALF // CHUNK)
    prefix(kv_lo, 0, n_lo)
    prefix(kv_hi, 1, n_hi)
    if final:
        for part in range(2):
            for kv in range(KV_LOC):
                o = jnp.transpose(acc_ref[part, kv] / l_ref[part, kv])
                for g in range(GROUP):
                    h = kv * GROUP + g
                    out_ref[part * HALF : (part + 1) * HALF, h * D : (h + 1) * D] = o[g * HALF : (g + 1) * HALF].astype(
                        jnp.bfloat16
                    )
    else:
        acc_out[...] = acc_ref[...]
        ml_out[:, :, 0:1, :] = m_ref[...]
        ml_out[:, :, 1:2, :] = l_ref[...]
        ml_out[:, :, 2:, :] = jnp.zeros_like(ml_out[:, :, 2:, :])


def prefill(block_pair, ctx, queries, arrays, blocks, state, final):
    n = sum(len(at) for at in blocks)
    first = state is None
    acc = jax.ShapeDtypeStruct((2, KV_LOC, D, QROWS), jnp.float32)
    ml = jax.ShapeDtypeStruct((2, KV_LOC, 8, QROWS), jnp.float32)
    vmem = pl.BlockSpec(memory_space=pltpu.VMEM)
    return pl.pallas_call(
        functools.partial(prefill_kernel, blocks=blocks, first=first, final=final),
        out_shape=jax.ShapeDtypeStruct(queries.shape, jnp.bfloat16) if final else (acc, ml),
        in_specs=[pl.BlockSpec(memory_space=pltpu.SMEM)] * 2
        + [vmem]
        + [pl.BlockSpec(memory_space=pl.ANY)] * len(arrays)
        + ([] if first else [vmem, vmem]),
        out_specs=vmem if final else (vmem, vmem),
        scratch_shapes=[pltpu.VMEM((n * HALF, 2 * KV_LOC * D), jnp.bfloat16)] * 2
        + [pltpu.VMEM((2, KV_LOC, 2 * D, QROWS), jnp.bfloat16)]
        + [pltpu.VMEM((2, KV_LOC, 1, QROWS), jnp.float32)] * 2
        + [pltpu.VMEM((2, KV_LOC, D, QROWS), jnp.float32), pltpu.SemaphoreType.DMA((2 * n,))],
        compiler_params=pltpu.CompilerParams(vmem_limit_bytes=VMEM_LIMIT),
        cost_estimate=pl.CostEstimate(
            flops=n * 2**28, bytes_accessed=4 * 2**20, transcendentals=n * 2**18
        ),
        name="prefill_end" if final else "prefill_start",
    )(block_pair, ctx, queries, *arrays, *(() if first else state))


def shift(x, dz, dx):
    def to(i):
        z, xx = divmod(i, NX)
        return ((z + dz) % NZ) * NX + (xx + dx) % NX

    return lax.ppermute(x, "ctx", [(i, to(i)) for i in range(N)])


def gather(own):
    cat = functools.partial(jnp.concatenate, axis=0)
    up1, down1 = shift(own, 1, 0), shift(own, -1, 0)
    near = cat([own, up1, down1])
    near_z = [0, 1, -1]
    right1, left1 = shift(near, 0, 1), shift(near, 0, -1)
    up2, down2 = shift(near[:2], 2, 0), shift(cat([own, down1]), -2, 0)
    up4 = shift(up2[1:], 1, 0)
    far = cat([up2, down2, up4])
    far_z = [2, 3, -2, -3, 4]
    right2, left2 = shift(far, 0, 1), shift(far, 0, -1)
    right3 = shift(cat([right1[:2], right2[:2]]), 0, 1)
    left3 = shift(cat([left1[2:], left2[2:]]), 0, -1)
    early = [
        (near, [(d, 0) for d in near_z]),
        (right1, [(d, 1) for d in near_z]),
        (left1, [(d, -1) for d in near_z]),
        (far, [(d, 0) for d in far_z]),
        (right2, [(d, 1) for d in far_z]),
        (left2, [(d, -1) for d in far_z]),
    ]
    late = [
        (right3, [(d, 2) for d in near_z[:2] + far_z[:2]]),
        (left3, [(d, 2) for d in near_z[2:] + far_z[2:]]),
    ]
    return early, late


def local(
    prefill_queries,
    prefill_keys,
    prefill_values,
    block_pair,
    decode_queries,
    cache_keys,
    cache_values,
    draft_keys,
    draft_values,
    cache_len,
):
    ctx = lax.axis_index("ctx").astype(jnp.int32).reshape(1)
    kv = jnp.concatenate([prefill_keys, prefill_values], axis=1)
    early, late = gather(kv[None])

    q72 = decode_queries.reshape(REQ, ROWS, D)
    pad = ((0, 0), (0, 8 - STEPS), (0, 0))
    dk8, dv8 = jnp.pad(draft_keys, pad), jnp.pad(draft_values, pad)
    partials = decode_partials(ctx, cache_len, q72, cache_keys, cache_values)
    recv = lax.all_to_all(partials, "ctx", 0, 0, tiled=True)
    done = combine(ctx, recv, q72, dk8, dv8)
    spread = lax.all_to_all(jnp.broadcast_to(done[None], (N, ROWS, D)), "ctx", 0, 0, tiled=True)
    decode_out = spread.reshape(REQ, STEPS, H_LOC * D)

    parts = [([a for a, _ in group], [at for _, at in group]) for group in (early, late)]
    state = prefill(block_pair, ctx, prefill_queries, *parts[0], None, False)
    prefill_out = prefill(block_pair, ctx, prefill_queries, *parts[1], state, True)
    return (prefill_out, decode_out)


def solution(mesh):
    return jax.shard_map(
        local,
        mesh=mesh,
        in_specs=(
            P(("rep", "ctx"), "head"),
            P(("rep", "ctx"), "head"),
            P(("rep", "ctx"), "head"),
            P("rep"),
            P("rep", None, "head"),
            P("rep", "ctx", "head"),
            P("rep", "ctx", "head"),
            P("rep", None, "head"),
            P("rep", None, "head"),
            P("rep"),
        ),
        out_specs=(P(("rep", "ctx"), "head"), P("rep", None, "head")),
        check_vma=False,
    )
```

time: 144 us -> 124 us (0.86)
  starting transfers between devices: 48.1 us -> 37.1 us
  Pallas kernels: 36.9 us -> 31.9 us
  local copies, waits for them, and re-layouts: 13.5 us -> 9.15 us
  other arithmetic: 0.94 us -> 3.93 us
  waiting for transfers between devices: 43.1 us -> 40.5 us
    ppermute x22 -> x11, starting transfers between devices: 34.6 us -> 21.1 us  [shift(): return lax.ppermute(x, 'ctx', [(i, to(i)) for i in range(N)])]
    pallas_call x1 -> x2, Pallas kernels: 27.6 us -> 22.6 us  [prefill(): pl.pallas_call(functools.partial(prefill_kernel, blocks=blocks, first=fir...]
    unnamed x26 -> x20, local copies, waits for them, and re-layouts: 9.34 us -> 5.76 us
    ppermute x22 -> x11, waiting for transfers between devices: 43.1 us -> 40.5 us  [shift(): return lax.ppermute(x, 'ctx', [(i, to(i)) for i in range(N)])]
    concatenate x0 -> x4, other arithmetic: none -> 2.25 us  [the longest x1 1.07 us: gather(): near = cat([own, up1, down1])]
    broadcast_in_dim x0 -> x1, other arithmetic: none -> 1.68 us  [local(): early, late = gather(kv[None])]
  transfers between devices with their start and end apart: 24 -> 13, of which waited for: 7 -> 4; matrix products, arithmetic and copies ran while one was open for 5% -> 7% of each run, Pallas kernels for 26% -> 26%
where the time goes in v2:
time: 124 us; the launch traced here: 123 us
  waiting for transfers between devices  40.5 us (33%)
  starting transfers between devices  37.1 us (30%)
  Pallas kernels  31.9 us (26%)
  local copies, waits for them, and re-layouts  9.15 us (7%)
  other arithmetic  3.93 us (3%)
    ppermute x11, waiting for transfers between devices, shift(): return lax.ppermute(x, 'ctx', [(i, to(i)) for i in range(N)])  40.5 us
    pallas_call x2, Pallas kernels, prefill(): pl.pallas_call(functools.partial(prefill_kernel, blocks=blocks, first=fir...  22.6 us
    ppermute x11, starting transfers between devices, shift(): return lax.ppermute(x, 'ctx', [(i, to(i)) for i in range(N)])  21.1 us
    all_to_all x1, starting transfers between devices, local(): recv = lax.all_to_all(partials, 'ctx', 0, 0, tiled=True)  8.82 us
    pallas_call x1, Pallas kernels, decode_partials(): pl.pallas_call(decode_kernel, out_shape=jax.ShapeDtypeStruct((REQ, PAY, D...  8.38 us
    all_to_all x1, starting transfers between devices, local(): lax.all_to_all(jnp.broadcast_to(done[None], (N, ROWS, D)), 'ctx', 0, 0, t...  7.12 us
    unnamed x20, local copies, waits for them, and re-layouts  5.76 us
  transfers between devices with their start and end apart: 13, of which 4 were waited for; matrix products, arithmetic and copies ran while one was open for 7% of the time, Pallas kernels for 26%

profile of v2, /device:TPU:16, one launch (start us, length us, event | category | flops | bytes accessed | tf_op | source)
XLA Modules:
  0.0 123.5 jit_solution(11927687826440895580)
XLA Ops:
  0.7 1.7 %maximum_bitcast_fusion = bf16[1,128,512]{2,1,0:T(8,128)(2,1)} fusion(bf16[128,256]{1,0:T(8,128)(2,1)} %param.12, bf16[128,256]{1,0:T(8,128)(2,1)} %param.11), kind=kLoop, calls=%fused_computation.5 | loop fusion | flops 262144 | bytes 262144 | tf_op jit(solution)/shard_map/broadcast_in_dim | solution.py:383
  2.3 1.9 %collective-permute-start = (bf16[1,128,512]{2,1,0:T(8,128)(2,1)}, bf16[1,128,512]{2,1,0:T(8,128)(2,1)}, u32[]{:S(2)}, u32[]{:S(2)}) collective-permute-start(bf16[1,128,512]{2,1,0:T(8,128)(2,1)} %maximum_bitcast_fusion), channel_id=1, source_target_pairs={{0,32},{8,40},{16,48},{24,56},{32,64},{40,72},{48,80},{56,88},{64,... | collective-permute-start | bytes 393224 | tf_op jit(solution)/shard_map/ppermute | solution.py:338
  4.3 3.9 %collective-permute-start.1 = (bf16[1,128,512]{2,1,0:T(8,128)(2,1)}, bf16[1,128,512]{2,1,0:T(8,128)(2,1)}, u32[]{:S(2)}, u32[]{:S(2)}) collective-permute-start(bf16[1,128,512]{2,1,0:T(8,128)(2,1)} %maximum_bitcast_fusion), channel_id=1, source_target_pairs={{0,224},{8,232},{16,240},{24,248},{32,0},{40,8},{48,16},{56,24},{6... | collective-permute-start | bytes 393224 | tf_op jit(solution)/shard_map/ppermute | solution.py:338
  8.2 1.6 %copy.15 = bf16[32,3,3072]{2,1,0:T(4,128)(2,1)S(1)} copy(bf16[32,3,3072]{2,0,1:T(8,128)(2,1)} %param.14) | data formatting | bytes 1179648 | tf_op args[4]
  10.4 1.6 %copy-done.1 = bf16[32,128,256]{2,1,0:T(8,128)(2,1)S(1)} copy-done((bf16[32,128,256]{2,1,0:T(8,128)(2,1)S(1)}, bf16[32,128,256]{2,1,0:T(8,128)(2,1)}, u32[]{:S(2)}) %copy-start.1) | copy-done | bytes 2097176
  11.9 8.4 %decode_partials.1 = bf16[32,80,128]{2,1,0:T(8,128)(2,1)} custom-call(s32[1]{0:T(128)} %bitcast.ctx_ref, s32[32]{0:T(128)S(1)} %copy-done.2, bf16[32,72,128]{2,1,0:T(8,128)(2,1)S(1)} %reshape.15.q_ref, bf16[32,128,256]{2,1,0:T(8,128)(2,1)S(1)} %copy-done, bf16[32,128,256]{2,1,0:T(8,128)(2,1)S(1)} %copy-done.1), custom_call_target="tpu_custom_call" | custom-call | flops 301989888 | bytes 6291456 | tf_op jit(solution)/shard_map/decode_partials/pallas_call | solution.py:95
  20.3 8.8 %all-to-all-start = ((bf16[32,80,128]{2,1,0:T(8,128)(2,1)}), bf16[32,80,128]{2,1,0:T(8,128)(2,1)S(1)}, u32[]{:S(2)}, u32[]{:S(2)}) async-start(bf16[32,80,128]{2,1,0:T(8,128)(2,1)} %decode_partials.1), calls=%async_computation | async-start | bytes 1310720 | tf_op jit(solution)/shard_map/all_to_all | solution.py:389
  29.2 1.1 pad_maximum_fusion.3
  30.2 2.8 %collective-permute-start.3 = (bf16[2,128,512]{2,1,0:T(8,128)(2,1)S(1)}, bf16[2,128,512]{2,1,0:T(8,128)(2,1)S(1)}, u32[]{:S(2)}, u32[]{:S(2)}) collective-permute-start(bf16[2,128,512]{2,1,0:T(8,128)(2,1)S(1)} %get-tuple-element.9), channel_id=1, source_target_pairs={{0,64},{8,72},{16,80},{24,88},{32,96},{40,104},{48,112},{56,120},{... | collective-permute-start | bytes 786440 | tf_op jit(solution)/shard_map/ppermute | solution.py:338
  33.0 1.4 %collective-permute-start.4 = (bf16[2,128,512]{2,1,0:T(8,128)(2,1)S(1)}, bf16[2,128,512]{2,1,0:T(8,128)(2,1)S(1)}, u32[]{:S(2)}, u32[]{:S(2)}) collective-permute-start(bf16[2,128,512]{2,1,0:T(8,128)(2,1)S(1)} %get-tuple-element.8), channel_id=1, source_target_pairs={{0,192},{8,200},{16,208},{24,216},{32,224},{40,232},{48,240},{56,2... | collective-permute-start | bytes 786440 | tf_op jit(solution)/shard_map/ppermute | solution.py:338
  34.5 21.7 %collective-permute-done.3 = bf16[2,128,512]{2,1,0:T(8,128)(2,1)S(1)} collective-permute-done((bf16[2,128,512]{2,1,0:T(8,128)(2,1)S(1)}, bf16[2,128,512]{2,1,0:T(8,128)(2,1)S(1)}, u32[]{:S(2)}, u32[]{:S(2)}) %collective-permute-start.3) | collective-permute-done | bytes 262176 | tf_op jit(solution)/shard_map/ppermute | solution.py:338
  56.2 2.5 %collective-permute-start.5 = (bf16[1,128,512]{2,1,0:T(8,128)(2,1)S(1)}, bf16[1,128,512]{2,1,0:T(8,128)(2,1)S(1)}, u32[]{:S(2)}, u32[]{:S(2)}) collective-permute-start(bf16[1,128,512]{2,1,0:T(8,128)(2,1)S(1)} %slice.23), channel_id=1, source_target_pairs={{0,32},{8,40},{16,48},{24,56},{32,64},{40,72},{48,80},{56,88},{64,... | collective-permute-start | bytes 393224 | tf_op jit(solution)/shard_map/ppermute | solution.py:338
  60.2 2.3 %collective-permute-done.5 = bf16[1,128,512]{2,1,0:T(8,128)(2,1)S(1)} collective-permute-done((bf16[1,128,512]{2,1,0:T(8,128)(2,1)S(1)}, bf16[1,128,512]{2,1,0:T(8,128)(2,1)S(1)}, u32[]{:S(2)}, u32[]{:S(2)}) %collective-permute-start.5) | collective-permute-done | bytes 131104 | tf_op jit(solution)/shard_map/ppermute | solution.py:338
  63.1 2.9 %collective-permute-start.9 = (bf16[5,128,512]{2,1,0:T(8,128)(2,1)}, bf16[5,128,512]{2,1,0:T(8,128)(2,1)S(1)}, u32[]{:S(2)}, u32[]{:S(2)}) collective-permute-start(bf16[5,128,512]{2,1,0:T(8,128)(2,1)} %constant_dynamic-update-slice_fusion.refs_4_), channel_id=1, source_target_pairs={{0,24},{8,0},{16,8},{24,16},{32,56},{40,32},{48,40},{56,48},{64,88... | collective-permute-start | bytes 1966088 | tf_op jit(solution)/shard_map/ppermute | solution.py:338
  66.0 1.1 pad_maximum_fusion.2.refs_1_
  67.0 3.3 %collective-permute-start.8 = (bf16[3,128,512]{2,1,0:T(8,128)(2,1)S(1)}, bf16[3,128,512]{2,1,0:T(8,128)(2,1)S(1)}, u32[]{:S(2)}, u32[]{:S(2)}) collective-permute-start(bf16[3,128,512]{2,1,0:T(8,128)(2,1)S(1)} %pad_maximum_fusion.2.refs_1_), channel_id=1, source_target_pairs={{0,24},{8,0},{16,8},{24,16},{32,56},{40,32},{48,40},{56,48},{64,88... | collective-permute-start | bytes 1179656 | tf_op jit(solution)/shard_map/ppermute | solution.py:338
  72.4 7.1 %all-to-all-start.1 = ((bf16[32,72,128]{2,1,0:T(8,128)(2,1)}), bf16[32,72,128]{2,1,0:T(8,128)(2,1)S(1)}, u32[]{:S(2)}, u32[]{:S(2)}) async-start(bf16[32,72,128]{2,1,0:T(8,128)(2,1)} %broadcast_in_dim.10), calls=%async_computation.1 | async-start | bytes 1179648 | tf_op jit(solution)/shard_map/all_to_all | solution.py:391
  79.5 13.5 %collective-permute-done.8.refs_3_ = bf16[3,128,512]{2,1,0:T(8,128)(2,1)S(1)} collective-permute-done((bf16[3,128,512]{2,1,0:T(8,128)(2,1)S(1)}, bf16[3,128,512]{2,1,0:T(8,128)(2,1)S(1)}, u32[]{:S(2)}, u32[]{:S(2)}) %collective-permute-start.8) | collective-permute-done | bytes 393248 | tf_op jit(solution)/shard_map/ppermute | solution.py:338
  93.0 3.0 %collective-permute-done.2.refs_2_ = bf16[3,128,512]{2,1,0:T(8,128)(2,1)S(1)} collective-permute-done((bf16[3,128,512]{2,1,0:T(8,128)(2,1)S(1)}, bf16[3,128,512]{2,1,0:T(8,128)(2,1)S(1)}, u32[]{:S(2)}, u32[]{:S(2)}) %collective-permute-start.2) | collective-permute-done | bytes 393248 | tf_op jit(solution)/shard_map/ppermute | solution.py:338
  96.8 1.0 slice.24
  97.9 1.7 %collective-permute-start.7 = (bf16[4,128,512]{2,1,0:T(8,128)(2,1)S(1)}, bf16[4,128,512]{2,1,0:T(8,128)(2,1)S(1)}, u32[]{:S(2)}, u32[]{:S(2)}) collective-permute-start(bf16[4,128,512]{2,1,0:T(8,128)(2,1)S(1)} %pad_maximum_fusion), channel_id=1, source_target_pairs={{0,8},{8,16},{16,24},{24,0},{32,40},{40,48},{48,56},{56,32},{64,72... | collective-permute-start | bytes 1572872 | tf_op jit(solution)/shard_map/ppermute | solution.py:338
  99.6 14.4 %prefill_start.1 = (f32[2,2,128,768]{3,2,1,0:T(8,128)S(1)}, f32[2,2,8,768]{3,2,1,0:T(8,128)S(1)}) custom-call(s32[32]{0:T(128)S(1)} %copy-done.4, s32[1]{0:T(128)} %bitcast.ctx_ref, bf16[128,3072]{1,0:T(8,128)(2,1)S(1)} %copy-done.3, bf16[3,128,512]{2,1,0:T(8,128)(2,1)S(1)} %pad_maximum_fusion.2.refs_1_, ...), custom_call_target="tpu_custom_call" | custom-call | flops 6442450944 | bytes 4194304 | tf_op jit(solution)/shard_map/prefill_start/pallas_call | solution.py:313
  114.0 8.2 %prefill_end.1 = bf16[128,3072]{1,0:T(8,128)(2,1)} custom-call(s32[32]{0:T(128)S(1)} %copy-done.4, s32[1]{0:T(128)} %bitcast.ctx_ref, bf16[128,3072]{1,0:T(8,128)(2,1)S(1)} %copy-done.3, bf16[4,128,512]{2,1,0:T(8,128)(2,1)S(1)} %collective-permute-done.7.refs_1_, bf16[4,128,512]{2,1,0:T(8,128)(2,1)S(1)} %collective-permute-done.10.refs_2_, ...), custom_call_target="tpu_custom_call" | custom-call | flops 2147483648 | bytes 4194304 | tf_op jit(solution)/shard_map/prefill_end/pallas_call | solution.py:313
  122.4 1.0 copy.18
  (42 shorter events, 5.7 us)
Async XLA Ops:
  0.6 9.7 %copy-start = (bf16[32,128,256]{2,1,0:T(8,128)(2,1)S(1)}, bf16[32,128,256]{2,1,0:T(8,128)(2,1)}, u32[]{:S(2)}) copy-start(bf16[32,128,256]{2,1,0:T(8,128)(2,1)} %k_ref.1) | copy-start | bytes 6291460
  0.6 9.7 %copy-start.2 = (s32[32]{0:T(128)S(1)}, s32[32]{0:T(128)}, u32[]{:S(2)}) copy-start(s32[32]{0:T(128)} %len_ref.1) | copy-start | bytes 388
  2.3 26.8 %collective-permute-start = (bf16[1,128,512]{2,1,0:T(8,128)(2,1)}, bf16[1,128,512]{2,1,0:T(8,128)(2,1)}, u32[]{:S(2)}, u32[]{:S(2)}) collective-permute-start(bf16[1,128,512]{2,1,0:T(8,128)(2,1)} %maximum_bitcast_fusion), channel_id=1, source_target_pairs={{0,32},{8,40},{16,48},{24,56},{32,64},{40,72},{48,80},{56,88},{64,... | collective-permute-start | bytes 393224 | tf_op jit(solution)/shard_map/ppermute | solution.py:338
  4.3 24.9 %collective-permute-start.1 = (bf16[1,128,512]{2,1,0:T(8,128)(2,1)}, bf16[1,128,512]{2,1,0:T(8,128)(2,1)}, u32[]{:S(2)}, u32[]{:S(2)}) collective-permute-start(bf16[1,128,512]{2,1,0:T(8,128)(2,1)} %maximum_bitcast_fusion), channel_id=1, source_target_pairs={{0,224},{8,232},{16,240},{24,248},{32,0},{40,8},{48,16},{56,24},{6... | collective-permute-start | bytes 393224 | tf_op jit(solution)/shard_map/ppermute | solution.py:338
  10.3 1.6 %copy-start.1 = (bf16[32,128,256]{2,1,0:T(8,128)(2,1)S(1)}, bf16[32,128,256]{2,1,0:T(8,128)(2,1)}, u32[]{:S(2)}) copy-start(bf16[32,128,256]{2,1,0:T(8,128)(2,1)} %v_ref.1) | copy-start | bytes 6291460
  20.3 50.0 %copy-start.5 = (bf16[32,3,256]{2,0,1:T(8,128)(2,1)S(1)}, bf16[32,3,256]{2,0,1:T(8,128)(2,1)}, u32[]{:S(2)}) copy-start(bf16[32,3,256]{2,0,1:T(8,128)(2,1)} %param.17) | copy-start | bytes 147460
  20.3 50.1 %copy-start.6 = (bf16[32,3,256]{2,0,1:T(8,128)(2,1)S(1)}, bf16[32,3,256]{2,0,1:T(8,128)(2,1)}, u32[]{:S(2)}) copy-start(bf16[32,3,256]{2,0,1:T(8,128)(2,1)} %param.18) | copy-start | bytes 147460
  20.3 50.2 %all-to-all-start = ((bf16[32,80,128]{2,1,0:T(8,128)(2,1)}), bf16[32,80,128]{2,1,0:T(8,128)(2,1)S(1)}, u32[]{:S(2)}, u32[]{:S(2)}) async-start(bf16[32,80,128]{2,1,0:T(8,128)(2,1)} %decode_partials.1), calls=%async_computation | async-start | bytes 1310720 | tf_op jit(solution)/shard_map/all_to_all | solution.py:389
  30.2 25.9 %collective-permute-start.3 = (bf16[2,128,512]{2,1,0:T(8,128)(2,1)S(1)}, bf16[2,128,512]{2,1,0:T(8,128)(2,1)S(1)}, u32[]{:S(2)}, u32[]{:S(2)}) collective-permute-start(bf16[2,128,512]{2,1,0:T(8,128)(2,1)S(1)} %get-tuple-element.9), channel_id=1, source_target_pairs={{0,64},{8,72},{16,80},{24,88},{32,96},{40,104},{48,112},{56,120},{... | collective-permute-start | bytes 786440 | tf_op jit(solution)/shard_map/ppermute | solution.py:338
  33.0 26.4 %collective-permute-start.4 = (bf16[2,128,512]{2,1,0:T(8,128)(2,1)S(1)}, bf16[2,128,512]{2,1,0:T(8,128)(2,1)S(1)}, u32[]{:S(2)}, u32[]{:S(2)}) collective-permute-start(bf16[2,128,512]{2,1,0:T(8,128)(2,1)S(1)} %get-tuple-element.8), channel_id=1, source_target_pairs={{0,192},{8,200},{16,208},{24,216},{32,224},{40,232},{48,240},{56,2... | collective-permute-start | bytes 786440 | tf_op jit(solution)/shard_map/ppermute | solution.py:338
  56.2 6.3 %collective-permute-start.5 = (bf16[1,128,512]{2,1,0:T(8,128)(2,1)S(1)}, bf16[1,128,512]{2,1,0:T(8,128)(2,1)S(1)}, u32[]{:S(2)}, u32[]{:S(2)}) collective-permute-start(bf16[1,128,512]{2,1,0:T(8,128)(2,1)S(1)} %slice.23), channel_id=1, source_target_pairs={{0,32},{8,40},{16,48},{24,56},{32,64},{40,72},{48,80},{56,88},{64,... | collective-permute-start | bytes 393224 | tf_op jit(solution)/shard_map/ppermute | solution.py:338
  63.1 33.0 %collective-permute-start.9 = (bf16[5,128,512]{2,1,0:T(8,128)(2,1)}, bf16[5,128,512]{2,1,0:T(8,128)(2,1)S(1)}, u32[]{:S(2)}, u32[]{:S(2)}) collective-permute-start(bf16[5,128,512]{2,1,0:T(8,128)(2,1)} %constant_dynamic-update-slice_fusion.refs_4_), channel_id=1, source_target_pairs={{0,24},{8,0},{16,8},{24,16},{32,56},{40,32},{48,40},{56,48},{64,88... | collective-permute-start | bytes 1966088 | tf_op jit(solution)/shard_map/ppermute | solution.py:338
  66.0 30.9 %collective-permute-start.6 = (bf16[5,128,512]{2,1,0:T(8,128)(2,1)}, bf16[5,128,512]{2,1,0:T(8,128)(2,1)}, u32[]{:S(2)}, u32[]{:S(2)}) collective-permute-start(bf16[5,128,512]{2,1,0:T(8,128)(2,1)} %constant_dynamic-update-slice_fusion.refs_4_), channel_id=1, source_target_pairs={{0,8},{8,16},{16,24},{24,0},{32,40},{40,48},{48,56},{56,32},{64,72... | collective-permute-start | bytes 1966088 | tf_op jit(solution)/shard_map/ppermute | solution.py:338
  67.0 26.0 %collective-permute-start.8 = (bf16[3,128,512]{2,1,0:T(8,128)(2,1)S(1)}, bf16[3,128,512]{2,1,0:T(8,128)(2,1)S(1)}, u32[]{:S(2)}, u32[]{:S(2)}) collective-permute-start(bf16[3,128,512]{2,1,0:T(8,128)(2,1)S(1)} %pad_maximum_fusion.2.refs_1_), channel_id=1, source_target_pairs={{0,24},{8,0},{16,8},{24,16},{32,56},{40,32},{48,40},{56,48},{64,88... | collective-permute-start | bytes 1179656 | tf_op jit(solution)/shard_map/ppermute | solution.py:338
  70.4 25.7 %collective-permute-start.2 = (bf16[3,128,512]{2,1,0:T(8,128)(2,1)S(1)}, bf16[3,128,512]{2,1,0:T(8,128)(2,1)S(1)}, u32[]{:S(2)}, u32[]{:S(2)}) collective-permute-start(bf16[3,128,512]{2,1,0:T(8,128)(2,1)S(1)} %pad_maximum_fusion.2.refs_1_), channel_id=1, source_target_pairs={{0,8},{8,16},{16,24},{24,0},{32,40},{40,48},{48,56},{56,32},{64,72... | collective-permute-start | bytes 1179656 | tf_op jit(solution)/shard_map/ppermute | solution.py:338
  72.4 49.8 %all-to-all-start.1 = ((bf16[32,72,128]{2,1,0:T(8,128)(2,1)}), bf16[32,72,128]{2,1,0:T(8,128)(2,1)S(1)}, u32[]{:S(2)}, u32[]{:S(2)}) async-start(bf16[32,72,128]{2,1,0:T(8,128)(2,1)} %broadcast_in_dim.10), calls=%async_computation.1 | async-start | bytes 1179648 | tf_op jit(solution)/shard_map/all_to_all | solution.py:391
  79.5 20.1 %copy-start.3 = (bf16[128,3072]{1,0:T(8,128)(2,1)S(1)}, bf16[128,3072]{1,0:T(8,128)(2,1)}, u32[]{:S(2)}) copy-start(bf16[128,3072]{1,0:T(8,128)(2,1)} %refs_0_.3) | copy-start | bytes 2359300
  79.5 20.1 %copy-start.4 = (s32[32]{0:T(128)S(1)}, s32[32]{0:T(128)}, u32[]{:S(2)}) copy-start(s32[32]{0:T(128)} %pair_ref.3) | copy-start | bytes 388
  96.2 17.8 %collective-permute-start.10 = (bf16[4,128,512]{2,1,0:T(8,128)(2,1)S(1)}, bf16[4,128,512]{2,1,0:T(8,128)(2,1)S(1)}, u32[]{:S(2)}, u32[]{:S(2)}) collective-permute-start(bf16[4,128,512]{2,1,0:T(8,128)(2,1)S(1)} %pad_maximum_fusion.1), channel_id=1, source_target_pairs={{0,24},{8,0},{16,8},{24,16},{32,56},{40,32},{48,40},{56,48},{64,88... | collective-permute-start | bytes 1572872 | tf_op jit(solution)/shard_map/ppermute | solution.py:338
  97.9 16.1 %collective-permute-start.7 = (bf16[4,128,512]{2,1,0:T(8,128)(2,1)S(1)}, bf16[4,128,512]{2,1,0:T(8,128)(2,1)S(1)}, u32[]{:S(2)}, u32[]{:S(2)}) collective-permute-start(bf16[4,128,512]{2,1,0:T(8,128)(2,1)S(1)} %pad_maximum_fusion), channel_id=1, source_target_pairs={{0,8},{8,16},{16,24},{24,0},{32,40},{40,48},{48,56},{56,32},{64,72... | collective-permute-start | bytes 1572872 | tf_op jit(solution)/shard_map/ppermute | solution.py:338

commit v3 on v2

--- a/solution.py
+++ b/solution.py
@@ -25,8 +25,8 @@
 CHUNK = 512
 LANES = 256
 QROWS = GROUP * HALF
-VMEM_LIMIT = 48 * 1024 * 1024
-RB = 4
+VMEM_LIMIT = 60 * 1024 * 1024
+RB = 8
 
 
 def row_iota(shape):
@@ -62,7 +62,7 @@
     return out
 
 
-def decode_kernel(ctx_ref, len_ref, q_ref, k_ref, v_ref, out_ref):
+def decode_kernel(ctx_ref, len_ref, q_ref, k_ref, v_ref, out_ref, q72_ref):
     first = ctx_ref[0] * D
     step = pl.program_id(0)
     shape = (ROWS, 2 * D)
@@ -72,45 +72,63 @@
     same = kv_of_row == kv_of_lane
     slot = jnp.where(lane >= D, lane - D, lane) + first
     sub = row_iota((8, D))
-    for i in range(RB):
-        length = len_ref[step * RB + i]
+    for t in range(STEPS):
+        heads = [q_ref[t, :, h * D : (h + 1) * D].astype(jnp.float32) for h in range(H_LOC)]
+        turned = jnp.transpose(jnp.stack(heads), (1, 0, 2))
+        q72_ref[:, t * H_LOC : (t + 1) * H_LOC, :] = turned.astype(jnp.bfloat16)
+
+    def score(i):
         k = k_ref[i]
-        v = v_ref[i]
         k2 = jnp.concatenate([k[:, :D], k[:, D:]], axis=0)
-        v2 = jnp.concatenate([v[:, :D], v[:, D:]], axis=0)
-        s = dot_t(q_ref[i], k2) * C2
-        live = same & (slot < length)
+        return dot_t(q72_ref[i], k2) * C2
+
+    def soft(i, s):
+        live = same & (slot < len_ref[step * RB + i])
         s = jnp.where(live, s, NEG)
         top = jnp.max(s, axis=1, keepdims=True)
         p = jnp.where(live, jnp.exp2(s - top), 0.0)
-        total = jnp.sum(p, axis=1, keepdims=True)
-        o = dot(p.astype(jnp.bfloat16), v2)
+        return top, jnp.sum(p, axis=1, keepdims=True), p.astype(jnp.bfloat16)
+
+    def mix(i, top, total, p):
+        v = v_ref[i]
+        o = dot(p, jnp.concatenate([v[:, :D], v[:, D:]], axis=0))
         tail = jnp.zeros((8, D), jnp.float32)
         for j, term in enumerate(split(top, 3) + split(total, 2)):
             tail = jnp.where(sub == j, to_lanes(jnp.broadcast_to(term, (ROWS, D)), ROWS), tail)
         out_ref[i] = jnp.concatenate([o, tail], axis=0).astype(jnp.bfloat16)
 
-
-def decode_partials(ctx, cache_len, q72, cache_k, cache_v):
+    scores = [score(i) for i in range(RB)]
+    weights = [soft(i, s) for i, s in enumerate(scores)]
+    for i, w in enumerate(weights):
+        mix(i, *w)
+
+
+def decode_partials(ctx, cache_len, queries, cache_k, cache_v):
     return pl.pallas_call(
         decode_kernel,
-        out_shape=jax.ShapeDtypeStruct((REQ, PAY, D), jnp.bfloat16),
+        out_shape=(
+            jax.ShapeDtypeStruct((REQ, PAY, D), jnp.bfloat16),
+            jax.ShapeDtypeStruct((REQ, ROWS, D), jnp.bfloat16),
+        ),
         grid_spec=pltpu.PrefetchScalarGridSpec(
             num_scalar_prefetch=2,
             grid=(REQ // RB,),
             in_specs=[
-                pl.BlockSpec((RB, ROWS, D), lambda i, c, n: (i, 0, 0)),
+                pl.BlockSpec((STEPS, RB, H_LOC * D), lambda i, c, n: (0, i, 0)),
                 pl.BlockSpec((RB, D, 2 * D), lambda i, c, n: (i, 0, 0)),
                 pl.BlockSpec((RB, D, 2 * D), lambda i, c, n: (i, 0, 0)),
             ],
-            out_specs=pl.BlockSpec((RB, PAY, D), lambda i, c, n: (i, 0, 0)),
+            out_specs=(
+                pl.BlockSpec((RB, PAY, D), lambda i, c, n: (i, 0, 0)),
+                pl.BlockSpec((RB, ROWS, D), lambda i, c, n: (i, 0, 0)),
+            ),
         ),
         compiler_params=pltpu.CompilerParams(vmem_limit_bytes=VMEM_LIMIT),
         cost_estimate=pl.CostEstimate(
             flops=REQ * ROWS * 256 * D * 4, bytes_accessed=6 * 2**20, transcendentals=REQ * ROWS * 256
         ),
         name="decode_partials",
-    )(ctx, cache_len, q72, cache_k, cache_v)
+    )(ctx, cache_len, queries, cache_k, cache_v)
 
 
 def combine_kernel(ctx_ref, recv_ref, q_ref, dk_ref, dv_ref, out_ref):
@@ -147,13 +165,15 @@
     acc = d_out * w_cols[:, N : N + 1]
     for src in range(N):
         acc = acc + recv_ref[src, :ROWS, :].astype(jnp.float32) * w_cols[:, src : src + 1]
-    out_ref[...] = acc.astype(jnp.bfloat16)
+    out = acc.astype(jnp.bfloat16)
+    for dst in range(N):
+        out_ref[dst] = out
 
 
 def combine(ctx, recv, q72, dk8, dv8):
     return pl.pallas_call(
         combine_kernel,
-        out_shape=jax.ShapeDtypeStruct((ROWS, D), jnp.bfloat16),
+        out_shape=jax.ShapeDtypeStruct((N, ROWS, D), jnp.bfloat16),
         grid_spec=pltpu.PrefetchScalarGridSpec(
             num_scalar_prefetch=1,
             grid=(1,),
@@ -163,7 +183,7 @@
                 pl.BlockSpec((1, 8, 2 * D), lambda i, c: (c[0], 0, 0)),
                 pl.BlockSpec((1, 8, 2 * D), lambda i, c: (c[0], 0, 0)),
             ],
-            out_specs=pl.BlockSpec((ROWS, D), lambda i, c: (0, 0)),
+            out_specs=pl.BlockSpec((N, ROWS, D), lambda i, c: (0, 0, 0)),
         ),
         compiler_params=pltpu.CompilerParams(vmem_limit_bytes=VMEM_LIMIT),
         cost_estimate=pl.CostEstimate(flops=4 * 2**20, bytes_accessed=2**20, transcendentals=2**14),
@@ -181,15 +201,18 @@
         out_ref = refs.pop(0)
     else:
         acc_out, ml_out = refs.pop(0), refs.pop(0)
-    kv_lo, kv_hi, qs, m_ref, l_ref, acc_ref, sems = refs
+    kv_lo, kv_hi, qs, m_ref, l_ref, acc_ref, q_vmem, ml_vmem, sems = refs
+    q_copy = pltpu.make_async_copy(q_ref, q_vmem, sems.at[0])
+    q_copy.start()
     ctx = ctx_ref[0]
     z, x = ctx // NX, lax.rem(ctx, NX)
     b = pair_ref[ctx]
 
     places = [(ref, j, dz, dx) for ref, at in zip(srcs, blocks) for j, (dz, dx) in enumerate(at)]
     n = len(places)
+    chunk = min(CHUNK, n * HALF)
     pairs = [pair_ref[lax.rem(z + NZ - dz, NZ) * NX + lax.rem(x + NX - dx, NX)] for _, _, dz, dx in places]
-    made = []
+    ranks, low, high = [], [], []
     n_lo = n_hi = jnp.int32(0)
     for i, (ref, j, _, _) in enumerate(places):
         rank = jnp.int32(0)
@@ -198,18 +221,31 @@
                 rank = rank + (pairs[k] < pairs[i]).astype(jnp.int32)
         n_lo = n_lo + (pairs[i] < b).astype(jnp.int32)
         n_hi = n_hi + (pairs[i] > b).astype(jnp.int32)
-        for half, dst, r in ((0, kv_lo, rank), (1, kv_hi, n - 1 - rank)):
-            copy = pltpu.make_async_copy(
-                ref.at[j, pl.ds(half * HALF, HALF)],
-                dst.at[pl.ds(pl.multiple_of(r * HALF, HALF), HALF)],
-                sems.at[len(made)],
-            )
+        ranks.append(rank)
+        copy = pltpu.make_async_copy(
+            ref.at[j, pl.ds(0, HALF)], kv_lo.at[pl.ds(pl.multiple_of(rank * HALF, HALF), HALF)], sems.at[4 + i]
+        )
+        copy.start()
+        low.append(copy)
+    for i, (ref, j, _, _) in enumerate(places):
+        rank = n - 1 - ranks[i]
+        copy = pltpu.make_async_copy(
+            ref.at[j, pl.ds(HALF, HALF)], kv_hi.at[pl.ds(pl.multiple_of(rank * HALF, HALF), HALF)], sems.at[4 + n + i]
+        )
+        copy.start()
+        high.append(copy)
+    if not first:
+        back = [
+            pltpu.make_async_copy(acc_in, acc_ref, sems.at[1]),
+            pltpu.make_async_copy(ml_in, ml_vmem, sems.at[2]),
+        ]
+        for copy in back:
             copy.start()
-            made.append(copy)
+    q_copy.wait()
     for part in range(2):
         for kv in range(KV_LOC):
             rows = [
-                q_ref[part * HALF : (part + 1) * HALF, (kv * GROUP + g) * D : (kv * GROUP + g + 1) * D]
+                q_vmem[part * HALF : (part + 1) * HALF, (kv * GROUP + g) * D : (kv * GROUP + g + 1) * D]
                 for g in range(GROUP)
             ]
             t = jnp.transpose(jnp.concatenate(rows, axis=0).astype(jnp.float32) * C2)
@@ -221,24 +257,28 @@
         l_ref[...] = jnp.zeros_like(l_ref)
         acc_ref[...] = jnp.zeros_like(acc_ref)
     else:
-        acc_ref[...] = acc_in[...]
-        m_ref[...] = ml_in[:, :, 0:1, :]
-        l_ref[...] = ml_in[:, :, 1:2, :]
-    for copy in made:
+        for copy in back:
+            copy.wait()
+        m_ref[...] = ml_vmem[:, :, 0:1, :]
+        l_ref[...] = ml_vmem[:, :, 1:2, :]
+    if kv_lo.shape[0] > n * HALF:
+        for ref in (kv_lo, kv_hi):
+            ref[n * HALF :, :] = jnp.zeros((ref.shape[0] - n * HALF, ref.shape[1]), ref.dtype)
+    for copy in low:
         copy.wait()
 
-    def step(ref, part, start, limit, diag):
+    def step(ref, part, start, limit, diag, width=chunk):
         keys, values = [], []
         for kv in range(KV_LOC):
-            k = ref[pl.ds(start, CHUNK), kv * D : (kv + 1) * D]
+            k = ref[pl.ds(start, width), kv * D : (kv + 1) * D]
             keys.append(jnp.concatenate([k, k], axis=1))
-            values.append(ref[pl.ds(start, CHUNK), (KV_LOC + kv) * D : (KV_LOC + kv + 1) * D])
+            values.append(ref[pl.ds(start, width), (KV_LOC + kv) * D : (KV_LOC + kv + 1) * D])
 
         def score(kv, r):
             s = dot(keys[kv], qs[part, kv, :, r : r + LANES])
             if limit is not None:
-                pos = start + row_iota((CHUNK, LANES))
-                own = limit + (lane_iota((CHUNK, LANES)) & (HALF - 1)) if diag else limit - 1
+                pos = start + row_iota((width, LANES))
+                own = limit + (lane_iota((width, LANES)) & (HALF - 1)) if diag else limit - 1
                 s = jnp.where(pos <= own, s, NEG)
             return s
 
@@ -268,25 +308,34 @@
         mix(*pending)
 
     def dense(ref, part, count):
+        if isinstance(count, int):
+            for i in range(count):
+                step(ref, part, i * chunk, None, False)
+            return
+
         @pl.loop(0, count)
         def _(i):
-            step(ref, part, pl.multiple_of(i * CHUNK, CHUNK), None, False)
+            step(ref, part, pl.multiple_of(i * chunk, chunk), None, False)
 
     def prefix(ref, part, count):
         limit = count * HALF
-        full = limit // CHUNK
+        full = limit // chunk
         dense(ref, part, full)
-        start = pl.multiple_of(full * CHUNK, CHUNK)
+        start = pl.multiple_of(full * chunk, chunk)
         if first:
             step(ref, part, start, limit, True)
         else:
 
-            @pl.when(limit > full * CHUNK)
+            @pl.when(limit > full * chunk)
             def _():
                 step(ref, part, start, limit, False)
 
-    dense(kv_lo, 1, n * HALF // CHUNK)
+    dense(kv_lo, 1, n * HALF // chunk)
+    if n * HALF % chunk:
+        step(kv_lo, 1, n * HALF // chunk * chunk, None, False, n * HALF % chunk)
     prefix(kv_lo, 0, n_lo)
+    for copy in high:
+        copy.wait()
     prefix(kv_hi, 1, n_hi)
     if final:
         for part in range(2):
@@ -298,30 +347,40 @@
                         jnp.bfloat16
                     )
     else:
-        acc_out[...] = acc_ref[...]
-        ml_out[:, :, 0:1, :] = m_ref[...]
-        ml_out[:, :, 1:2, :] = l_ref[...]
-        ml_out[:, :, 2:, :] = jnp.zeros_like(ml_out[:, :, 2:, :])
+        acc_copy = pltpu.make_async_copy(acc_ref, acc_out, sems.at[1])
+        acc_copy.start()
+        ml_vmem[:, :, 0:1, :] = m_ref[...]
+        ml_vmem[:, :, 1:2, :] = l_ref[...]
+        ml_vmem[:, :, 2:, :] = jnp.zeros((2, KV_LOC, 6, QROWS), jnp.float32)
+        ml_copy = pltpu.make_async_copy(ml_vmem, ml_out, sems.at[2])
+        ml_copy.start()
+        ml_copy.wait()
+        acc_copy.wait()
 
 
 def prefill(block_pair, ctx, queries, arrays, blocks, state, final):
     n = sum(len(at) for at in blocks)
     first = state is None
+    chunk = min(CHUNK, n * HALF)
+    rows = -(-n * HALF // chunk) * chunk
     acc = jax.ShapeDtypeStruct((2, KV_LOC, D, QROWS), jnp.float32)
     ml = jax.ShapeDtypeStruct((2, KV_LOC, 8, QROWS), jnp.float32)
-    vmem = pl.BlockSpec(memory_space=pltpu.VMEM)
+    anywhere = pl.BlockSpec(memory_space=pl.ANY)
     return pl.pallas_call(
         functools.partial(prefill_kernel, blocks=blocks, first=first, final=final),
         out_shape=jax.ShapeDtypeStruct(queries.shape, jnp.bfloat16) if final else (acc, ml),
         in_specs=[pl.BlockSpec(memory_space=pltpu.SMEM)] * 2
-        + [vmem]
-        + [pl.BlockSpec(memory_space=pl.ANY)] * len(arrays)
-        + ([] if first else [vmem, vmem]),
-        out_specs=vmem if final else (vmem, vmem),
-        scratch_shapes=[pltpu.VMEM((n * HALF, 2 * KV_LOC * D), jnp.bfloat16)] * 2
+        + [anywhere] * (1 + len(arrays) + (0 if first else 2)),
+        out_specs=pl.BlockSpec(memory_space=pltpu.VMEM) if final else (anywhere, anywhere),
+        scratch_shapes=[pltpu.VMEM((rows, 2 * KV_LOC * D), jnp.bfloat16)] * 2
         + [pltpu.VMEM((2, KV_LOC, 2 * D, QROWS), jnp.bfloat16)]
         + [pltpu.VMEM((2, KV_LOC, 1, QROWS), jnp.float32)] * 2
-        + [pltpu.VMEM((2, KV_LOC, D, QROWS), jnp.float32), pltpu.SemaphoreType.DMA((2 * n,))],
+        + [
+            pltpu.VMEM((2, KV_LOC, D, QROWS), jnp.float32),
+            pltpu.VMEM(queries.shape, jnp.bfloat16),
+            pltpu.VMEM((2, KV_LOC, 8, QROWS), jnp.float32),
+            pltpu.SemaphoreType.DMA((4 + 2 * n,)),
+        ],
         compiler_params=pltpu.CompilerParams(vmem_limit_bytes=VMEM_LIMIT),
         cost_estimate=pl.CostEstimate(
             flops=n * 2**28, bytes_accessed=4 * 2**20, transcendentals=n * 2**18
@@ -338,32 +397,38 @@
     return lax.ppermute(x, "ctx", [(i, to(i)) for i in range(N)])
 
 
-def gather(own):
-    cat = functools.partial(jnp.concatenate, axis=0)
-    up1, down1 = shift(own, 1, 0), shift(own, -1, 0)
-    near = cat([own, up1, down1])
-    near_z = [0, 1, -1]
-    right1, left1 = shift(near, 0, 1), shift(near, 0, -1)
-    up2, down2 = shift(near[:2], 2, 0), shift(cat([own, down1]), -2, 0)
-    up4 = shift(up2[1:], 1, 0)
-    far = cat([up2, down2, up4])
-    far_z = [2, 3, -2, -3, 4]
-    right2, left2 = shift(far, 0, 1), shift(far, 0, -1)
-    right3 = shift(cat([right1[:2], right2[:2]]), 0, 1)
-    left3 = shift(cat([left1[2:], left2[2:]]), 0, -1)
-    early = [
-        (near, [(d, 0) for d in near_z]),
-        (right1, [(d, 1) for d in near_z]),
-        (left1, [(d, -1) for d in near_z]),
-        (far, [(d, 0) for d in far_z]),
-        (right2, [(d, 1) for d in far_z]),
-        (left2, [(d, -1) for d in far_z]),
-    ]
-    late = [
-        (right3, [(d, 2) for d in near_z[:2] + far_z[:2]]),
-        (left3, [(d, 2) for d in near_z[2:] + far_z[2:]]),
-    ]
-    return early, late
+def cat(*arrays):
+    return jnp.concatenate(arrays, axis=0)
+
+
+def join_kernel(*refs, ranges):
+    *srcs, dst, sems = refs
+    copies, at = [], 0
+    for i, (src, (lo, hi)) in enumerate(zip(srcs, ranges)):
+        copies.append(pltpu.make_async_copy(src.at[pl.ds(lo, hi - lo)], dst.at[pl.ds(at, hi - lo)], sems.at[i]))
+        copies[-1].start()
+        at += hi - lo
+    for copy in copies:
+        copy.wait()
+
+
+def join(*pieces):
+    arrays = [a for a, _, _ in pieces]
+    ranges = [(lo, hi) for _, lo, hi in pieces]
+    rows = sum(hi - lo for lo, hi in ranges)
+    return pl.pallas_call(
+        functools.partial(join_kernel, ranges=ranges),
+        out_shape=jax.ShapeDtypeStruct((rows, *arrays[0].shape[1:]), arrays[0].dtype),
+        in_specs=[pl.BlockSpec(memory_space=pl.ANY)] * len(arrays),
+        out_specs=pl.BlockSpec(memory_space=pltpu.VMEM),
+        scratch_shapes=[pltpu.SemaphoreType.DMA((len(arrays),))],
+        cost_estimate=pl.CostEstimate(flops=0, bytes_accessed=rows * 2**18, transcendentals=0),
+        name="join",
+    )(*arrays)
+
+
+def after(x, *others):
+    return lax.optimization_barrier((x, *others))[0]
 
 
 def local(
@@ -379,21 +444,45 @@
     cache_len,
 ):
     ctx = lax.axis_index("ctx").astype(jnp.int32).reshape(1)
-    kv = jnp.concatenate([prefill_keys, prefill_values], axis=1)
-    early, late = gather(kv[None])
-
-    q72 = decode_queries.reshape(REQ, ROWS, D)
     pad = ((0, 0), (0, 8 - STEPS), (0, 0))
     dk8, dv8 = jnp.pad(draft_keys, pad), jnp.pad(draft_values, pad)
-    partials = decode_partials(ctx, cache_len, q72, cache_keys, cache_values)
-    recv = lax.all_to_all(partials, "ctx", 0, 0, tiled=True)
-    done = combine(ctx, recv, q72, dk8, dv8)
-    spread = lax.all_to_all(jnp.broadcast_to(done[None], (N, ROWS, D)), "ctx", 0, 0, tiled=True)
+
+    own = jnp.concatenate([prefill_keys, prefill_values], axis=1)[None]
+    up1, down1 = shift(own, 1, 0), shift(own, -1, 0)
+    near, near_z = cat(own, up1, down1), [0, 1, -1]
+    right1, left1, across1 = shift(near, 0, 1), shift(near, 0, -1), shift(near, 0, 2)
+    up2, down2 = shift(near[:2], 2, 0), shift(cat(own, down1), -2, 0)
+
+    turned = jnp.transpose(decode_queries, (1, 0, 2))
+    partials, q72 = decode_partials(ctx, after(cache_len, up1, down1), turned, cache_keys, cache_values)
+
+    up4 = shift(up2[1:], 1, 0)
+    recv = lax.all_to_all(after(partials, right1, left1, up2, down2, up4, across1), "ctx", 0, 0, tiled=True)
+    far, far_z = join((up2, 0, 2), (down2, 0, 2), (up4, 0, 1)), [2, 3, -2, -3, 4]
+    right2, left2 = shift(far, 0, 1), shift(far, 0, -1)
+
+    def at(zs, x):
+        return [(d, x) for d in zs]
+
+    state = prefill(
+        block_pair,
+        ctx,
+        prefill_queries,
+        [near, right1, left1, across1, far],
+        [at(near_z, 0), at(near_z, 1), at(near_z, -1), at(near_z, 2), at(far_z, 0)],
+        None,
+        False,
+    )
+    done = combine(after(ctx, *state, right2, left2), recv, q72, dk8, dv8)
+    spread = lax.all_to_all(done, "ctx", 0, 0, tiled=True)
     decode_out = spread.reshape(REQ, STEPS, H_LOC * D)
 
-    parts = [([a for a, _ in group], [at for _, at in group]) for group in (early, late)]
-    state = prefill(block_pair, ctx, prefill_queries, *parts[0], None, False)
-    prefill_out = prefill(block_pair, ctx, prefill_queries, *parts[1], state, True)
+    right3, left3 = shift(right2[:3], 0, 1), shift(left2[3:], 0, -1)
+    state = prefill(
+        after(block_pair, done), ctx, prefill_queries, [right2, left2], [at(far_z, 1), at(far_z, -1)], state, False
+    )
+    last = [at(far_z[:3], 2), at(far_z[3:], 2)]
+    prefill_out = prefill(block_pair, ctx, prefill_queries, [right3, left3], last, state, True)
     return (prefill_out, decode_out)
 
 

time: 124 us -> 104 us (0.84)
  waiting for transfers between devices: 40.5 us -> 23.1 us
  Pallas kernels: 31.9 us -> 37.3 us
  local copies, waits for them, and re-layouts: 9.15 us -> 4.4 us
  other arithmetic: 3.93 us -> 0.97 us
    ppermute x11 -> x12, waiting for transfers between devices: 40.5 us -> 23.1 us  [shift(): return lax.ppermute(x, 'ctx', [(i, to(i)) for i in range(N)])]
    pallas_call x2 -> x3, Pallas kernels: 22.6 us -> 26.5 us  [prefill(): pl.pallas_call(functools.partial(prefill_kernel, blocks=blocks, first=fir...]
    all_to_all x2, starting transfers between devices: 15.9 us -> 12.6 us  [the longest x1 7 us: local(): spread = lax.all_to_all(done, 'ctx', 0, 0, tiled=True)]
    unnamed x20 -> x31, local copies, waits for them, and re-layouts: 5.76 us -> 2.8 us
    ppermute x11 -> x12, starting transfers between devices: 21.1 us -> 24 us  [shift(): return lax.ppermute(x, 'ctx', [(i, to(i)) for i in range(N)])]
    concatenate x4 -> x2, other arithmetic: 2.25 us -> 0.09 us  [cat(): return jnp.concatenate(arrays, axis=0)]
    pallas_call x2 -> x3, Pallas kernels: 9.29 us -> 10.9 us  [the longest x1 6.09 us: decode_partials(): pl.pallas_call(decode_kernel, out_shape=(jax.ShapeDtypeStruct((REQ, PAY,...]
    pad x2, local copies, waits for them, and re-layouts: 0.05 us -> 1.35 us  [local(): dk8, dv8 = (jnp.pad(draft_keys, pad), jnp.pad(draft_values, pad))]
  transfers between devices with their start and end apart: 13 -> 14, of which waited for: 4 -> 6; matrix products, arithmetic and copies ran while one was open for 7% -> 1% of each run, Pallas kernels for 26% -> 33%
where the time goes in v3:
time: 104 us; the launch traced here: 103 us
  Pallas kernels  37.3 us (36%)
  starting transfers between devices  36.6 us (35%)
  waiting for transfers between devices  23.1 us (22%)
  local copies, waits for them, and re-layouts  4.4 us (4%)
    pallas_call x3, Pallas kernels, prefill(): pl.pallas_call(functools.partial(prefill_kernel, blocks=blocks, first=fir...  26.5 us
    ppermute x12, starting transfers between devices, shift(): return lax.ppermute(x, 'ctx', [(i, to(i)) for i in range(N)])  24 us
    ppermute x12, waiting for transfers between devices, shift(): return lax.ppermute(x, 'ctx', [(i, to(i)) for i in range(N)])  23.1 us
    all_to_all x1, starting transfers between devices, local(): spread = lax.all_to_all(done, 'ctx', 0, 0, tiled=True)  7 us
    pallas_call x1, Pallas kernels, decode_partials(): pl.pallas_call(decode_kernel, out_shape=(jax.ShapeDtypeStruct((REQ, PAY,...  6.09 us
    all_to_all x1, starting transfers between devices, local(): lax.all_to_all(after(partials, right1, left1, up2, down2, up4, across1),...  5.56 us
    pallas_call x1, Pallas kernels, combine(): pl.pallas_call(combine_kernel, out_shape=jax.ShapeDtypeStruct((N, ROWS, D...  2.86 us
    unnamed x31, local copies, waits for them, and re-layouts  2.8 us
  transfers between devices with their start and end apart: 14, of which 6 were waited for; matrix products, arithmetic and copies ran while one was open for 1% of the time, Pallas kernels for 33%

profile of v3, /device:TPU:16, one launch (start us, length us, event | category | flops | bytes accessed | tf_op | source)
XLA Modules:
  0.0 103.3 jit_solution(10731093906954861150)
XLA Ops:
  1.5 2.0 %collective-permute-start = (bf16[1,128,512]{2,1,0:T(8,128)(2,1)S(1)}, bf16[1,128,512]{2,1,0:T(8,128)(2,1)S(1)}, u32[]{:S(2)}, u32[]{:S(2)}) collective-permute-start(bf16[1,128,512]{2,1,0:T(8,128)(2,1)S(1)} %maximum_bitcast_fusion), channel_id=1, source_target_pairs={{0,32},{8,40},{16,48},{24,56},{32,64},{40,72},{48,80},{56,88},{64,... | collective-permute-start | bytes 393224 | tf_op jit(solution)/shard_map/ppermute | solution.py:397
  3.5 4.0 %collective-permute-start.2 = (bf16[1,128,512]{2,1,0:T(8,128)(2,1)S(1)}, bf16[1,128,512]{2,1,0:T(8,128)(2,1)S(1)}, u32[]{:S(2)}, u32[]{:S(2)}) collective-permute-start(bf16[1,128,512]{2,1,0:T(8,128)(2,1)S(1)} %maximum_bitcast_fusion), channel_id=1, source_target_pairs={{0,224},{8,232},{16,240},{24,248},{32,0},{40,8},{48,16},{56,24},{6... | collective-permute-start | bytes 393224 | tf_op jit(solution)/shard_map/ppermute | solution.py:397
  7.5 3.4 %collective-permute-done = bf16[1,128,512]{2,1,0:T(8,128)(2,1)S(1)} collective-permute-done((bf16[1,128,512]{2,1,0:T(8,128)(2,1)S(1)}, bf16[1,128,512]{2,1,0:T(8,128)(2,1)S(1)}, u32[]{:S(2)}, u32[]{:S(2)}) %collective-permute-start) | collective-permute-done | bytes 131104 | tf_op jit(solution)/shard_map/ppermute | solution.py:397
  11.0 2.3 %collective-permute-start.1 = (bf16[2,128,512]{2,1,0:T(8,128)(2,1)S(1)}, bf16[2,128,512]{2,1,0:T(8,128)(2,1)S(1)}, u32[]{:S(2)}, u32[]{:S(2)}) collective-permute-start(bf16[2,128,512]{2,1,0:T(8,128)(2,1)S(1)} %get-tuple-element.27), channel_id=1, source_target_pairs={{0,64},{8,72},{16,80},{24,88},{32,96},{40,104},{48,112},{56,120},{... | collective-permute-start | bytes 786440 | tf_op jit(solution)/shard_map/ppermute | solution.py:397
  13.3 2.8 %collective-permute-start.10 = (bf16[3,128,512]{2,1,0:T(8,128)(2,1)S(1)}, bf16[3,128,512]{2,1,0:T(8,128)(2,1)S(1)}, u32[]{:S(2)}, u32[]{:S(2)}) collective-permute-start(bf16[3,128,512]{2,1,0:T(8,128)(2,1)S(1)} %pad_maximum_fusion.refs_1_), channel_id=1, source_target_pairs={{0,24},{8,0},{16,8},{24,16},{32,56},{40,32},{48,40},{56,48},{64,88... | collective-permute-start | bytes 1179656 | tf_op jit(solution)/shard_map/ppermute | solution.py:397
  17.8 2.0 %collective-permute-start.3 = (bf16[2,128,512]{2,1,0:T(8,128)(2,1)S(1)}, bf16[2,128,512]{2,1,0:T(8,128)(2,1)S(1)}, u32[]{:S(2)}, u32[]{:S(2)}) collective-permute-start(bf16[2,128,512]{2,1,0:T(8,128)(2,1)S(1)} %get-tuple-element.26), channel_id=1, source_target_pairs={{0,192},{8,200},{16,208},{24,216},{32,224},{40,232},{48,240},{56,2... | collective-permute-start | bytes 786440 | tf_op jit(solution)/shard_map/ppermute | solution.py:397
  19.8 4.6 %collective-permute-done.1.refs_0_ = bf16[2,128,512]{2,1,0:T(8,128)(2,1)S(1)} collective-permute-done((bf16[2,128,512]{2,1,0:T(8,128)(2,1)S(1)}, bf16[2,128,512]{2,1,0:T(8,128)(2,1)S(1)}, u32[]{:S(2)}, u32[]{:S(2)}) %collective-permute-start.1) | collective-permute-done | bytes 262176 | tf_op jit(solution)/shard_map/ppermute | solution.py:397
  24.4 2.3 %collective-permute-start.4 = (bf16[1,128,512]{2,1,0:T(8,128)(2,1)S(1)}, bf16[1,128,512]{2,1,0:T(8,128)(2,1)S(1)}, u32[]{:S(2)}, u32[]{:S(2)}) collective-permute-start(bf16[1,128,512]{2,1,0:T(8,128)(2,1)S(1)} %slice.14), channel_id=1, source_target_pairs={{0,32},{8,40},{16,48},{24,56},{32,64},{40,72},{48,80},{56,88},{64,... | collective-permute-start | bytes 393224 | tf_op jit(solution)/shard_map/ppermute | solution.py:397
  26.7 6.1 %decode_partials.1 = (bf16[32,80,128]{2,1,0:T(8,128)(2,1)}, bf16[32,72,128]{2,1,0:T(8,128)(2,1)}) custom-call(s32[1]{0:T(128)} %bitcast.ctx_ref, s32[32]{0:T(128)} %len_ref, bf16[3,32,3072]{2,1,0:T(8,128)(2,1)} %bitcast.4, bf16[32,128,256]{2,1,0:T(8,128)(2,1)} %k_ref.1, bf16[32,128,256]{2,1,0:T(8,128)(2,1)} %v_ref.1), custom_call_target="tpu_custom_call" | custom-call | flops 301989888 | bytes 6291456 | tf_op jit(solution)/shard_map/decode_partials/pallas_call | solution.py:107
  32.9 2.6 %collective-permute-done.9.refs_2_ = bf16[3,128,512]{2,1,0:T(8,128)(2,1)S(1)} collective-permute-done((bf16[3,128,512]{2,1,0:T(8,128)(2,1)S(1)}, bf16[3,128,512]{2,1,0:T(8,128)(2,1)S(1)}, u32[]{:S(2)}, u32[]{:S(2)}) %collective-permute-start.9) | collective-permute-done | bytes 393248 | tf_op jit(solution)/shard_map/ppermute | solution.py:397
  35.5 5.6 %all-to-all-start = ((bf16[32,80,128]{2,1,0:T(8,128)(2,1)}), bf16[32,80,128]{2,1,0:T(8,128)(2,1)S(1)}, u32[]{:S(2)}, u32[]{:S(2)}) async-start(bf16[32,80,128]{2,1,0:T(8,128)(2,1)} %get-tuple-element.17), calls=%async_computation | async-start | bytes 1310720 | tf_op jit(solution)/shard_map/all_to_all | solution.py:460
  41.1 1.9 %join.1.refs_5_ = bf16[5,128,512]{2,1,0:T(8,128)(2,1)} custom-call(bf16[2,128,512]{2,1,0:T(8,128)(2,1)} %copy-done.1, bf16[2,128,512]{2,1,0:T(8,128)(2,1)} %copy-done.3, bf16[1,128,512]{2,1,0:T(8,128)(2,1)} %copy-done.5), custom_call_target="tpu_custom_call" | custom-call | bytes 1310720 | tf_op jit(solution)/shard_map/join/pallas_call | solution.py:419
  43.0 1.9 %collective-permute-start.5 = (bf16[5,128,512]{2,1,0:T(8,128)(2,1)}, bf16[5,128,512]{2,1,0:T(8,128)(2,1)S(1)}, u32[]{:S(2)}, u32[]{:S(2)}) collective-permute-start(bf16[5,128,512]{2,1,0:T(8,128)(2,1)} %join.1.refs_5_), channel_id=1, source_target_pairs={{0,8},{8,16},{16,24},{24,0},{32,40},{40,48},{48,56},{56,32},{64,72... | collective-permute-start | bytes 1966088 | tf_op jit(solution)/shard_map/ppermute | solution.py:397
  44.9 1.5 %collective-permute-start.7 = (bf16[5,128,512]{2,1,0:T(8,128)(2,1)}, bf16[5,128,512]{2,1,0:T(8,128)(2,1)S(1)}, u32[]{:S(2)}, u32[]{:S(2)}) collective-permute-start(bf16[5,128,512]{2,1,0:T(8,128)(2,1)} %join.1.refs_5_), channel_id=1, source_target_pairs={{0,24},{8,0},{16,8},{24,16},{32,56},{40,32},{48,40},{56,48},{64,88... | collective-permute-start | bytes 1966088 | tf_op jit(solution)/shard_map/ppermute | solution.py:397
  47.8 10.8 %prefill_start.2 = (f32[2,2,128,768]{3,2,1,0:T(8,128)}, f32[2,2,8,768]{3,2,1,0:T(8,128)}) custom-call(s32[32]{0:T(128)} %pair_ref.4, s32[1]{0:T(128)} %bitcast.ctx_ref, bf16[128,3072]{1,0:T(8,128)(2,1)} %refs_0_.5, bf16[3,128,512]{2,1,0:T(8,128)(2,1)} %copy-done.2, bf16[3,128,512]{2,1,0:T(8,128)(2,1)} %copy-done.11, bf16[3,128,512]{2,1,0:T(8,128)(2,1)} %copy-done.9, ...), custom_call_target="tpu_custom_call" | custom-call | flops 4563402752 | bytes 4194304 | tf_op jit(solution)/shard_map/prefill_start/pallas_call | solution.py:369
  58.7 7.9 %collective-permute-done.5.refs_1_ = bf16[5,128,512]{2,1,0:T(8,128)(2,1)S(1)} collective-permute-done((bf16[5,128,512]{2,1,0:T(8,128)(2,1)}, bf16[5,128,512]{2,1,0:T(8,128)(2,1)S(1)}, u32[]{:S(2)}, u32[]{:S(2)}) %collective-permute-start.5) | collective-permute-done | bytes 655392 | tf_op jit(solution)/shard_map/ppermute | solution.py:397
  67.5 2.9 %combine.1 = bf16[32,72,128]{2,1,0:T(8,128)(2,1)} custom-call(s32[1]{0:T(128)} %bitcast.ctx_ref, bf16[32,80,128]{2,1,0:T(8,128)(2,1)} %copy-done, bf16[32,72,128]{2,1,0:T(8,128)(2,1)} %get-tuple-element.18.q_ref, bf16[32,8,256]{2,1,0:T(8,128)(2,1)} %pad.7.dk_ref, bf16[32,8,256]{2,1,0:T(8,128)(2,1)} %pad.8.dv_ref), custom_call_target="tpu_custom_call" | custom-call | flops 4194304 | bytes 1048576 | tf_op jit(solution)/shard_map/combine/pallas_call | solution.py:174
  70.4 7.0 %all-to-all-start.1 = ((bf16[32,72,128]{2,1,0:T(8,128)(2,1)}), bf16[32,72,128]{2,1,0:T(8,128)(2,1)S(1)}, u32[]{:S(2)}, u32[]{:S(2)}) async-start(bf16[32,72,128]{2,1,0:T(8,128)(2,1)} %combine.1), calls=%async_computation.1 | async-start | bytes 1179648 | tf_op jit(solution)/shard_map/all_to_all | solution.py:477
  77.4 1.9 %collective-permute-start.6 = (bf16[3,128,512]{2,1,0:T(8,128)(2,1)S(1)}, bf16[3,128,512]{2,1,0:T(8,128)(2,1)S(1)}, u32[]{:S(2)}, u32[]{:S(2)}) collective-permute-start(bf16[3,128,512]{2,1,0:T(8,128)(2,1)S(1)} %slice.15), channel_id=1, source_target_pairs={{0,8},{8,16},{16,24},{24,0},{32,40},{40,48},{48,56},{56,32},{64,72... | collective-permute-start | bytes 1179656 | tf_op jit(solution)/shard_map/ppermute | solution.py:397
  79.3 1.7 %collective-permute-start.8 = (bf16[2,128,512]{2,1,0:T(8,128)(2,1)S(1)}, bf16[2,128,512]{2,1,0:T(8,128)(2,1)S(1)}, u32[]{:S(2)}, u32[]{:S(2)}) collective-permute-start(bf16[2,128,512]{2,1,0:T(8,128)(2,1)S(1)} %slice.16), channel_id=1, source_target_pairs={{0,24},{8,0},{16,8},{24,16},{32,56},{40,32},{48,40},{56,48},{64,88... | collective-permute-start | bytes 786440 | tf_op jit(solution)/shard_map/ppermute | solution.py:397
  81.0 8.6 %prefill_start.3 = (f32[2,2,128,768]{3,2,1,0:T(8,128)}, f32[2,2,8,768]{3,2,1,0:T(8,128)}) custom-call(s32[32]{0:T(128)} %pair_ref.4, s32[1]{0:T(128)} %bitcast.ctx_ref, bf16[128,3072]{1,0:T(8,128)(2,1)} %refs_0_.5, bf16[5,128,512]{2,1,0:T(8,128)(2,1)} %copy-done.4, bf16[5,128,512]{2,1,0:T(8,128)(2,1)} %copy-done.6, ...), custom_call_target="tpu_custom_call" | custom-call | flops 2684354560 | bytes 4194304 | tf_op jit(solution)/shard_map/prefill_start/pallas_call | solution.py:369
  90.6 3.6 %collective-permute-done.6.refs_1_ = bf16[3,128,512]{2,1,0:T(8,128)(2,1)S(1)} collective-permute-done((bf16[3,128,512]{2,1,0:T(8,128)(2,1)S(1)}, bf16[3,128,512]{2,1,0:T(8,128)(2,1)S(1)}, u32[]{:S(2)}, u32[]{:S(2)}) %collective-permute-start.6) | collective-permute-done | bytes 393248 | tf_op jit(solution)/shard_map/ppermute | solution.py:397
  94.9 7.1 %prefill_end.1 = bf16[128,3072]{1,0:T(8,128)(2,1)} custom-call(s32[32]{0:T(128)} %pair_ref.4, s32[1]{0:T(128)} %bitcast.ctx_ref, bf16[128,3072]{1,0:T(8,128)(2,1)} %refs_0_.5, bf16[3,128,512]{2,1,0:T(8,128)(2,1)} %copy-done.12, bf16[2,128,512]{2,1,0:T(8,128)(2,1)} %copy-done.13, f32[2,2,128,768]{3,2,1,0:T(8,128)} %get-tuple-element.20.refs_3_, ...), custom_call_target="tpu_custom_call" | custom-call | flops 1342177280 | bytes 4194304 | tf_op jit(solution)/shard_map/prefill_end/pallas_call | solution.py:369
  102.2 1.0 %copy.17 = bf16[32,3,3072]{2,0,1:T(8,128)(2,1)} copy(bf16[32,3,3072]{2,1,0:T(4,128)(2,1)S(1)} %reshape.11) | data formatting | bytes 1179648
  (50 shorter events, 7.0 us)
Async XLA Ops:
  1.5 9.4 %collective-permute-start = (bf16[1,128,512]{2,1,0:T(8,128)(2,1)S(1)}, bf16[1,128,512]{2,1,0:T(8,128)(2,1)S(1)}, u32[]{:S(2)}, u32[]{:S(2)}) collective-permute-start(bf16[1,128,512]{2,1,0:T(8,128)(2,1)S(1)} %maximum_bitcast_fusion), channel_id=1, source_target_pairs={{0,32},{8,40},{16,48},{24,56},{32,64},{40,72},{48,80},{56,88},{64,... | collective-permute-start | bytes 393224 | tf_op jit(solution)/shard_map/ppermute | solution.py:397
  3.5 7.4 %collective-permute-start.2 = (bf16[1,128,512]{2,1,0:T(8,128)(2,1)S(1)}, bf16[1,128,512]{2,1,0:T(8,128)(2,1)S(1)}, u32[]{:S(2)}, u32[]{:S(2)}) collective-permute-start(bf16[1,128,512]{2,1,0:T(8,128)(2,1)S(1)} %maximum_bitcast_fusion), channel_id=1, source_target_pairs={{0,224},{8,232},{16,240},{24,248},{32,0},{40,8},{48,16},{56,24},{6... | collective-permute-start | bytes 393224 | tf_op jit(solution)/shard_map/ppermute | solution.py:397
  11.0 13.4 %collective-permute-start.1 = (bf16[2,128,512]{2,1,0:T(8,128)(2,1)S(1)}, bf16[2,128,512]{2,1,0:T(8,128)(2,1)S(1)}, u32[]{:S(2)}, u32[]{:S(2)}) collective-permute-start(bf16[2,128,512]{2,1,0:T(8,128)(2,1)S(1)} %get-tuple-element.27), channel_id=1, source_target_pairs={{0,64},{8,72},{16,80},{24,88},{32,96},{40,104},{48,112},{56,120},{... | collective-permute-start | bytes 786440 | tf_op jit(solution)/shard_map/ppermute | solution.py:397
  13.3 19.5 %copy-start.2 = (bf16[3,128,512]{2,1,0:T(8,128)(2,1)}, bf16[3,128,512]{2,1,0:T(8,128)(2,1)S(1)}, u32[]{:S(2)}) copy-start(bf16[3,128,512]{2,1,0:T(8,128)(2,1)S(1)} %pad_maximum_fusion.refs_1_) | copy-start | bytes 1179652
  13.3 19.6 %collective-permute-start.10 = (bf16[3,128,512]{2,1,0:T(8,128)(2,1)S(1)}, bf16[3,128,512]{2,1,0:T(8,128)(2,1)S(1)}, u32[]{:S(2)}, u32[]{:S(2)}) collective-permute-start(bf16[3,128,512]{2,1,0:T(8,128)(2,1)S(1)} %pad_maximum_fusion.refs_1_), channel_id=1, source_target_pairs={{0,24},{8,0},{16,8},{24,16},{32,56},{40,32},{48,40},{56,48},{64,88... | collective-permute-start | bytes 1179656 | tf_op jit(solution)/shard_map/ppermute | solution.py:397
  16.1 16.8 %collective-permute-start.11 = (bf16[3,128,512]{2,1,0:T(8,128)(2,1)S(1)}, bf16[3,128,512]{2,1,0:T(8,128)(2,1)S(1)}, u32[]{:S(2)}, u32[]{:S(2)}) collective-permute-start(bf16[3,128,512]{2,1,0:T(8,128)(2,1)S(1)} %pad_maximum_fusion.refs_1_), channel_id=1, source_target_pairs={{0,16},{8,24},{16,0},{24,8},{32,48},{40,56},{48,32},{56,40},{64,80... | collective-permute-start | bytes 1179656 | tf_op jit(solution)/shard_map/ppermute | solution.py:397
  16.9 18.6 %collective-permute-start.9 = (bf16[3,128,512]{2,1,0:T(8,128)(2,1)S(1)}, bf16[3,128,512]{2,1,0:T(8,128)(2,1)S(1)}, u32[]{:S(2)}, u32[]{:S(2)}) collective-permute-start(bf16[3,128,512]{2,1,0:T(8,128)(2,1)S(1)} %pad_maximum_fusion.refs_1_), channel_id=1, source_target_pairs={{0,8},{8,16},{16,24},{24,0},{32,40},{40,48},{48,56},{56,32},{64,72... | collective-permute-start | bytes 1179656 | tf_op jit(solution)/shard_map/ppermute | solution.py:397
  17.8 15.0 %collective-permute-start.3 = (bf16[2,128,512]{2,1,0:T(8,128)(2,1)S(1)}, bf16[2,128,512]{2,1,0:T(8,128)(2,1)S(1)}, u32[]{:S(2)}, u32[]{:S(2)}) collective-permute-start(bf16[2,128,512]{2,1,0:T(8,128)(2,1)S(1)} %get-tuple-element.26), channel_id=1, source_target_pairs={{0,192},{8,200},{16,208},{24,216},{32,224},{40,232},{48,240},{56,2... | collective-permute-start | bytes 786440 | tf_op jit(solution)/shard_map/ppermute | solution.py:397
  24.4 8.4 %copy-start.1 = (bf16[2,128,512]{2,1,0:T(8,128)(2,1)}, bf16[2,128,512]{2,1,0:T(8,128)(2,1)S(1)}, u32[]{:S(2)}) copy-start(bf16[2,128,512]{2,1,0:T(8,128)(2,1)S(1)} %collective-permute-done.1.refs_0_) | copy-start | bytes 786436
  24.4 8.5 %collective-permute-start.4 = (bf16[1,128,512]{2,1,0:T(8,128)(2,1)S(1)}, bf16[1,128,512]{2,1,0:T(8,128)(2,1)S(1)}, u32[]{:S(2)}, u32[]{:S(2)}) collective-permute-start(bf16[1,128,512]{2,1,0:T(8,128)(2,1)S(1)} %slice.14), channel_id=1, source_target_pairs={{0,32},{8,40},{16,48},{24,56},{32,64},{40,72},{48,80},{56,88},{64,... | collective-permute-start | bytes 393224 | tf_op jit(solution)/shard_map/ppermute | solution.py:397
  32.8 13.6 %copy-start.7 = (bf16[32,3,256]{2,0,1:T(8,128)(2,1)S(1)}, bf16[32,3,256]{2,0,1:T(8,128)(2,1)}, u32[]{:S(2)}) copy-start(bf16[32,3,256]{2,0,1:T(8,128)(2,1)} %param.17) | copy-start | bytes 147460
  32.8 13.6 %copy-start.8 = (bf16[32,3,256]{2,0,1:T(8,128)(2,1)S(1)}, bf16[32,3,256]{2,0,1:T(8,128)(2,1)}, u32[]{:S(2)}) copy-start(bf16[32,3,256]{2,0,1:T(8,128)(2,1)} %param.18) | copy-start | bytes 147460
  32.8 8.2 %copy-start.3 = (bf16[2,128,512]{2,1,0:T(8,128)(2,1)}, bf16[2,128,512]{2,1,0:T(8,128)(2,1)S(1)}, u32[]{:S(2)}) copy-start(bf16[2,128,512]{2,1,0:T(8,128)(2,1)S(1)} %collective-permute-done.3.refs_1_) | copy-start | bytes 786436
  32.9 14.9 %copy-start.9 = (bf16[3,128,512]{2,1,0:T(8,128)(2,1)}, bf16[3,128,512]{2,1,0:T(8,128)(2,1)S(1)}, u32[]{:S(2)}) copy-start(bf16[3,128,512]{2,1,0:T(8,128)(2,1)S(1)} %collective-permute-done.10.refs_3_) | copy-start | bytes 1179652
  32.9 14.9 %copy-start.10 = (bf16[3,128,512]{2,1,0:T(8,128)(2,1)}, bf16[3,128,512]{2,1,0:T(8,128)(2,1)S(1)}, u32[]{:S(2)}) copy-start(bf16[3,128,512]{2,1,0:T(8,128)(2,1)S(1)} %collective-permute-done.11.refs_4_) | copy-start | bytes 1179652
  35.5 12.3 %copy-start.11 = (bf16[3,128,512]{2,1,0:T(8,128)(2,1)}, bf16[3,128,512]{2,1,0:T(8,128)(2,1)S(1)}, u32[]{:S(2)}) copy-start(bf16[3,128,512]{2,1,0:T(8,128)(2,1)S(1)} %collective-permute-done.9.refs_2_) | copy-start | bytes 1179652
  35.5 31.1 %all-to-all-start = ((bf16[32,80,128]{2,1,0:T(8,128)(2,1)}), bf16[32,80,128]{2,1,0:T(8,128)(2,1)S(1)}, u32[]{:S(2)}, u32[]{:S(2)}) async-start(bf16[32,80,128]{2,1,0:T(8,128)(2,1)} %get-tuple-element.17), calls=%async_computation | async-start | bytes 1310720 | tf_op jit(solution)/shard_map/all_to_all | solution.py:460
  43.0 23.6 %collective-permute-start.5 = (bf16[5,128,512]{2,1,0:T(8,128)(2,1)}, bf16[5,128,512]{2,1,0:T(8,128)(2,1)S(1)}, u32[]{:S(2)}, u32[]{:S(2)}) collective-permute-start(bf16[5,128,512]{2,1,0:T(8,128)(2,1)} %join.1.refs_5_), channel_id=1, source_target_pairs={{0,8},{8,16},{16,24},{24,0},{32,40},{40,48},{48,56},{56,32},{64,72... | collective-permute-start | bytes 1966088 | tf_op jit(solution)/shard_map/ppermute | solution.py:397
  44.9 21.7 %collective-permute-start.7 = (bf16[5,128,512]{2,1,0:T(8,128)(2,1)}, bf16[5,128,512]{2,1,0:T(8,128)(2,1)S(1)}, u32[]{:S(2)}, u32[]{:S(2)}) collective-permute-start(bf16[5,128,512]{2,1,0:T(8,128)(2,1)} %join.1.refs_5_), channel_id=1, source_target_pairs={{0,24},{8,0},{16,8},{24,16},{32,56},{40,32},{48,40},{56,48},{64,88... | collective-permute-start | bytes 1966088 | tf_op jit(solution)/shard_map/ppermute | solution.py:397
  66.6 14.4 %copy-start.4 = (bf16[5,128,512]{2,1,0:T(8,128)(2,1)}, bf16[5,128,512]{2,1,0:T(8,128)(2,1)S(1)}, u32[]{:S(2)}) copy-start(bf16[5,128,512]{2,1,0:T(8,128)(2,1)S(1)} %collective-permute-done.5.refs_1_) | copy-start | bytes 1966084
  66.6 14.4 %copy-start.6 = (bf16[5,128,512]{2,1,0:T(8,128)(2,1)}, bf16[5,128,512]{2,1,0:T(8,128)(2,1)S(1)}, u32[]{:S(2)}) copy-start(bf16[5,128,512]{2,1,0:T(8,128)(2,1)S(1)} %collective-permute-done.7.refs_2_) | copy-start | bytes 1966084
  70.4 31.6 %all-to-all-start.1 = ((bf16[32,72,128]{2,1,0:T(8,128)(2,1)}), bf16[32,72,128]{2,1,0:T(8,128)(2,1)S(1)}, u32[]{:S(2)}, u32[]{:S(2)}) async-start(bf16[32,72,128]{2,1,0:T(8,128)(2,1)} %combine.1), calls=%async_computation.1 | async-start | bytes 1179648 | tf_op jit(solution)/shard_map/all_to_all | solution.py:477
  77.4 16.8 %collective-permute-start.6 = (bf16[3,128,512]{2,1,0:T(8,128)(2,1)S(1)}, bf16[3,128,512]{2,1,0:T(8,128)(2,1)S(1)}, u32[]{:S(2)}, u32[]{:S(2)}) collective-permute-start(bf16[3,128,512]{2,1,0:T(8,128)(2,1)S(1)} %slice.15), channel_id=1, source_target_pairs={{0,8},{8,16},{16,24},{24,0},{32,40},{40,48},{48,56},{56,32},{64,72... | collective-permute-start | bytes 1179656 | tf_op jit(solution)/shard_map/ppermute | solution.py:397
  79.3 11.3 %collective-permute-start.8 = (bf16[2,128,512]{2,1,0:T(8,128)(2,1)S(1)}, bf16[2,128,512]{2,1,0:T(8,128)(2,1)S(1)}, u32[]{:S(2)}, u32[]{:S(2)}) collective-permute-start(bf16[2,128,512]{2,1,0:T(8,128)(2,1)S(1)} %slice.16), channel_id=1, source_target_pairs={{0,24},{8,0},{16,8},{24,16},{32,56},{40,32},{48,40},{56,48},{64,88... | collective-permute-start | bytes 786440 | tf_op jit(solution)/shard_map/ppermute | solution.py:397
  (4 other events, 13.4 us)

commit v4 on v3

--- a/solution.py
+++ b/solution.py
@@ -62,9 +62,10 @@
     return out
 
 
-def decode_kernel(ctx_ref, len_ref, q_ref, k_ref, v_ref, out_ref, q72_ref):
+def decode_kernel(base, carried, ctx_ref, len_ref, q_ref, k_ref, v_ref, *refs):
+    out_ref, q72_ref = refs[carried:]
     first = ctx_ref[0] * D
-    step = pl.program_id(0)
+    step = base + pl.program_id(0)
     shape = (ROWS, 2 * D)
     lane = lane_iota(shape)
     kv_of_row = (lax.rem(row_iota(shape), H_LOC) >= GROUP).astype(jnp.int32)
@@ -103,32 +104,38 @@
         mix(i, *w)
 
 
-def decode_partials(ctx, cache_len, queries, cache_k, cache_v):
+def decode_partials(ctx, cache_len, queries, cache_k, cache_v, before):
+    steps = REQ // RB // 2
+    base = 0 if before is None else steps
+    before = () if before is None else before
+    kernel = functools.partial(decode_kernel, base, len(before))
     return pl.pallas_call(
-        decode_kernel,
+        kernel,
         out_shape=(
             jax.ShapeDtypeStruct((REQ, PAY, D), jnp.bfloat16),
             jax.ShapeDtypeStruct((REQ, ROWS, D), jnp.bfloat16),
         ),
         grid_spec=pltpu.PrefetchScalarGridSpec(
             num_scalar_prefetch=2,
-            grid=(REQ // RB,),
+            grid=(steps,),
             in_specs=[
-                pl.BlockSpec((STEPS, RB, H_LOC * D), lambda i, c, n: (0, i, 0)),
-                pl.BlockSpec((RB, D, 2 * D), lambda i, c, n: (i, 0, 0)),
-                pl.BlockSpec((RB, D, 2 * D), lambda i, c, n: (i, 0, 0)),
-            ],
+                pl.BlockSpec((STEPS, RB, H_LOC * D), lambda i, c, n: (0, base + i, 0)),
+                pl.BlockSpec((RB, D, 2 * D), lambda i, c, n: (base + i, 0, 0)),
+                pl.BlockSpec((RB, D, 2 * D), lambda i, c, n: (base + i, 0, 0)),
+            ]
+            + [pl.BlockSpec(memory_space=pl.ANY)] * len(before),
             out_specs=(
-                pl.BlockSpec((RB, PAY, D), lambda i, c, n: (i, 0, 0)),
-                pl.BlockSpec((RB, ROWS, D), lambda i, c, n: (i, 0, 0)),
+                pl.BlockSpec((RB, PAY, D), lambda i, c, n: (base + i, 0, 0)),
+                pl.BlockSpec((RB, ROWS, D), lambda i, c, n: (base + i, 0, 0)),
             ),
         ),
+        input_output_aliases={5 + i: i for i in range(len(before))},
         compiler_params=pltpu.CompilerParams(vmem_limit_bytes=VMEM_LIMIT),
         cost_estimate=pl.CostEstimate(
-            flops=REQ * ROWS * 256 * D * 4, bytes_accessed=6 * 2**20, transcendentals=REQ * ROWS * 256
+            flops=REQ * ROWS * 256 * D * 2, bytes_accessed=3 * 2**20, transcendentals=REQ * ROWS * 128
         ),
         name="decode_partials",
-    )(ctx, cache_len, queries, cache_k, cache_v)
+    )(ctx, cache_len, queries, cache_k, cache_v, *before)
 
 
 def combine_kernel(ctx_ref, recv_ref, q_ref, dk_ref, dv_ref, out_ref):
@@ -185,7 +192,7 @@
             ],
             out_specs=pl.BlockSpec((N, ROWS, D), lambda i, c: (0, 0, 0)),
         ),
-        compiler_params=pltpu.CompilerParams(vmem_limit_bytes=VMEM_LIMIT),
+        compiler_params=pltpu.CompilerParams(vmem_limit_bytes=8 * 1024 * 1024),
         cost_estimate=pl.CostEstimate(flops=4 * 2**20, bytes_accessed=2**20, transcendentals=2**14),
         name="combine",
     )(ctx, recv, q72, dk8, dv8)
@@ -449,14 +456,15 @@
 
     own = jnp.concatenate([prefill_keys, prefill_values], axis=1)[None]
     up1, down1 = shift(own, 1, 0), shift(own, -1, 0)
-    near, near_z = cat(own, up1, down1), [0, 1, -1]
+    turned = jnp.transpose(decode_queries, (1, 0, 2))
+    half = decode_partials(ctx, cache_len, turned, cache_keys, cache_values, None)
+    near, near_z = cat(own, after(up1, *half), down1), [0, 1, -1]
     right1, left1, across1 = shift(near, 0, 1), shift(near, 0, -1), shift(near, 0, 2)
     up2, down2 = shift(near[:2], 2, 0), shift(cat(own, down1), -2, 0)
 
-    turned = jnp.transpose(decode_queries, (1, 0, 2))
-    partials, q72 = decode_partials(ctx, after(cache_len, up1, down1), turned, cache_keys, cache_values)
-
-    up4 = shift(up2[1:], 1, 0)
+    partials, q72 = decode_partials(ctx, after(cache_len, up1, down1), turned, cache_keys, cache_values, half)
+
+    up4 = shift(after(up2[1:], partials), 1, 0)
     recv = lax.all_to_all(after(partials, right1, left1, up2, down2, up4, across1), "ctx", 0, 0, tiled=True)
     far, far_z = join((up2, 0, 2), (down2, 0, 2), (up4, 0, 1)), [2, 3, -2, -3, 4]
     right2, left2 = shift(far, 0, 1), shift(far, 0, -1)

time: 104 us -> 102 us (0.981)
  local copies, waits for them, and re-layouts: 4.4 us -> 2.24 us
  starting transfers between devices: 36.6 us -> 35 us
  waiting for transfers between devices: 23.1 us -> 24.4 us
    ppermute x12, starting transfers between devices: 24 us -> 21.8 us  [shift(): return lax.ppermute(x, 'ctx', [(i, to(i)) for i in range(N)])]
    pallas_call x1 -> x2, Pallas kernels: 6.09 us -> 7.99 us  [decode_partials(): pl.pallas_call(kernel, out_shape=(jax.ShapeDtypeStruct((REQ, PAY, D), jnp...]
    ppermute x12, waiting for transfers between devices: 23.1 us -> 24.4 us  [shift(): return lax.ppermute(x, 'ctx', [(i, to(i)) for i in range(N)])]
    pad x2, local copies, waits for them, and re-layouts: 1.35 us -> 0.05 us  [local(): dk8, dv8 = (jnp.pad(draft_keys, pad), jnp.pad(draft_values, pad))]
    pallas_call x1, Pallas kernels: 2.86 us -> 1.76 us  [combine(): pl.pallas_call(combine_kernel, out_shape=jax.ShapeDtypeStruct((N, ROWS, D...]
  transfers between devices with their start and end apart: 14 -> 14, of which waited for: 6 -> 7; matrix products, arithmetic and copies ran while one was open for 1% -> 0% of each run, Pallas kernels for 33% -> 36%
where the time goes in v4:
time: 102 us
  Pallas kernels  38.3 us (38%)
  starting transfers between devices  35 us (34%)
  waiting for transfers between devices  24.4 us (24%)
  local copies, waits for them, and re-layouts  2.24 us (2%)
    pallas_call x3, Pallas kernels, prefill(): pl.pallas_call(functools.partial(prefill_kernel, blocks=blocks, first=fir...  26.6 us
    ppermute x12, waiting for transfers between devices, shift(): return lax.ppermute(x, 'ctx', [(i, to(i)) for i in range(N)])  24.4 us
    ppermute x12, starting transfers between devices, shift(): return lax.ppermute(x, 'ctx', [(i, to(i)) for i in range(N)])  21.8 us
    pallas_call x2, Pallas kernels, decode_partials(): pl.pallas_call(kernel, out_shape=(jax.ShapeDtypeStruct((REQ, PAY, D), jnp...  7.99 us
    all_to_all x1, starting transfers between devices, local(): spread = lax.all_to_all(done, 'ctx', 0, 0, tiled=True)  6.87 us
    all_to_all x1, starting transfers between devices, local(): lax.all_to_all(after(partials, right1, left1, up2, down2, up4, across1),...  6.34 us
  transfers between devices with their start and end apart: 14, of which 7 were waited for; matrix products, arithmetic and copies ran while one was open for 0% of the time, Pallas kernels for 36%

profile of v4, /device:TPU:16, one launch (start us, length us, event | category | flops | bytes accessed | tf_op | source)
XLA Modules:
  0.0 101.8 jit_solution(6381969287395529282)
XLA Ops:
  1.5 2.0 %collective-permute-start = (bf16[1,128,512]{2,1,0:T(8,128)(2,1)S(1)}, bf16[1,128,512]{2,1,0:T(8,128)(2,1)S(1)}, u32[]{:S(2)}, u32[]{:S(2)}) collective-permute-start(bf16[1,128,512]{2,1,0:T(8,128)(2,1)S(1)} %maximum_bitcast_fusion), channel_id=1, source_target_pairs={{0,32},{8,40},{16,48},{24,56},{32,64},{40,72},{48,80},{56,88},{64,... | collective-permute-start | bytes 393224 | tf_op jit(solution)/shard_map/ppermute | solution.py:404
  3.5 4.0 %collective-permute-start.2 = (bf16[1,128,512]{2,1,0:T(8,128)(2,1)S(1)}, bf16[1,128,512]{2,1,0:T(8,128)(2,1)S(1)}, u32[]{:S(2)}, u32[]{:S(2)}) collective-permute-start(bf16[1,128,512]{2,1,0:T(8,128)(2,1)S(1)} %maximum_bitcast_fusion), channel_id=1, source_target_pairs={{0,224},{8,232},{16,240},{24,248},{32,0},{40,8},{48,16},{56,24},{6... | collective-permute-start | bytes 393224 | tf_op jit(solution)/shard_map/ppermute | solution.py:404
  7.5 4.0 %decode_partials.2 = (bf16[32,80,128]{2,1,0:T(8,128)(2,1)}, bf16[32,72,128]{2,1,0:T(8,128)(2,1)}) custom-call(s32[1]{0:T(128)} %bitcast.ctx_ref, s32[32]{0:T(128)} %len_ref.2, bf16[3,32,3072]{2,1,0:T(8,128)(2,1)} %bitcast.4, bf16[32,128,256]{2,1,0:T(8,128)(2,1)} %k_ref.3, bf16[32,128,256]{2,1,0:T(8,128)(2,1)} %v_ref.3), custom_call_target="tpu_custom_call" | custom-call | flops 150994944 | bytes 3145728 | tf_op jit(solution)/shard_map/decode_partials/pallas_call | solution.py:112
  11.6 1.7 %collective-permute-start.1 = (bf16[2,128,512]{2,1,0:T(8,128)(2,1)S(1)}, bf16[2,128,512]{2,1,0:T(8,128)(2,1)S(1)}, u32[]{:S(2)}, u32[]{:S(2)}) collective-permute-start(bf16[2,128,512]{2,1,0:T(8,128)(2,1)S(1)} %get-tuple-element.35), channel_id=1, source_target_pairs={{0,64},{8,72},{16,80},{24,88},{32,96},{40,104},{48,112},{56,120},{... | collective-permute-start | bytes 786440 | tf_op jit(solution)/shard_map/ppermute | solution.py:404
  13.3 2.8 %collective-permute-start.10 = (bf16[3,128,512]{2,1,0:T(8,128)(2,1)S(1)}, bf16[3,128,512]{2,1,0:T(8,128)(2,1)S(1)}, u32[]{:S(2)}, u32[]{:S(2)}) collective-permute-start(bf16[3,128,512]{2,1,0:T(8,128)(2,1)S(1)} %pad_maximum_fusion.refs_1_), channel_id=1, source_target_pairs={{0,24},{8,0},{16,8},{24,16},{32,56},{40,32},{48,40},{56,48},{64,88... | collective-permute-start | bytes 1179656 | tf_op jit(solution)/shard_map/ppermute | solution.py:404
  17.8 2.6 %collective-permute-start.3 = (bf16[2,128,512]{2,1,0:T(8,128)(2,1)S(1)}, bf16[2,128,512]{2,1,0:T(8,128)(2,1)S(1)}, u32[]{:S(2)}, u32[]{:S(2)}) collective-permute-start(bf16[2,128,512]{2,1,0:T(8,128)(2,1)S(1)} %get-tuple-element.34), channel_id=1, source_target_pairs={{0,192},{8,200},{16,208},{24,216},{32,224},{40,232},{48,240},{56,2... | collective-permute-start | bytes 786440 | tf_op jit(solution)/shard_map/ppermute | solution.py:404
  20.4 4.0 %decode_partials.3 = (bf16[32,80,128]{2,1,0:T(8,128)(2,1)}, bf16[32,72,128]{2,1,0:T(8,128)(2,1)}) custom-call(s32[1]{0:T(128)} %bitcast.ctx_ref, s32[32]{0:T(128)} %len_ref.2, bf16[3,32,3072]{2,1,0:T(8,128)(2,1)} %bitcast.5, bf16[32,128,256]{2,1,0:T(8,128)(2,1)} %k_ref.3, bf16[32,128,256]{2,1,0:T(8,128)(2,1)} %v_ref.3, ...), custom_call_target="tpu_custom_call", output_to_operand_aliasing={{0}: (5, {}), {1}: (6, {})} | custom-call | flops 150994944 | bytes 3145728 | tf_op jit(solution)/shard_map/decode_partials/pallas_call | solution.py:112
  24.4 2.8 %collective-permute-done.1.refs_0_ = bf16[2,128,512]{2,1,0:T(8,128)(2,1)S(1)} collective-permute-done((bf16[2,128,512]{2,1,0:T(8,128)(2,1)S(1)}, bf16[2,128,512]{2,1,0:T(8,128)(2,1)S(1)}, u32[]{:S(2)}, u32[]{:S(2)}) %collective-permute-start.1) | collective-permute-done | bytes 262176 | tf_op jit(solution)/shard_map/ppermute | solution.py:404
  27.3 4.3 %collective-permute-done.3.refs_1_ = bf16[2,128,512]{2,1,0:T(8,128)(2,1)S(1)} collective-permute-done((bf16[2,128,512]{2,1,0:T(8,128)(2,1)S(1)}, bf16[2,128,512]{2,1,0:T(8,128)(2,1)S(1)}, u32[]{:S(2)}, u32[]{:S(2)}) %collective-permute-start.3) | collective-permute-done | bytes 262176 | tf_op jit(solution)/shard_map/ppermute | solution.py:404
  31.5 1.9 %collective-permute-done.4.refs_2_ = bf16[1,128,512]{2,1,0:T(8,128)(2,1)S(1)} collective-permute-done((bf16[1,128,512]{2,1,0:T(8,128)(2,1)S(1)}, bf16[1,128,512]{2,1,0:T(8,128)(2,1)S(1)}, u32[]{:S(2)}, u32[]{:S(2)}) %collective-permute-start.4) | collective-permute-done | bytes 131104 | tf_op jit(solution)/shard_map/ppermute | solution.py:404
  33.5 2.0 %collective-permute-done.9.refs_2_ = bf16[3,128,512]{2,1,0:T(8,128)(2,1)S(1)} collective-permute-done((bf16[3,128,512]{2,1,0:T(8,128)(2,1)S(1)}, bf16[3,128,512]{2,1,0:T(8,128)(2,1)S(1)}, u32[]{:S(2)}, u32[]{:S(2)}) %collective-permute-start.9) | collective-permute-done | bytes 393248 | tf_op jit(solution)/shard_map/ppermute | solution.py:404
  35.5 6.3 %all-to-all-start = ((bf16[32,80,128]{2,1,0:T(8,128)(2,1)}), bf16[32,80,128]{2,1,0:T(8,128)(2,1)S(1)}, u32[]{:S(2)}, u32[]{:S(2)}) async-start(bf16[32,80,128]{2,1,0:T(8,128)(2,1)} %get-tuple-element.25), calls=%async_computation | async-start | bytes 1310720 | tf_op jit(solution)/shard_map/all_to_all | solution.py:468
  41.9 1.9 %join.1.refs_5_ = bf16[5,128,512]{2,1,0:T(8,128)(2,1)} custom-call(bf16[2,128,512]{2,1,0:T(8,128)(2,1)} %copy-done.1, bf16[2,128,512]{2,1,0:T(8,128)(2,1)} %copy-done.3, bf16[1,128,512]{2,1,0:T(8,128)(2,1)} %copy-done.5), custom_call_target="tpu_custom_call" | custom-call | bytes 1310720 | tf_op jit(solution)/shard_map/join/pallas_call | solution.py:426
  43.8 1.9 %collective-permute-start.5 = (bf16[5,128,512]{2,1,0:T(8,128)(2,1)}, bf16[5,128,512]{2,1,0:T(8,128)(2,1)S(1)}, u32[]{:S(2)}, u32[]{:S(2)}) collective-permute-start(bf16[5,128,512]{2,1,0:T(8,128)(2,1)} %join.1.refs_5_), channel_id=1, source_target_pairs={{0,8},{8,16},{16,24},{24,0},{32,40},{40,48},{48,56},{56,32},{64,72... | collective-permute-start | bytes 1966088 | tf_op jit(solution)/shard_map/ppermute | solution.py:404
  45.7 1.5 %collective-permute-start.7 = (bf16[5,128,512]{2,1,0:T(8,128)(2,1)}, bf16[5,128,512]{2,1,0:T(8,128)(2,1)S(1)}, u32[]{:S(2)}, u32[]{:S(2)}) collective-permute-start(bf16[5,128,512]{2,1,0:T(8,128)(2,1)} %join.1.refs_5_), channel_id=1, source_target_pairs={{0,24},{8,0},{16,8},{24,16},{32,56},{40,32},{48,40},{56,48},{64,88... | collective-permute-start | bytes 1966088 | tf_op jit(solution)/shard_map/ppermute | solution.py:404
  47.4 11.0 %prefill_start.2 = (f32[2,2,128,768]{3,2,1,0:T(8,128)}, f32[2,2,8,768]{3,2,1,0:T(8,128)}) custom-call(s32[32]{0:T(128)} %pair_ref.4, s32[1]{0:T(128)} %bitcast.ctx_ref, bf16[128,3072]{1,0:T(8,128)(2,1)} %refs_0_.5, bf16[3,128,512]{2,1,0:T(8,128)(2,1)} %copy-done.2, bf16[3,128,512]{2,1,0:T(8,128)(2,1)} %copy-done.11, bf16[3,128,512]{2,1,0:T(8,128)(2,1)} %copy-done.9, ...), custom_call_target="tpu_custom_call" | custom-call | flops 4563402752 | bytes 4194304 | tf_op jit(solution)/shard_map/prefill_start/pallas_call | solution.py:376
  58.4 9.0 %collective-permute-done.5.refs_1_ = bf16[5,128,512]{2,1,0:T(8,128)(2,1)S(1)} collective-permute-done((bf16[5,128,512]{2,1,0:T(8,128)(2,1)}, bf16[5,128,512]{2,1,0:T(8,128)(2,1)S(1)}, u32[]{:S(2)}, u32[]{:S(2)}) %collective-permute-start.5) | collective-permute-done | bytes 655392 | tf_op jit(solution)/shard_map/ppermute | solution.py:404
  67.4 1.8 %combine.1 = bf16[32,72,128]{2,1,0:T(8,128)(2,1)} custom-call(s32[1]{0:T(128)} %bitcast.ctx_ref, bf16[32,80,128]{2,1,0:T(8,128)(2,1)S(1)} %all-to-all-done.recv_ref, bf16[32,72,128]{2,1,0:T(8,128)(2,1)S(1)} %copy-done, bf16[32,8,256]{2,1,0:T(8,128)(2,1)S(1)} %pad.7.dk_ref, bf16[32,8,256]{2,1,0:T(8,128)(2,1)S(1)} %pad.8.dv_ref), custom_call_target="tpu_custom_call" | custom-call | flops 4194304 | bytes 1048576 | tf_op jit(solution)/shard_map/combine/pallas_call | solution.py:181
  69.2 6.9 %all-to-all-start.1 = ((bf16[32,72,128]{2,1,0:T(8,128)(2,1)}), bf16[32,72,128]{2,1,0:T(8,128)(2,1)S(1)}, u32[]{:S(2)}, u32[]{:S(2)}) async-start(bf16[32,72,128]{2,1,0:T(8,128)(2,1)} %combine.1), calls=%async_computation.1 | async-start | bytes 1179648 | tf_op jit(solution)/shard_map/all_to_all | solution.py:485
  76.1 1.9 %collective-permute-start.6 = (bf16[3,128,512]{2,1,0:T(8,128)(2,1)S(1)}, bf16[3,128,512]{2,1,0:T(8,128)(2,1)S(1)}, u32[]{:S(2)}, u32[]{:S(2)}) collective-permute-start(bf16[3,128,512]{2,1,0:T(8,128)(2,1)S(1)} %slice.15), channel_id=1, source_target_pairs={{0,8},{8,16},{16,24},{24,0},{32,40},{40,48},{48,56},{56,32},{64,72... | collective-permute-start | bytes 1179656 | tf_op jit(solution)/shard_map/ppermute | solution.py:404
  78.0 1.7 %collective-permute-start.8 = (bf16[2,128,512]{2,1,0:T(8,128)(2,1)S(1)}, bf16[2,128,512]{2,1,0:T(8,128)(2,1)S(1)}, u32[]{:S(2)}, u32[]{:S(2)}) collective-permute-start(bf16[2,128,512]{2,1,0:T(8,128)(2,1)S(1)} %slice.16), channel_id=1, source_target_pairs={{0,24},{8,0},{16,8},{24,16},{32,56},{40,32},{48,40},{56,48},{64,88... | collective-permute-start | bytes 786440 | tf_op jit(solution)/shard_map/ppermute | solution.py:404
  79.8 8.6 %prefill_start.3 = (f32[2,2,128,768]{3,2,1,0:T(8,128)}, f32[2,2,8,768]{3,2,1,0:T(8,128)}) custom-call(s32[32]{0:T(128)} %pair_ref.4, s32[1]{0:T(128)} %bitcast.ctx_ref, bf16[128,3072]{1,0:T(8,128)(2,1)} %refs_0_.5, bf16[5,128,512]{2,1,0:T(8,128)(2,1)} %copy-done.4, bf16[5,128,512]{2,1,0:T(8,128)(2,1)} %copy-done.6, ...), custom_call_target="tpu_custom_call" | custom-call | flops 2684354560 | bytes 4194304 | tf_op jit(solution)/shard_map/prefill_start/pallas_call | solution.py:376
  89.2 3.5 %collective-permute-done.6.refs_1_ = bf16[3,128,512]{2,1,0:T(8,128)(2,1)S(1)} collective-permute-done((bf16[3,128,512]{2,1,0:T(8,128)(2,1)S(1)}, bf16[3,128,512]{2,1,0:T(8,128)(2,1)S(1)}, u32[]{:S(2)}, u32[]{:S(2)}) %collective-permute-start.6) | collective-permute-done | bytes 393248 | tf_op jit(solution)/shard_map/ppermute | solution.py:404
  93.5 7.1 %prefill_end.1 = bf16[128,3072]{1,0:T(8,128)(2,1)} custom-call(s32[32]{0:T(128)} %pair_ref.4, s32[1]{0:T(128)} %bitcast.ctx_ref, bf16[128,3072]{1,0:T(8,128)(2,1)} %refs_0_.5, bf16[3,128,512]{2,1,0:T(8,128)(2,1)} %copy-done.12, bf16[2,128,512]{2,1,0:T(8,128)(2,1)} %copy-done.13, f32[2,2,128,768]{3,2,1,0:T(8,128)} %get-tuple-element.28.refs_3_, ...), custom_call_target="tpu_custom_call" | custom-call | flops 1342177280 | bytes 4194304 | tf_op jit(solution)/shard_map/prefill_end/pallas_call | solution.py:376
  (51 shorter events, 5.9 us)
Async XLA Ops:
  1.5 10.0 %collective-permute-start = (bf16[1,128,512]{2,1,0:T(8,128)(2,1)S(1)}, bf16[1,128,512]{2,1,0:T(8,128)(2,1)S(1)}, u32[]{:S(2)}, u32[]{:S(2)}) collective-permute-start(bf16[1,128,512]{2,1,0:T(8,128)(2,1)S(1)} %maximum_bitcast_fusion), channel_id=1, source_target_pairs={{0,32},{8,40},{16,48},{24,56},{32,64},{40,72},{48,80},{56,88},{64,... | collective-permute-start | bytes 393224 | tf_op jit(solution)/shard_map/ppermute | solution.py:404
  3.5 8.0 %collective-permute-start.2 = (bf16[1,128,512]{2,1,0:T(8,128)(2,1)S(1)}, bf16[1,128,512]{2,1,0:T(8,128)(2,1)S(1)}, u32[]{:S(2)}, u32[]{:S(2)}) collective-permute-start(bf16[1,128,512]{2,1,0:T(8,128)(2,1)S(1)} %maximum_bitcast_fusion), channel_id=1, source_target_pairs={{0,224},{8,232},{16,240},{24,248},{32,0},{40,8},{48,16},{56,24},{6... | collective-permute-start | bytes 393224 | tf_op jit(solution)/shard_map/ppermute | solution.py:404
  11.6 15.6 %collective-permute-start.1 = (bf16[2,128,512]{2,1,0:T(8,128)(2,1)S(1)}, bf16[2,128,512]{2,1,0:T(8,128)(2,1)S(1)}, u32[]{:S(2)}, u32[]{:S(2)}) collective-permute-start(bf16[2,128,512]{2,1,0:T(8,128)(2,1)S(1)} %get-tuple-element.35), channel_id=1, source_target_pairs={{0,64},{8,72},{16,80},{24,88},{32,96},{40,104},{48,112},{56,120},{... | collective-permute-start | bytes 786440 | tf_op jit(solution)/shard_map/ppermute | solution.py:404
  13.3 11.1 %copy-start.2 = (bf16[3,128,512]{2,1,0:T(8,128)(2,1)}, bf16[3,128,512]{2,1,0:T(8,128)(2,1)S(1)}, u32[]{:S(2)}) copy-start(bf16[3,128,512]{2,1,0:T(8,128)(2,1)S(1)} %pad_maximum_fusion.refs_1_) | copy-start | bytes 1179652
  13.3 20.1 %collective-permute-start.10 = (bf16[3,128,512]{2,1,0:T(8,128)(2,1)S(1)}, bf16[3,128,512]{2,1,0:T(8,128)(2,1)S(1)}, u32[]{:S(2)}, u32[]{:S(2)}) collective-permute-start(bf16[3,128,512]{2,1,0:T(8,128)(2,1)S(1)} %pad_maximum_fusion.refs_1_), channel_id=1, source_target_pairs={{0,24},{8,0},{16,8},{24,16},{32,56},{40,32},{48,40},{56,48},{64,88... | collective-permute-start | bytes 1179656 | tf_op jit(solution)/shard_map/ppermute | solution.py:404
  16.1 17.3 %collective-permute-start.11 = (bf16[3,128,512]{2,1,0:T(8,128)(2,1)S(1)}, bf16[3,128,512]{2,1,0:T(8,128)(2,1)S(1)}, u32[]{:S(2)}, u32[]{:S(2)}) collective-permute-start(bf16[3,128,512]{2,1,0:T(8,128)(2,1)S(1)} %pad_maximum_fusion.refs_1_), channel_id=1, source_target_pairs={{0,16},{8,24},{16,0},{24,8},{32,48},{40,56},{48,32},{56,40},{64,80... | collective-permute-start | bytes 1179656 | tf_op jit(solution)/shard_map/ppermute | solution.py:404
  16.9 18.6 %collective-permute-start.9 = (bf16[3,128,512]{2,1,0:T(8,128)(2,1)S(1)}, bf16[3,128,512]{2,1,0:T(8,128)(2,1)S(1)}, u32[]{:S(2)}, u32[]{:S(2)}) collective-permute-start(bf16[3,128,512]{2,1,0:T(8,128)(2,1)S(1)} %pad_maximum_fusion.refs_1_), channel_id=1, source_target_pairs={{0,8},{8,16},{16,24},{24,0},{32,40},{40,48},{48,56},{56,32},{64,72... | collective-permute-start | bytes 1179656 | tf_op jit(solution)/shard_map/ppermute | solution.py:404
  17.8 13.7 %collective-permute-start.3 = (bf16[2,128,512]{2,1,0:T(8,128)(2,1)S(1)}, bf16[2,128,512]{2,1,0:T(8,128)(2,1)S(1)}, u32[]{:S(2)}, u32[]{:S(2)}) collective-permute-start(bf16[2,128,512]{2,1,0:T(8,128)(2,1)S(1)} %get-tuple-element.34), channel_id=1, source_target_pairs={{0,192},{8,200},{16,208},{24,216},{32,224},{40,232},{48,240},{56,2... | collective-permute-start | bytes 786440 | tf_op jit(solution)/shard_map/ppermute | solution.py:404
  24.4 22.8 %copy-start.7 = (bf16[32,3,256]{2,0,1:T(8,128)(2,1)S(1)}, bf16[32,3,256]{2,0,1:T(8,128)(2,1)}, u32[]{:S(2)}) copy-start(bf16[32,3,256]{2,0,1:T(8,128)(2,1)} %param.17) | copy-start | bytes 147460
  24.4 22.8 %copy-start.8 = (bf16[32,3,256]{2,0,1:T(8,128)(2,1)S(1)}, bf16[32,3,256]{2,0,1:T(8,128)(2,1)}, u32[]{:S(2)}) copy-start(bf16[32,3,256]{2,0,1:T(8,128)(2,1)} %param.18) | copy-start | bytes 147460
  27.2 14.7 %copy-start.1 = (bf16[2,128,512]{2,1,0:T(8,128)(2,1)}, bf16[2,128,512]{2,1,0:T(8,128)(2,1)S(1)}, u32[]{:S(2)}) copy-start(bf16[2,128,512]{2,1,0:T(8,128)(2,1)S(1)} %collective-permute-done.1.refs_0_) | copy-start | bytes 786436
  27.2 6.3 %collective-permute-start.4 = (bf16[1,128,512]{2,1,0:T(8,128)(2,1)S(1)}, bf16[1,128,512]{2,1,0:T(8,128)(2,1)S(1)}, u32[]{:S(2)}, u32[]{:S(2)}) collective-permute-start(bf16[1,128,512]{2,1,0:T(8,128)(2,1)S(1)} %slice.14), channel_id=1, source_target_pairs={{0,32},{8,40},{16,48},{24,56},{32,64},{40,72},{48,80},{56,88},{64,... | collective-permute-start | bytes 393224 | tf_op jit(solution)/shard_map/ppermute | solution.py:404
  31.5 10.3 %copy-start.3 = (bf16[2,128,512]{2,1,0:T(8,128)(2,1)}, bf16[2,128,512]{2,1,0:T(8,128)(2,1)S(1)}, u32[]{:S(2)}) copy-start(bf16[2,128,512]{2,1,0:T(8,128)(2,1)S(1)} %collective-permute-done.3.refs_1_) | copy-start | bytes 786436
  33.4 8.4 %copy-start.5 = (bf16[1,128,512]{2,1,0:T(8,128)(2,1)}, bf16[1,128,512]{2,1,0:T(8,128)(2,1)S(1)}, u32[]{:S(2)}) copy-start(bf16[1,128,512]{2,1,0:T(8,128)(2,1)S(1)} %collective-permute-done.4.refs_2_) | copy-start | bytes 393220
  33.4 13.9 %copy-start.9 = (bf16[3,128,512]{2,1,0:T(8,128)(2,1)}, bf16[3,128,512]{2,1,0:T(8,128)(2,1)S(1)}, u32[]{:S(2)}) copy-start(bf16[3,128,512]{2,1,0:T(8,128)(2,1)S(1)} %collective-permute-done.10.refs_3_) | copy-start | bytes 1179652
  35.5 31.9 %all-to-all-start = ((bf16[32,80,128]{2,1,0:T(8,128)(2,1)}), bf16[32,80,128]{2,1,0:T(8,128)(2,1)S(1)}, u32[]{:S(2)}, u32[]{:S(2)}) async-start(bf16[32,80,128]{2,1,0:T(8,128)(2,1)} %get-tuple-element.25), calls=%async_computation | async-start | bytes 1310720 | tf_op jit(solution)/shard_map/all_to_all | solution.py:468
  43.8 23.6 %collective-permute-start.5 = (bf16[5,128,512]{2,1,0:T(8,128)(2,1)}, bf16[5,128,512]{2,1,0:T(8,128)(2,1)S(1)}, u32[]{:S(2)}, u32[]{:S(2)}) collective-permute-start(bf16[5,128,512]{2,1,0:T(8,128)(2,1)} %join.1.refs_5_), channel_id=1, source_target_pairs={{0,8},{8,16},{16,24},{24,0},{32,40},{40,48},{48,56},{56,32},{64,72... | collective-permute-start | bytes 1966088 | tf_op jit(solution)/shard_map/ppermute | solution.py:404
  45.7 21.7 %collective-permute-start.7 = (bf16[5,128,512]{2,1,0:T(8,128)(2,1)}, bf16[5,128,512]{2,1,0:T(8,128)(2,1)S(1)}, u32[]{:S(2)}, u32[]{:S(2)}) collective-permute-start(bf16[5,128,512]{2,1,0:T(8,128)(2,1)} %join.1.refs_5_), channel_id=1, source_target_pairs={{0,24},{8,0},{16,8},{24,16},{32,56},{40,32},{48,40},{56,48},{64,88... | collective-permute-start | bytes 1966088 | tf_op jit(solution)/shard_map/ppermute | solution.py:404
  47.4 20.1 %copy-start = (bf16[32,72,128]{2,1,0:T(8,128)(2,1)S(1)}, bf16[32,72,128]{2,1,0:T(8,128)(2,1)}, u32[]{:S(2)}) copy-start(bf16[32,72,128]{2,1,0:T(8,128)(2,1)} %get-tuple-element.26.q_ref) | copy-start | bytes 1769476
  67.4 10.6 %copy-start.4 = (bf16[5,128,512]{2,1,0:T(8,128)(2,1)}, bf16[5,128,512]{2,1,0:T(8,128)(2,1)S(1)}, u32[]{:S(2)}) copy-start(bf16[5,128,512]{2,1,0:T(8,128)(2,1)S(1)} %collective-permute-done.5.refs_1_) | copy-start | bytes 1966084
  67.4 10.6 %copy-start.6 = (bf16[5,128,512]{2,1,0:T(8,128)(2,1)}, bf16[5,128,512]{2,1,0:T(8,128)(2,1)S(1)}, u32[]{:S(2)}) copy-start(bf16[5,128,512]{2,1,0:T(8,128)(2,1)S(1)} %collective-permute-done.7.refs_2_) | copy-start | bytes 1966084
  69.2 31.4 %all-to-all-start.1 = ((bf16[32,72,128]{2,1,0:T(8,128)(2,1)}), bf16[32,72,128]{2,1,0:T(8,128)(2,1)S(1)}, u32[]{:S(2)}, u32[]{:S(2)}) async-start(bf16[32,72,128]{2,1,0:T(8,128)(2,1)} %combine.1), calls=%async_computation.1 | async-start | bytes 1179648 | tf_op jit(solution)/shard_map/all_to_all | solution.py:485
  76.1 16.6 %collective-permute-start.6 = (bf16[3,128,512]{2,1,0:T(8,128)(2,1)S(1)}, bf16[3,128,512]{2,1,0:T(8,128)(2,1)S(1)}, u32[]{:S(2)}, u32[]{:S(2)}) collective-permute-start(bf16[3,128,512]{2,1,0:T(8,128)(2,1)S(1)} %slice.15), channel_id=1, source_target_pairs={{0,8},{8,16},{16,24},{24,0},{32,40},{40,48},{48,56},{56,32},{64,72... | collective-permute-start | bytes 1179656 | tf_op jit(solution)/shard_map/ppermute | solution.py:404
  78.0 11.2 %collective-permute-start.8 = (bf16[2,128,512]{2,1,0:T(8,128)(2,1)S(1)}, bf16[2,128,512]{2,1,0:T(8,128)(2,1)S(1)}, u32[]{:S(2)}, u32[]{:S(2)}) collective-permute-start(bf16[2,128,512]{2,1,0:T(8,128)(2,1)S(1)} %slice.16), channel_id=1, source_target_pairs={{0,24},{8,0},{16,8},{24,16},{32,56},{40,32},{48,40},{56,48},{64,88... | collective-permute-start | bytes 786440 | tf_op jit(solution)/shard_map/ppermute | solution.py:404
  (4 other events, 21.0 us)

commit v5 on v4

--- a/solution.py
+++ b/solution.py
@@ -458,15 +458,15 @@
     up1, down1 = shift(own, 1, 0), shift(own, -1, 0)
     turned = jnp.transpose(decode_queries, (1, 0, 2))
     half = decode_partials(ctx, cache_len, turned, cache_keys, cache_values, None)
-    near, near_z = cat(own, after(up1, *half), down1), [0, 1, -1]
+    near, near_z = cat(after(up1, *half), own, down1), [1, 0, -1]
     right1, left1, across1 = shift(near, 0, 1), shift(near, 0, -1), shift(near, 0, 2)
-    up2, down2 = shift(near[:2], 2, 0), shift(cat(own, down1), -2, 0)
+    up2, down2 = shift(near[:2], 2, 0), shift(near[1:], -2, 0)
 
     partials, q72 = decode_partials(ctx, after(cache_len, up1, down1), turned, cache_keys, cache_values, half)
 
-    up4 = shift(after(up2[1:], partials), 1, 0)
+    up4 = shift(after(up2[:1], partials), 1, 0)
     recv = lax.all_to_all(after(partials, right1, left1, up2, down2, up4, across1), "ctx", 0, 0, tiled=True)
-    far, far_z = join((up2, 0, 2), (down2, 0, 2), (up4, 0, 1)), [2, 3, -2, -3, 4]
+    far, far_z = join((up2, 0, 2), (down2, 0, 2), (up4, 0, 1)), [3, 2, -2, -3, 4]
     right2, left2 = shift(far, 0, 1), shift(far, 0, -1)
 
     def at(zs, x):

time: 102 us -> 102 us (level)
  waiting for transfers between devices: 24.4 us -> 23.1 us
  Pallas kernels: 38.3 us -> 39.5 us
    ppermute x12, waiting for transfers between devices: 24.4 us -> 23.1 us  [shift(): return lax.ppermute(x, 'ctx', [(i, to(i)) for i in range(N)])]
    pallas_call x3, Pallas kernels: 26.6 us -> 27.9 us  [prefill(): pl.pallas_call(functools.partial(prefill_kernel, blocks=blocks, first=fir...]
  transfers between devices with their start and end apart: 14 -> 14, of which waited for: 7 -> 6; matrix products, arithmetic and copies ran while one was open for 0% -> 0% of each run, Pallas kernels for 36% -> 37%
where the time goes in v5:
time: 102 us
  Pallas kernels  39.5 us (39%)
  starting transfers between devices  35 us (34%)
  waiting for transfers between devices  23.1 us (23%)
  local copies, waits for them, and re-layouts  2.24 us (2%)
    pallas_call x3, Pallas kernels, prefill(): pl.pallas_call(functools.partial(prefill_kernel, blocks=blocks, first=fir...  27.9 us
    ppermute x12, waiting for transfers between devices, shift(): return lax.ppermute(x, 'ctx', [(i, to(i)) for i in range(N)])  23.1 us
    ppermute x12, starting transfers between devices, shift(): return lax.ppermute(x, 'ctx', [(i, to(i)) for i in range(N)])  21.8 us
    pallas_call x2, Pallas kernels, decode_partials(): pl.pallas_call(kernel, out_shape=(jax.ShapeDtypeStruct((REQ, PAY, D), jnp...  8 us
    all_to_all x1, starting transfers between devices, local(): spread = lax.all_to_all(done, 'ctx', 0, 0, tiled=True)  6.87 us
    all_to_all x1, starting transfers between devices, local(): lax.all_to_all(after(partials, right1, left1, up2, down2, up4, across1),...  6.34 us
  transfers between devices with their start and end apart: 14, of which 6 were waited for; matrix products, arithmetic and copies ran while one was open for 0% of the time, Pallas kernels for 37%

profile of v5, /device:TPU:16, one launch (start us, length us, event | category | flops | bytes accessed | tf_op | source)
XLA Modules:
  0.0 101.8 jit_solution(2931982179357081780)
XLA Ops:
  1.5 2.0 %collective-permute-start = (bf16[1,128,512]{2,1,0:T(8,128)(2,1)S(1)}, bf16[1,128,512]{2,1,0:T(8,128)(2,1)S(1)}, u32[]{:S(2)}, u32[]{:S(2)}) collective-permute-start(bf16[1,128,512]{2,1,0:T(8,128)(2,1)S(1)} %maximum_bitcast_fusion), channel_id=1, source_target_pairs={{0,32},{8,40},{16,48},{24,56},{32,64},{40,72},{48,80},{56,88},{64,... | collective-permute-start | bytes 393224 | tf_op jit(solution)/shard_map/ppermute | solution.py:404
  3.5 4.0 %collective-permute-start.2 = (bf16[1,128,512]{2,1,0:T(8,128)(2,1)S(1)}, bf16[1,128,512]{2,1,0:T(8,128)(2,1)S(1)}, u32[]{:S(2)}, u32[]{:S(2)}) collective-permute-start(bf16[1,128,512]{2,1,0:T(8,128)(2,1)S(1)} %maximum_bitcast_fusion), channel_id=1, source_target_pairs={{0,224},{8,232},{16,240},{24,248},{32,0},{40,8},{48,16},{56,24},{6... | collective-permute-start | bytes 393224 | tf_op jit(solution)/shard_map/ppermute | solution.py:404
  7.5 4.0 %decode_partials.2 = (bf16[32,80,128]{2,1,0:T(8,128)(2,1)}, bf16[32,72,128]{2,1,0:T(8,128)(2,1)}) custom-call(s32[1]{0:T(128)} %bitcast.ctx_ref, s32[32]{0:T(128)} %len_ref.2, bf16[3,32,3072]{2,1,0:T(8,128)(2,1)} %bitcast.4, bf16[32,128,256]{2,1,0:T(8,128)(2,1)} %k_ref.3, bf16[32,128,256]{2,1,0:T(8,128)(2,1)} %v_ref.3), custom_call_target="tpu_custom_call" | custom-call | flops 150994944 | bytes 3145728 | tf_op jit(solution)/shard_map/decode_partials/pallas_call | solution.py:112
  11.6 1.7 %collective-permute-start.1 = (bf16[2,128,512]{2,1,0:T(8,128)(2,1)S(1)}, bf16[2,128,512]{2,1,0:T(8,128)(2,1)S(1)}, u32[]{:S(2)}, u32[]{:S(2)}) collective-permute-start(bf16[2,128,512]{2,1,0:T(8,128)(2,1)S(1)} %get-tuple-element.35), channel_id=1, source_target_pairs={{0,64},{8,72},{16,80},{24,88},{32,96},{40,104},{48,112},{56,120},{... | collective-permute-start | bytes 786440 | tf_op jit(solution)/shard_map/ppermute | solution.py:404
  13.3 2.8 %collective-permute-start.10 = (bf16[3,128,512]{2,1,0:T(8,128)(2,1)S(1)}, bf16[3,128,512]{2,1,0:T(8,128)(2,1)S(1)}, u32[]{:S(2)}, u32[]{:S(2)}) collective-permute-start(bf16[3,128,512]{2,1,0:T(8,128)(2,1)S(1)} %pad_maximum_fusion.refs_1_), channel_id=1, source_target_pairs={{0,24},{8,0},{16,8},{24,16},{32,56},{40,32},{48,40},{56,48},{64,88... | collective-permute-start | bytes 1179656 | tf_op jit(solution)/shard_map/ppermute | solution.py:404
  17.8 2.6 %collective-permute-start.3 = (bf16[2,128,512]{2,1,0:T(8,128)(2,1)S(1)}, bf16[2,128,512]{2,1,0:T(8,128)(2,1)S(1)}, u32[]{:S(2)}, u32[]{:S(2)}) collective-permute-start(bf16[2,128,512]{2,1,0:T(8,128)(2,1)S(1)} %get-tuple-element.34), channel_id=1, source_target_pairs={{0,192},{8,200},{16,208},{24,216},{32,224},{40,232},{48,240},{56,2... | collective-permute-start | bytes 786440 | tf_op jit(solution)/shard_map/ppermute | solution.py:404
  20.4 4.0 %decode_partials.3 = (bf16[32,80,128]{2,1,0:T(8,128)(2,1)}, bf16[32,72,128]{2,1,0:T(8,128)(2,1)}) custom-call(s32[1]{0:T(128)} %bitcast.ctx_ref, s32[32]{0:T(128)} %len_ref.2, bf16[3,32,3072]{2,1,0:T(8,128)(2,1)} %bitcast.5, bf16[32,128,256]{2,1,0:T(8,128)(2,1)} %k_ref.3, bf16[32,128,256]{2,1,0:T(8,128)(2,1)} %v_ref.3, ...), custom_call_target="tpu_custom_call", output_to_operand_aliasing={{0}: (5, {}), {1}: (6, {})} | custom-call | flops 150994944 | bytes 3145728 | tf_op jit(solution)/shard_map/decode_partials/pallas_call | solution.py:112
  24.4 2.8 %collective-permute-done.1.refs_0_ = bf16[2,128,512]{2,1,0:T(8,128)(2,1)S(1)} collective-permute-done((bf16[2,128,512]{2,1,0:T(8,128)(2,1)S(1)}, bf16[2,128,512]{2,1,0:T(8,128)(2,1)S(1)}, u32[]{:S(2)}, u32[]{:S(2)}) %collective-permute-start.1) | collective-permute-done | bytes 262176 | tf_op jit(solution)/shard_map/ppermute | solution.py:404
  27.3 4.3 %collective-permute-done.3.refs_1_ = bf16[2,128,512]{2,1,0:T(8,128)(2,1)S(1)} collective-permute-done((bf16[2,128,512]{2,1,0:T(8,128)(2,1)S(1)}, bf16[2,128,512]{2,1,0:T(8,128)(2,1)S(1)}, u32[]{:S(2)}, u32[]{:S(2)}) %collective-permute-start.3) | collective-permute-done | bytes 262176 | tf_op jit(solution)/shard_map/ppermute | solution.py:404
  31.5 1.9 %collective-permute-done.4.refs_2_ = bf16[1,128,512]{2,1,0:T(8,128)(2,1)S(1)} collective-permute-done((bf16[1,128,512]{2,1,0:T(8,128)(2,1)S(1)}, bf16[1,128,512]{2,1,0:T(8,128)(2,1)S(1)}, u32[]{:S(2)}, u32[]{:S(2)}) %collective-permute-start.4) | collective-permute-done | bytes 131104 | tf_op jit(solution)/shard_map/ppermute | solution.py:404
  33.5 2.0 %collective-permute-done.9.refs_2_ = bf16[3,128,512]{2,1,0:T(8,128)(2,1)S(1)} collective-permute-done((bf16[3,128,512]{2,1,0:T(8,128)(2,1)S(1)}, bf16[3,128,512]{2,1,0:T(8,128)(2,1)S(1)}, u32[]{:S(2)}, u32[]{:S(2)}) %collective-permute-start.9) | collective-permute-done | bytes 393248 | tf_op jit(solution)/shard_map/ppermute | solution.py:404
  35.5 6.3 %all-to-all-start = ((bf16[32,80,128]{2,1,0:T(8,128)(2,1)}), bf16[32,80,128]{2,1,0:T(8,128)(2,1)S(1)}, u32[]{:S(2)}, u32[]{:S(2)}) async-start(bf16[32,80,128]{2,1,0:T(8,128)(2,1)} %get-tuple-element.25), calls=%async_computation | async-start | bytes 1310720 | tf_op jit(solution)/shard_map/all_to_all | solution.py:468
  41.9 1.9 %join.1.refs_5_ = bf16[5,128,512]{2,1,0:T(8,128)(2,1)} custom-call(bf16[2,128,512]{2,1,0:T(8,128)(2,1)} %copy-done.1, bf16[2,128,512]{2,1,0:T(8,128)(2,1)} %copy-done.3, bf16[1,128,512]{2,1,0:T(8,128)(2,1)} %copy-done.5), custom_call_target="tpu_custom_call" | custom-call | bytes 1310720 | tf_op jit(solution)/shard_map/join/pallas_call | solution.py:426
  43.8 1.9 %collective-permute-start.5 = (bf16[5,128,512]{2,1,0:T(8,128)(2,1)}, bf16[5,128,512]{2,1,0:T(8,128)(2,1)S(1)}, u32[]{:S(2)}, u32[]{:S(2)}) collective-permute-start(bf16[5,128,512]{2,1,0:T(8,128)(2,1)} %join.1.refs_5_), channel_id=1, source_target_pairs={{0,8},{8,16},{16,24},{24,0},{32,40},{40,48},{48,56},{56,32},{64,72... | collective-permute-start | bytes 1966088 | tf_op jit(solution)/shard_map/ppermute | solution.py:404
  45.7 1.5 %collective-permute-start.7 = (bf16[5,128,512]{2,1,0:T(8,128)(2,1)}, bf16[5,128,512]{2,1,0:T(8,128)(2,1)S(1)}, u32[]{:S(2)}, u32[]{:S(2)}) collective-permute-start(bf16[5,128,512]{2,1,0:T(8,128)(2,1)} %join.1.refs_5_), channel_id=1, source_target_pairs={{0,24},{8,0},{16,8},{24,16},{32,56},{40,32},{48,40},{56,48},{64,88... | collective-permute-start | bytes 1966088 | tf_op jit(solution)/shard_map/ppermute | solution.py:404
  47.4 11.0 %prefill_start.2 = (f32[2,2,128,768]{3,2,1,0:T(8,128)}, f32[2,2,8,768]{3,2,1,0:T(8,128)}) custom-call(s32[32]{0:T(128)} %pair_ref.4, s32[1]{0:T(128)} %bitcast.ctx_ref, bf16[128,3072]{1,0:T(8,128)(2,1)} %refs_0_.5, bf16[3,128,512]{2,1,0:T(8,128)(2,1)} %copy-done.2, bf16[3,128,512]{2,1,0:T(8,128)(2,1)} %copy-done.11, bf16[3,128,512]{2,1,0:T(8,128)(2,1)} %copy-done.9, ...), custom_call_target="tpu_custom_call" | custom-call | flops 4563402752 | bytes 4194304 | tf_op jit(solution)/shard_map/prefill_start/pallas_call | solution.py:376
  58.4 9.0 %collective-permute-done.5.refs_1_ = bf16[5,128,512]{2,1,0:T(8,128)(2,1)S(1)} collective-permute-done((bf16[5,128,512]{2,1,0:T(8,128)(2,1)}, bf16[5,128,512]{2,1,0:T(8,128)(2,1)S(1)}, u32[]{:S(2)}, u32[]{:S(2)}) %collective-permute-start.5) | collective-permute-done | bytes 655392 | tf_op jit(solution)/shard_map/ppermute | solution.py:404
  67.4 1.8 %combine.1 = bf16[32,72,128]{2,1,0:T(8,128)(2,1)} custom-call(s32[1]{0:T(128)} %bitcast.ctx_ref, bf16[32,80,128]{2,1,0:T(8,128)(2,1)S(1)} %all-to-all-done.recv_ref, bf16[32,72,128]{2,1,0:T(8,128)(2,1)S(1)} %copy-done, bf16[32,8,256]{2,1,0:T(8,128)(2,1)S(1)} %pad.7.dk_ref, bf16[32,8,256]{2,1,0:T(8,128)(2,1)S(1)} %pad.8.dv_ref), custom_call_target="tpu_custom_call" | custom-call | flops 4194304 | bytes 1048576 | tf_op jit(solution)/shard_map/combine/pallas_call | solution.py:181
  69.2 6.9 %all-to-all-start.1 = ((bf16[32,72,128]{2,1,0:T(8,128)(2,1)}), bf16[32,72,128]{2,1,0:T(8,128)(2,1)S(1)}, u32[]{:S(2)}, u32[]{:S(2)}) async-start(bf16[32,72,128]{2,1,0:T(8,128)(2,1)} %combine.1), calls=%async_computation.1 | async-start | bytes 1179648 | tf_op jit(solution)/shard_map/all_to_all | solution.py:485
  76.1 1.9 %collective-permute-start.6 = (bf16[3,128,512]{2,1,0:T(8,128)(2,1)S(1)}, bf16[3,128,512]{2,1,0:T(8,128)(2,1)S(1)}, u32[]{:S(2)}, u32[]{:S(2)}) collective-permute-start(bf16[3,128,512]{2,1,0:T(8,128)(2,1)S(1)} %slice.17), channel_id=1, source_target_pairs={{0,8},{8,16},{16,24},{24,0},{32,40},{40,48},{48,56},{56,32},{64,72... | collective-permute-start | bytes 1179656 | tf_op jit(solution)/shard_map/ppermute | solution.py:404
  78.0 1.7 %collective-permute-start.8 = (bf16[2,128,512]{2,1,0:T(8,128)(2,1)S(1)}, bf16[2,128,512]{2,1,0:T(8,128)(2,1)S(1)}, u32[]{:S(2)}, u32[]{:S(2)}) collective-permute-start(bf16[2,128,512]{2,1,0:T(8,128)(2,1)S(1)} %slice.18), channel_id=1, source_target_pairs={{0,24},{8,0},{16,8},{24,16},{32,56},{40,32},{48,40},{56,48},{64,88... | collective-permute-start | bytes 786440 | tf_op jit(solution)/shard_map/ppermute | solution.py:404
  79.8 9.8 %prefill_start.3 = (f32[2,2,128,768]{3,2,1,0:T(8,128)}, f32[2,2,8,768]{3,2,1,0:T(8,128)}) custom-call(s32[32]{0:T(128)} %pair_ref.4, s32[1]{0:T(128)} %bitcast.ctx_ref, bf16[128,3072]{1,0:T(8,128)(2,1)} %refs_0_.5, bf16[5,128,512]{2,1,0:T(8,128)(2,1)} %copy-done.4, bf16[5,128,512]{2,1,0:T(8,128)(2,1)} %copy-done.6, ...), custom_call_target="tpu_custom_call" | custom-call | flops 2684354560 | bytes 4194304 | tf_op jit(solution)/shard_map/prefill_start/pallas_call | solution.py:376
  89.6 3.1 %collective-permute-done.6.refs_1_ = bf16[3,128,512]{2,1,0:T(8,128)(2,1)S(1)} collective-permute-done((bf16[3,128,512]{2,1,0:T(8,128)(2,1)S(1)}, bf16[3,128,512]{2,1,0:T(8,128)(2,1)S(1)}, u32[]{:S(2)}, u32[]{:S(2)}) %collective-permute-start.6) | collective-permute-done | bytes 393248 | tf_op jit(solution)/shard_map/ppermute | solution.py:404
  93.5 7.1 %prefill_end.1 = bf16[128,3072]{1,0:T(8,128)(2,1)} custom-call(s32[32]{0:T(128)} %pair_ref.4, s32[1]{0:T(128)} %bitcast.ctx_ref, bf16[128,3072]{1,0:T(8,128)(2,1)} %refs_0_.5, bf16[3,128,512]{2,1,0:T(8,128)(2,1)} %copy-done.12, bf16[2,128,512]{2,1,0:T(8,128)(2,1)} %copy-done.13, f32[2,2,128,768]{3,2,1,0:T(8,128)} %get-tuple-element.28.refs_3_, ...), custom_call_target="tpu_custom_call" | custom-call | flops 1342177280 | bytes 4194304 | tf_op jit(solution)/shard_map/prefill_end/pallas_call | solution.py:376
  (51 shorter events, 5.0 us)
Async XLA Ops:
  1.5 10.0 %collective-permute-start = (bf16[1,128,512]{2,1,0:T(8,128)(2,1)S(1)}, bf16[1,128,512]{2,1,0:T(8,128)(2,1)S(1)}, u32[]{:S(2)}, u32[]{:S(2)}) collective-permute-start(bf16[1,128,512]{2,1,0:T(8,128)(2,1)S(1)} %maximum_bitcast_fusion), channel_id=1, source_target_pairs={{0,32},{8,40},{16,48},{24,56},{32,64},{40,72},{48,80},{56,88},{64,... | collective-permute-start | bytes 393224 | tf_op jit(solution)/shard_map/ppermute | solution.py:404
  3.5 8.0 %collective-permute-start.2 = (bf16[1,128,512]{2,1,0:T(8,128)(2,1)S(1)}, bf16[1,128,512]{2,1,0:T(8,128)(2,1)S(1)}, u32[]{:S(2)}, u32[]{:S(2)}) collective-permute-start(bf16[1,128,512]{2,1,0:T(8,128)(2,1)S(1)} %maximum_bitcast_fusion), channel_id=1, source_target_pairs={{0,224},{8,232},{16,240},{24,248},{32,0},{40,8},{48,16},{56,24},{6... | collective-permute-start | bytes 393224 | tf_op jit(solution)/shard_map/ppermute | solution.py:404
  11.6 15.6 %collective-permute-start.1 = (bf16[2,128,512]{2,1,0:T(8,128)(2,1)S(1)}, bf16[2,128,512]{2,1,0:T(8,128)(2,1)S(1)}, u32[]{:S(2)}, u32[]{:S(2)}) collective-permute-start(bf16[2,128,512]{2,1,0:T(8,128)(2,1)S(1)} %get-tuple-element.35), channel_id=1, source_target_pairs={{0,64},{8,72},{16,80},{24,88},{32,96},{40,104},{48,112},{56,120},{... | collective-permute-start | bytes 786440 | tf_op jit(solution)/shard_map/ppermute | solution.py:404
  13.3 11.1 %copy-start.2 = (bf16[3,128,512]{2,1,0:T(8,128)(2,1)}, bf16[3,128,512]{2,1,0:T(8,128)(2,1)S(1)}, u32[]{:S(2)}) copy-start(bf16[3,128,512]{2,1,0:T(8,128)(2,1)S(1)} %pad_maximum_fusion.refs_1_) | copy-start | bytes 1179652
  13.3 20.1 %collective-permute-start.10 = (bf16[3,128,512]{2,1,0:T(8,128)(2,1)S(1)}, bf16[3,128,512]{2,1,0:T(8,128)(2,1)S(1)}, u32[]{:S(2)}, u32[]{:S(2)}) collective-permute-start(bf16[3,128,512]{2,1,0:T(8,128)(2,1)S(1)} %pad_maximum_fusion.refs_1_), channel_id=1, source_target_pairs={{0,24},{8,0},{16,8},{24,16},{32,56},{40,32},{48,40},{56,48},{64,88... | collective-permute-start | bytes 1179656 | tf_op jit(solution)/shard_map/ppermute | solution.py:404
  16.1 17.3 %collective-permute-start.11 = (bf16[3,128,512]{2,1,0:T(8,128)(2,1)S(1)}, bf16[3,128,512]{2,1,0:T(8,128)(2,1)S(1)}, u32[]{:S(2)}, u32[]{:S(2)}) collective-permute-start(bf16[3,128,512]{2,1,0:T(8,128)(2,1)S(1)} %pad_maximum_fusion.refs_1_), channel_id=1, source_target_pairs={{0,16},{8,24},{16,0},{24,8},{32,48},{40,56},{48,32},{56,40},{64,80... | collective-permute-start | bytes 1179656 | tf_op jit(solution)/shard_map/ppermute | solution.py:404
  16.9 18.6 %collective-permute-start.9 = (bf16[3,128,512]{2,1,0:T(8,128)(2,1)S(1)}, bf16[3,128,512]{2,1,0:T(8,128)(2,1)S(1)}, u32[]{:S(2)}, u32[]{:S(2)}) collective-permute-start(bf16[3,128,512]{2,1,0:T(8,128)(2,1)S(1)} %pad_maximum_fusion.refs_1_), channel_id=1, source_target_pairs={{0,8},{8,16},{16,24},{24,0},{32,40},{40,48},{48,56},{56,32},{64,72... | collective-permute-start | bytes 1179656 | tf_op jit(solution)/shard_map/ppermute | solution.py:404
  17.8 13.7 %collective-permute-start.3 = (bf16[2,128,512]{2,1,0:T(8,128)(2,1)S(1)}, bf16[2,128,512]{2,1,0:T(8,128)(2,1)S(1)}, u32[]{:S(2)}, u32[]{:S(2)}) collective-permute-start(bf16[2,128,512]{2,1,0:T(8,128)(2,1)S(1)} %get-tuple-element.34), channel_id=1, source_target_pairs={{0,192},{8,200},{16,208},{24,216},{32,224},{40,232},{48,240},{56,2... | collective-permute-start | bytes 786440 | tf_op jit(solution)/shard_map/ppermute | solution.py:404
  24.4 22.8 %copy-start.7 = (bf16[32,3,256]{2,0,1:T(8,128)(2,1)S(1)}, bf16[32,3,256]{2,0,1:T(8,128)(2,1)}, u32[]{:S(2)}) copy-start(bf16[32,3,256]{2,0,1:T(8,128)(2,1)} %param.17) | copy-start | bytes 147460
  24.4 22.8 %copy-start.8 = (bf16[32,3,256]{2,0,1:T(8,128)(2,1)S(1)}, bf16[32,3,256]{2,0,1:T(8,128)(2,1)}, u32[]{:S(2)}) copy-start(bf16[32,3,256]{2,0,1:T(8,128)(2,1)} %param.18) | copy-start | bytes 147460
  27.2 14.7 %copy-start.1 = (bf16[2,128,512]{2,1,0:T(8,128)(2,1)}, bf16[2,128,512]{2,1,0:T(8,128)(2,1)S(1)}, u32[]{:S(2)}) copy-start(bf16[2,128,512]{2,1,0:T(8,128)(2,1)S(1)} %collective-permute-done.1.refs_0_) | copy-start | bytes 786436
  27.2 6.3 %collective-permute-start.4 = (bf16[1,128,512]{2,1,0:T(8,128)(2,1)S(1)}, bf16[1,128,512]{2,1,0:T(8,128)(2,1)S(1)}, u32[]{:S(2)}, u32[]{:S(2)}) collective-permute-start(bf16[1,128,512]{2,1,0:T(8,128)(2,1)S(1)} %slice.16), channel_id=1, source_target_pairs={{0,32},{8,40},{16,48},{24,56},{32,64},{40,72},{48,80},{56,88},{64,... | collective-permute-start | bytes 393224 | tf_op jit(solution)/shard_map/ppermute | solution.py:404
  31.5 10.3 %copy-start.3 = (bf16[2,128,512]{2,1,0:T(8,128)(2,1)}, bf16[2,128,512]{2,1,0:T(8,128)(2,1)S(1)}, u32[]{:S(2)}) copy-start(bf16[2,128,512]{2,1,0:T(8,128)(2,1)S(1)} %collective-permute-done.3.refs_1_) | copy-start | bytes 786436
  33.4 8.4 %copy-start.5 = (bf16[1,128,512]{2,1,0:T(8,128)(2,1)}, bf16[1,128,512]{2,1,0:T(8,128)(2,1)S(1)}, u32[]{:S(2)}) copy-start(bf16[1,128,512]{2,1,0:T(8,128)(2,1)S(1)} %collective-permute-done.4.refs_2_) | copy-start | bytes 393220
  33.4 13.9 %copy-start.9 = (bf16[3,128,512]{2,1,0:T(8,128)(2,1)}, bf16[3,128,512]{2,1,0:T(8,128)(2,1)S(1)}, u32[]{:S(2)}) copy-start(bf16[3,128,512]{2,1,0:T(8,128)(2,1)S(1)} %collective-permute-done.10.refs_3_) | copy-start | bytes 1179652
  35.5 31.9 %all-to-all-start = ((bf16[32,80,128]{2,1,0:T(8,128)(2,1)}), bf16[32,80,128]{2,1,0:T(8,128)(2,1)S(1)}, u32[]{:S(2)}, u32[]{:S(2)}) async-start(bf16[32,80,128]{2,1,0:T(8,128)(2,1)} %get-tuple-element.25), calls=%async_computation | async-start | bytes 1310720 | tf_op jit(solution)/shard_map/all_to_all | solution.py:468
  43.8 23.6 %collective-permute-start.5 = (bf16[5,128,512]{2,1,0:T(8,128)(2,1)}, bf16[5,128,512]{2,1,0:T(8,128)(2,1)S(1)}, u32[]{:S(2)}, u32[]{:S(2)}) collective-permute-start(bf16[5,128,512]{2,1,0:T(8,128)(2,1)} %join.1.refs_5_), channel_id=1, source_target_pairs={{0,8},{8,16},{16,24},{24,0},{32,40},{40,48},{48,56},{56,32},{64,72... | collective-permute-start | bytes 1966088 | tf_op jit(solution)/shard_map/ppermute | solution.py:404
  45.7 21.7 %collective-permute-start.7 = (bf16[5,128,512]{2,1,0:T(8,128)(2,1)}, bf16[5,128,512]{2,1,0:T(8,128)(2,1)S(1)}, u32[]{:S(2)}, u32[]{:S(2)}) collective-permute-start(bf16[5,128,512]{2,1,0:T(8,128)(2,1)} %join.1.refs_5_), channel_id=1, source_target_pairs={{0,24},{8,0},{16,8},{24,16},{32,56},{40,32},{48,40},{56,48},{64,88... | collective-permute-start | bytes 1966088 | tf_op jit(solution)/shard_map/ppermute | solution.py:404
  47.4 20.1 %copy-start = (bf16[32,72,128]{2,1,0:T(8,128)(2,1)S(1)}, bf16[32,72,128]{2,1,0:T(8,128)(2,1)}, u32[]{:S(2)}) copy-start(bf16[32,72,128]{2,1,0:T(8,128)(2,1)} %get-tuple-element.26.q_ref) | copy-start | bytes 1769476
  67.4 10.6 %copy-start.4 = (bf16[5,128,512]{2,1,0:T(8,128)(2,1)}, bf16[5,128,512]{2,1,0:T(8,128)(2,1)S(1)}, u32[]{:S(2)}) copy-start(bf16[5,128,512]{2,1,0:T(8,128)(2,1)S(1)} %collective-permute-done.5.refs_1_) | copy-start | bytes 1966084
  67.4 10.6 %copy-start.6 = (bf16[5,128,512]{2,1,0:T(8,128)(2,1)}, bf16[5,128,512]{2,1,0:T(8,128)(2,1)S(1)}, u32[]{:S(2)}) copy-start(bf16[5,128,512]{2,1,0:T(8,128)(2,1)S(1)} %collective-permute-done.7.refs_2_) | copy-start | bytes 1966084
  69.2 31.4 %all-to-all-start.1 = ((bf16[32,72,128]{2,1,0:T(8,128)(2,1)}), bf16[32,72,128]{2,1,0:T(8,128)(2,1)S(1)}, u32[]{:S(2)}, u32[]{:S(2)}) async-start(bf16[32,72,128]{2,1,0:T(8,128)(2,1)} %combine.1), calls=%async_computation.1 | async-start | bytes 1179648 | tf_op jit(solution)/shard_map/all_to_all | solution.py:485
  76.1 16.6 %collective-permute-start.6 = (bf16[3,128,512]{2,1,0:T(8,128)(2,1)S(1)}, bf16[3,128,512]{2,1,0:T(8,128)(2,1)S(1)}, u32[]{:S(2)}, u32[]{:S(2)}) collective-permute-start(bf16[3,128,512]{2,1,0:T(8,128)(2,1)S(1)} %slice.17), channel_id=1, source_target_pairs={{0,8},{8,16},{16,24},{24,0},{32,40},{40,48},{48,56},{56,32},{64,72... | collective-permute-start | bytes 1179656 | tf_op jit(solution)/shard_map/ppermute | solution.py:404
  78.0 11.6 %collective-permute-start.8 = (bf16[2,128,512]{2,1,0:T(8,128)(2,1)S(1)}, bf16[2,128,512]{2,1,0:T(8,128)(2,1)S(1)}, u32[]{:S(2)}, u32[]{:S(2)}) collective-permute-start(bf16[2,128,512]{2,1,0:T(8,128)(2,1)S(1)} %slice.18), channel_id=1, source_target_pairs={{0,24},{8,0},{16,8},{24,16},{32,56},{40,32},{48,40},{56,48},{64,88... | collective-permute-start | bytes 786440 | tf_op jit(solution)/shard_map/ppermute | solution.py:404
  (4 other events, 20.6 us)
